TPU v7x, 512 devices: a whole 4x8x8 slice. The times are simulated.
512 devices in a mesh: seq: 64 (over y, z_lo, core), head: 8 (over x, z_hi).
Axes of the slice: x: 4, y: 8, z: 8 (z_hi: 2, z_lo: 4; z = z_hi * 4 + z_lo), core: 2. Of those that a mesh axis runs over, the one named last changes fastest.
Arguments:
- codes: int32 [4, 16384], P(None, 'seq'), may hold values from 0 to 1023
- delays: int32 [4], replicated, may hold values from 0 to 3
- targets: int32 [4, 16384], P(None, 'seq'), may hold values from 0 to 1023
- embed: bfloat16 [4, 1024, 2048], P(None, None, 'head'), may hold values from -3 to 3
- wqkv: bfloat16 [2048, 3, 1024], P(None, None, 'head'), may hold values from -1.9224466 to 1.9224466
- wout: bfloat16 [1024, 2048], P('head'), may hold values from -0.1875 to 0.1875
- heads_w: bfloat16 [4, 2048, 1024], P(None, 'seq', 'head'), may hold values from -6.894291 to 6.894291
Outputs:
- mixed: bfloat16 [16384, 2048], P('seq', 'head')
- loss: float32 [4, 16384], P(None, ('seq', 'head'))
All inputs are finite; a program needn't handle non-finite values.
Results may differ from a plain program's by a relative error of at most 0.034.
The roundings to bfloat16 on the way count: a program that leaves them out, or rounds other values in their place, can miss the bound.
Values may be sent and summed in bfloat16 or wider, within the bound.
No kernel may reach another device: no remote copies, remote signals or barrier semaphores. Data moves between devices by JAX's collectives and lax.ppermute only.
A program may use at most 128 MiB of HBM per device.

v0:
```python
import math

import jax
import jax.numpy as jnp
from jax import lax
from jax.sharding import PartitionSpec as P

HD = 64


def from_behind(array, axis, by):
    devices = lax.axis_size(axis)
    pairs = [(i, i + by) for i in range(devices) if 0 <= i + by < devices]
    return lax.ppermute(array, axis, pairs)


def normalize(rows):
    mean_sq = jnp.mean(jnp.square(rows), axis=-1, keepdims=True)
    return (rows * lax.rsqrt(mean_sq + 1e-05)).astype(jnp.bfloat16)


def sinusoid(frames_f, columns, width):
    half = width // 2
    freq = jnp.exp(-math.log(10000.0) * (columns % half).astype(jnp.float32) / half)
    angle = frames_f[:, None] * freq[None, :]
    return jnp.where(columns[None, :] < half, jnp.sin(angle), jnp.cos(angle))


def update(carry, query_heads, query_pos, key_rows, value_rows, key_pos):
    count = key_rows.shape[0]
    heads_here = query_heads.shape[1]
    head_size = query_heads.shape[2]
    key_heads = key_rows.reshape(count, heads_here, head_size)
    value_heads = value_rows.reshape(count, heads_here, head_size)
    scale = 1.0 / math.sqrt(head_size)
    scores = (
        jnp.einsum("qhe,khe->hqk", query_heads, key_heads, preferred_element_type=jnp.float32)
        * scale
    )
    allowed = key_pos[None, :] <= query_pos[:, None]
    masked = jnp.where(allowed[None], scores, -1e30)
    new_max = jnp.maximum(carry[0], jnp.max(masked, axis=-1))
    weights = jnp.where(allowed[None], jnp.exp(masked - new_max[:, :, None]), 0.0)
    totals = jnp.sum(weights, axis=-1)
    gathered = jnp.einsum(
        "hqk,khe->hqe",
        weights.astype(jnp.bfloat16),
        value_heads,
        preferred_element_type=jnp.float32,
    )
    return (new_max, totals, gathered)


def shards(codes, delays, targets, embed, wqkv, wout, heads_w):
    books, frame_count = codes.shape
    seq_pos = lax.axis_index("seq")
    head_pos = lax.axis_index("head")
    first = seq_pos * frame_count
    rim = from_behind(codes[:, frame_count - 3 :], "seq", 1)
    extended = jnp.concatenate([rim, codes], axis=1)
    local = jnp.arange(frame_count, dtype=jnp.int32)
    where_from = local[None, :] + 3 - delays[:, None]
    ids = jnp.take_along_axis(extended, where_from, axis=1)
    frame_pos = first + local
    valid = frame_pos[None, :] >= delays[:, None]
    looked = jax.vmap(lambda table, rows: jnp.take(table, rows, axis=0))(embed, ids)
    width_part = embed.shape[2]
    width = width_part * lax.axis_size("head")
    columns = head_pos * width_part + jnp.arange(width_part, dtype=jnp.int32)
    summed = jnp.sum(jnp.where(valid[:, :, None], looked.astype(jnp.float32), 0.0), axis=0)
    summed = summed + sinusoid(frame_pos.astype(jnp.float32), columns, width)
    x_part = summed.astype(jnp.bfloat16)
    x_full = lax.all_gather(x_part, "head", axis=1, tiled=True)
    normed = normalize(x_full.astype(jnp.float32))
    projected = jnp.einsum("td,dje->tje", normed, wqkv, preferred_element_type=jnp.float32).astype(
        jnp.bfloat16
    )
    queries = projected[:, 0]
    keys = projected[:, 1]
    values = projected[:, 2]
    heads_here = queries.shape[1] // HD
    query_heads = queries.reshape(frame_count, heads_here, HD)
    query_pos = first + local
    start_state = (
        jnp.full((heads_here, frame_count), -1e30, jnp.float32),
        jnp.zeros((heads_here, frame_count), jnp.float32),
        jnp.zeros((heads_here, frame_count, HD), jnp.float32),
    )
    key_rows = lax.all_gather(keys, "seq", axis=0, tiled=True)
    value_rows = lax.all_gather(values, "seq", axis=0, tiled=True)
    count = key_rows.shape[0]
    key_pos = jnp.arange(count, dtype=jnp.int32)
    folded = update(start_state, query_heads, query_pos, key_rows, value_rows, key_pos)
    attended = (folded[2] / folded[1][:, :, None]).astype(jnp.bfloat16)
    flat = jnp.transpose(attended, (1, 0, 2)).reshape(frame_count, heads_here * HD)
    terms = jnp.dot(flat, wout, preferred_element_type=jnp.float32)
    mixed = lax.psum_scatter(terms.astype(jnp.bfloat16), "head", scatter_dimension=1, tiled=True)
    resid_part = (x_part.astype(jnp.float32) + mixed.astype(jnp.float32)).astype(jnp.bfloat16)
    resid = lax.all_gather(resid_part, "head", axis=1, tiled=True)
    final = normalize(resid.astype(jnp.float32))
    logits = jnp.einsum(
        "td,kdv->tkv",
        final,
        lax.all_gather(heads_w, "seq", axis=1, tiled=True),
        preferred_element_type=jnp.float32,
    )
    share = frame_count // lax.axis_size("head")
    mine = head_pos * share
    spread = lax.all_to_all(
        logits.astype(jnp.bfloat16), "head", split_axis=0, concat_axis=2, tiled=True
    ).astype(logits.dtype)
    target_rows = lax.dynamic_slice_in_dim(targets, mine, share, 1)
    largest = jnp.max(spread, axis=-1)
    lse = largest + jnp.log(jnp.sum(jnp.exp(spread - largest[:, :, None]), axis=-1))
    picked = jnp.take_along_axis(spread, jnp.transpose(target_rows)[:, :, None], axis=-1)[:, :, 0]
    loss = jnp.transpose(lse - picked)
    return (mixed, loss)


def solution(mesh):
    placed = (
        P(None, "seq"),
        P(),
        P(None, "seq"),
        P(None, None, "head"),
        P(None, None, "head"),
        P("head", None),
        P(None, "seq", "head"),
    )
    return jax.shard_map(
        shards,
        mesh=mesh,
        in_specs=placed,
        out_specs=(P("seq", "head"), P(None, ("seq", "head"))),
        check_vma=False,
    )
```

profile of v0, /device:TPU:64, one launch (start us, length us, event | category | flops | bytes accessed | tf_op | source)
XLA Modules:
  0.0 681.0 jit_solution(6714338128218922274)
XLA Ops:
  7.2 0.0 copy-start
  7.2 0.0 copy-start.2
  7.2 0.0 all-gather.8.cloned.1.call-start
  7.2 0.9 slice.12
  8.1 1.9 collective-permute-start
  10.1 0.7 or_bitcast_fusion
  10.8 2.2 collective-permute-done
  13.0 0.8 pad_add_fusion
  13.8 9.1 %gather_fusion = s32[1024]{0:T(1024)S(1)} fusion(s32[4,259]{1,0:T(4,128)S(1)} %pad_add_fusion, s32[1024]{0:T(1024)S(1)} %bitcast.57), kind=kCustom, calls=%fused_computation | custom fusion | bytes 16384 | tf_op jit(solution)/shard_map/jit(take_along_axis)/gather | solution.py:63
  22.9 0.0 copy-done.2
  23.0 0.1 fusion.31
  23.0 0.1 broadcast_compare_fusion
  23.1 0.0 copy-done
  23.1 5.8 gather_fusion.1
  28.9 0.3 select_reduce_fusion
  29.3 1.8 fusion.27
  31.1 0.0 all-gather.8.cloned.1.call-update
  31.1 0.0 all-gather.14.cloned.1.call-start
  31.1 2.6 copy.30
  33.8 71.7 %all-gather.8.cloned.1.call-done = bf16[256,2048]{1,0:T(8,128)(2,1)} async-done(((bf16[256,256]{1,0:T(8,128)(2,1)}), bf16[256,2048]{1,0:T(8,128)(2,1)}) %all-gather.8.cloned.1.call-update) | async-done | bytes 1048592 | tf_op jit(solution)/shard_map/all_gather | solution.py:73
  105.4 1.5 fusion.6
  107.0 2.4 fusion.21
  109.4 0.7 fusion.53
  110.1 0.0 all-gather.14.cloned.1.call-update
  110.1 0.0 all-gather.16.cloned.1.call-start
  110.1 0.7 all-gather.16.cloned.1.call-update
  110.8 0.2 reduce-scatter.2.cloned.1.call-start
  111.0 4.5 iota_compare_fusion
  115.5 115.4 %all-gather.14.cloned.1.call-done = bf16[16384,1,128]{0,2,1:T(8,128)(2,1)} async-done(((bf16[256,1,128]{0,2,1:T(8,128)(2,1)}), bf16[16384,1,128]{0,2,1:T(8,128)(2,1)}) %all-gather.14.cloned.1.call-update) | async-done | bytes 4194320 | tf_op jit(solution)/shard_map/all_gather | solution.py:89
  230.9 17.5 %fusion = (f32[2,256]{1,0:T(2,128)S(1)}, f32[2,256,16384]{2,1,0:T(8,128)}) fusion(pred[256,16384]{1,0:T(8,128)(4,1)} %iota_compare_fusion, bf16[256,2,64]{0,2,1:T(8,128)(2,1)S(1)} %bitcast.65, bf16[16384,2,64]{0,2,1:T(8,128)(2,1)} %bitcast.67), kind=kOutput, calls=%fused_computation.5 | convolution fusion | flops 1098907136 | bytes 42010624 | tf_op jit(solution)/shard_map/qhe,khe->hqk/dot_general | solution.py:37
  248.4 16.3 %fusion.1 = f32[2,256]{1,0:T(2,128)S(1)} fusion(f32[2,256,16384]{2,1,0:T(8,128)} %get-tuple-element.14, f32[2,256]{1,0:T(2,128)S(1)} %broadcast_maximum_fusion, pred[256,16384]{1,0:T(8,128)(4,1)} %iota_compare_fusion), kind=kLoop, calls=%fused_computation.6 | loop fusion | flops 41942528 | bytes 37752832 | tf_op jit(solution)/shard_map/reduce_sum | solution.py:44
  264.7 89.2 %all-gather.16.cloned.1.call-done = bf16[16384,1,128]{0,2,1:T(8,128)(2,1)} async-done(((bf16[256,1,128]{0,2,1:T(8,128)(2,1)}), bf16[16384,1,128]{0,2,1:T(8,128)(2,1)}) %all-gather.16.cloned.1.call-update) | async-done | bytes 4194320 | tf_op jit(solution)/shard_map/all_gather | solution.py:90
  353.9 0.0 copy-start.1
  353.9 15.9 %fusion.16 = bf16[256,2,64]{0,2,1:T(8,128)(2,1)S(1)} fusion(bf16[16384,2,64]{0,2,1:T(8,128)(2,1)} %bitcast.68, f32[2,256,16384]{2,1,0:T(8,128)} %get-tuple-element.14, f32[2,256]{1,0:T(2,128)S(1)} %broadcast_maximum_fusion, pred[256,16384]{1,0:T(8,128)(4,1)} %iota_compare_fusion, f32[256,2]{0,1:T(2,128)S(1)} %bitcast.66), kind=kOutput, calls=%fused_computation.23 | convolution fusion | flops 1115750400 | bytes 42012672 | tf_op jit(solution)/shard_map/hqk,khe->hqe/dot_general | solution.py:45
  369.8 0.0 copy-done.1
  369.8 1.4 convolution_convert_fusion
  371.2 0.0 reduce-scatter.2.cloned.1.call-update
  371.2 0.0 all-gather.10.cloned.1.call-start
  371.3 88.2 %reduce-scatter.2.cloned.1.call-done = bf16[256,256]{1,0:T(8,128)(2,1)} async-done(((bf16[256,2048]{1,0:T(8,128)(2,1)}), bf16[256,256]{1,0:T(8,128)(2,1)}) %reduce-scatter.2.cloned.1.call-update) | async-done | bytes 131088 | tf_op jit(solution)/shard_map/reduce_scatter | solution.py:97
  459.5 2.6 add_convert_fusion
  462.1 0.0 copy-start.3
  462.1 0.0 all-gather.10.cloned.1.call-update
  462.2 0.3 all-gather.12.cloned.1.call-start
  462.4 0.3 all-gather.12.cloned.1.call-update
  462.7 64.2 %all-gather.10.cloned.1.call-done = bf16[256,2048]{1,0:T(8,128)(2,1)} async-done(((bf16[256,256]{1,0:T(8,128)(2,1)}), bf16[256,2048]{1,0:T(8,128)(2,1)}) %all-gather.10.cloned.1.call-update) | async-done | bytes 1048592 | tf_op jit(solution)/shard_map/all_gather | solution.py:99
  526.9 1.5 fusion.8
  528.4 115.3 %all-gather.12.cloned.1.call-done = bf16[4,2048,128]{2,1,0:T(8,128)(2,1)} async-done(((bf16[4,32,128]{2,1,0:T(8,128)(2,1)}), bf16[4,2048,128]{2,1,0:T(8,128)(2,1)}) %all-gather.12.cloned.1.call-update) | async-done | bytes 2097168 | tf_op jit(solution)/shard_map/all_gather | solution.py:104
  643.7 2.7 convolution_convert_fusion.1
  646.4 0.9 copy.31
  647.3 8.4 %all-to-all-start = ((bf16[256,4,128]{2,1,0:T(4,128)(2,1)}), bf16[256,4,128]{2,1,0:T(4,128)(2,1)S(1)}, u32[]{:S(2)}, u32[]{:S(2)}) async-start(bf16[256,4,128]{2,1,0:T(4,128)(2,1)} %copy.31), calls=%async_computation.1 | async-start | bytes 524288 | tf_op jit(solution)/shard_map/all_to_all | solution.py:109
  655.7 0.0 copy-done.3
  655.7 0.1 fusion.48
  655.8 0.1 copy.33
  655.9 0.1 reshape.301
  656.0 14.1 %all-to-all-done = bf16[256,4,128]{2,1,0:T(4,128)(2,1)S(1)} async-done(((bf16[256,4,128]{2,1,0:T(4,128)(2,1)}), bf16[256,4,128]{2,1,0:T(4,128)(2,1)S(1)}, u32[]{:S(2)}, u32[]{:S(2)}) %all-to-all-start) | async-done | bytes 262176 | tf_op jit(solution)/shard_map/all_to_all | solution.py:109
  670.1 0.4 bitcast_reduce_fusion
  670.5 0.2 bitcast_convert_fusion
  670.6 0.9 exponential_reduce_fusion
  671.5 0.1 reshape.286
  671.6 1.7 gather_fusion.2
  673.3 0.1 gather.20
  673.4 0.1 copy.34
  673.5 0.7 subtract_bitcast_fusion
  (17 shorter events, 0.1 us)
Async XLA Ops:
  7.2 16.0 %copy-start = (bf16[4,1024,256]{2,1,0:T(8,128)(2,1)S(1)}, bf16[4,1024,256]{2,1,0:T(8,128)(2,1)}, u32[]{:S(2)}) copy-start(bf16[4,1024,256]{2,1,0:T(8,128)(2,1)} %param.10) | copy-start | bytes 6291460
  7.2 15.8 %copy-start.2 = (s32[4]{0:T(128)S(1)}, s32[4]{0:T(128)}, u32[]{:S(2)}) copy-start(s32[4]{0:T(128)} %param.8) | copy-start | bytes 52
  7.2 98.2 %all-gather.8.cloned.1.call-start = ((), (), s32[]{:S(2)}) async-start(), calls=%async_computation.2 | async-start | bytes 1179648 | tf_op jit(solution)/shard_map/all_gather | solution.py:73
  8.1 4.9 collective-permute-start
  31.1 199.8 %all-gather.14.cloned.1.call-start = ((), (), s32[]{:S(2)}) async-start(), calls=%async_computation.6 | async-start | bytes 4259840 | tf_op jit(solution)/shard_map/all_gather | solution.py:89
  110.1 243.8 %all-gather.16.cloned.1.call-start = ((), (), s32[]{:S(2)}) async-start(), calls=%async_computation.7 | async-start | bytes 4259840 | tf_op jit(solution)/shard_map/all_gather | solution.py:90
  110.8 348.7 %reduce-scatter.2.cloned.1.call-start = ((), (), s32[]{:S(2)}) async-start(), calls=%async_computation.3 | async-start | bytes 1179648 | tf_op jit(solution)/shard_map/reduce_scatter | solution.py:97
  353.9 15.9 %copy-start.1 = (bf16[128,2048]{1,0:T(8,128)(2,1)S(1)}, bf16[128,2048]{1,0:T(8,128)(2,1)}, u32[]{:S(2)}) copy-start(bf16[128,2048]{1,0:T(8,128)(2,1)} %param.12) | copy-start | bytes 1572868
  371.2 155.7 %all-gather.10.cloned.1.call-start = ((), (), s32[]{:S(2)}) async-start(), calls=%async_computation.4 | async-start | bytes 1179648 | tf_op jit(solution)/shard_map/all_gather | solution.py:99
  462.1 193.6 %copy-start.3 = (s32[4,256]{1,0:T(4,128)S(1)}, s32[4,256]{1,0:T(4,128)}, u32[]{:S(2)}) copy-start(s32[4,256]{1,0:T(4,128)} %param.9) | copy-start | bytes 12292
  462.2 181.5 %all-gather.12.cloned.1.call-start = ((), (), s32[]{:S(2)}) async-start(), calls=%async_computation.5 | async-start | bytes 2129920 | tf_op jit(solution)/shard_map/all_gather | solution.py:104
  647.3 22.8 %all-to-all-start = ((bf16[256,4,128]{2,1,0:T(4,128)(2,1)}), bf16[256,4,128]{2,1,0:T(4,128)(2,1)S(1)}, u32[]{:S(2)}, u32[]{:S(2)}) async-start(bf16[256,4,128]{2,1,0:T(4,128)(2,1)} %copy.31), calls=%async_computation.1 | async-start | bytes 524288 | tf_op jit(solution)/shard_map/all_to_all | solution.py:109
Sparse Core Ops, SparseCore 0:
  31.2 74.1 all-gather.7
  110.2 120.6 all-gather.13
  232.9 120.8 all-gather.15
  371.4 88.1 reduce-scatter.1
  462.9 63.9 all-gather.9
  529.2 114.4 all-gather.11
where the time goes:
time: 681 us
  waiting for transfers between devices  561 us (82%)
  matrix products  39.9 us (6%)
  other arithmetic  32.4 us (5%)
  local copies, waits for them, and re-layouts  22.2 us (3%)
  between operations  14.3 us (2%)
  starting transfers between devices  11 us (2%)
    all_gather x1, waiting for transfers between devices, shards(): key_rows = lax.all_gather(keys, 'seq', axis=0, tiled=True)  115 us
    all_gather x1, waiting for transfers between devices, shards(): lax.all_gather(heads_w, 'seq', axis=1, tiled=True)  115 us
    all_gather x1, waiting for transfers between devices, shards(): value_rows = lax.all_gather(values, 'seq', axis=0, tiled=True)  89.2 us
    reduce_scatter x1, waiting for transfers between devices, shards(): lax.psum_scatter(terms.astype(jnp.bfloat16), 'head', scatter_dimension=1,...  88.2 us
    all_gather x1, waiting for transfers between devices, shards(): x_full = lax.all_gather(x_part, 'head', axis=1, tiled=True)  71.7 us
    all_gather x1, waiting for transfers between devices, shards(): resid = lax.all_gather(resid_part, 'head', axis=1, tiled=True)  64.2 us
    dot_general x1, matrix products, update(): jnp.einsum('qhe,khe->hqk', query_heads, key_heads, preferred_element_type...  17.5 us
    reduce_sum x1, other arithmetic, update(): totals = jnp.sum(weights, axis=-1)  16.3 us
  transfers between devices with their start and end apart: 8, of which 8 were waited for; matrix products, arithmetic and copies ran while one was open for 6% of the time, Pallas kernels for 0%

commit v1 on v0

v1 whole, which is shorter than its diff:
```python
import functools
import math

import jax
import jax.numpy as jnp
from jax import lax
from jax.experimental import pallas as pl
from jax.experimental.pallas import tpu as pltpu
from jax.sharding import Mesh, PartitionSpec as P

HD = 64
LOW = -1e30
BF = jnp.bfloat16
F32 = jnp.float32
SEQ = ("y", "z", "c")
HEAD = ("x", "h")
VMEM = pl.BlockSpec(memory_space=pltpu.VMEM)
SMEM = pl.BlockSpec(memory_space=pltpu.SMEM)
PARAMS = pltpu.CompilerParams(vmem_limit_bytes=48 * 1024 * 1024)


def flip(array, axis, by):
    size = lax.axis_size(axis)
    return lax.ppermute(array, axis, [(i, i ^ by) for i in range(size)])


def shift(array, axis, by):
    size = lax.axis_size(axis)
    return lax.ppermute(array, axis, [(i, (i + by) % size) for i in range(size)])


def gather(array, axis):
    size = lax.axis_size(axis)
    copies = jnp.broadcast_to(array[None], (size,) + array.shape)
    return lax.all_to_all(copies, axis, 0, 0, tiled=True)


def gather_heads(array):
    other = flip(array, "h", 1)
    low = lax.axis_index("h") == 0
    pair = jnp.stack([jnp.where(low, array, other), jnp.where(low, other, array)])
    return gather(pair, "x").reshape((8,) + array.shape)


def sinusoid(frames_f, columns, width):
    half = width // 2
    freq = jnp.exp(-math.log(10000.0) * (columns % half).astype(F32) / half)
    angle = frames_f[:, None] * freq[None, :]
    return jnp.where(columns[None, :] < half, jnp.sin(angle), jnp.cos(angle))


def project_kernel(x_ref, w_ref, q_ref, kv_ref):
    parts, _, width = x_ref.shape
    squares = 0.0
    for i in range(parts):
        xi = x_ref[i].astype(F32)
        squares = squares + jnp.sum(xi * xi, axis=-1, keepdims=True)
    r = lax.rsqrt(squares / (parts * width) + 1e-05)
    sums = [0.0, 0.0, 0.0]
    for i in range(parts):
        ni = (x_ref[i].astype(F32) * r).astype(BF)
        for j in range(3):
            sums[j] = sums[j] + jnp.dot(
                ni, w_ref[j, i * width : (i + 1) * width, :], preferred_element_type=F32
            )
    q_ref[...] = sums[0].astype(BF)
    kv_ref[:, :128] = sums[1].astype(BF)
    kv_ref[:, 128:] = sums[2].astype(BF)


def project(x8, w):
    rows = x8.shape[1]
    return pl.pallas_call(
        project_kernel,
        out_shape=(
            jax.ShapeDtypeStruct((rows, 128), BF),
            jax.ShapeDtypeStruct((rows, 256), BF),
        ),
        in_specs=[VMEM, VMEM],
        out_specs=(VMEM, VMEM),
        compiler_params=PARAMS,
        name="project",
    )(x8, w)


def attend_kernel(place_ref, q_ref, kv_ref, o_ref):
    rows = q_ref.shape[1]
    blocks = kv_ref.shape[0]
    plane = pl.program_id(0)
    mine, slot = place_ref[0], place_ref[1]
    lane = lax.broadcasted_iota(jnp.int32, (rows, 128), 1)

    def put_stats(lse):
        stats = jnp.zeros((rows, 128), F32)
        rest = list(lse)
        for part in range(3):
            for h in range(2):
                top = rest[h].astype(BF).astype(F32)
                rest[h] = rest[h] - top
                stats = jnp.where(lane == 2 * part + h, top, stats)
        turned = jnp.transpose(stats)[:16, :].astype(BF)
        o_ref[0, rows : rows + 16, :] = turned[:, :128]
        o_ref[0, rows + 16 : rows + 32, :] = turned[:, 128:]

    def compute(masked):
        q = q_ref[0] * jnp.asarray(0.125, BF)
        lse, outs = [], []
        for h in range(2):
            qh = jnp.where((lane >= 64) == (h == 1), q, jnp.zeros_like(q))
            scores = []
            for j in range(blocks):
                s = lax.dot_general(
                    qh, kv_ref[j, :, :128], (((1,), (1,)), ((), ())), preferred_element_type=F32
                )
                if masked:
                    first = (slot ^ j) * rows - slot * rows
                    row = lax.broadcasted_iota(jnp.int32, s.shape, 0)
                    col = lax.broadcasted_iota(jnp.int32, s.shape, 1)
                    s = jnp.where(col - row <= -first, s, LOW)
                scores.append(s)
            top = functools.reduce(jnp.maximum, scores)
            m = jnp.max(top, axis=-1, keepdims=True)
            total = 0.0
            acc = 0.0
            for j in range(blocks):
                p = jnp.exp(scores[j] - m)
                total = total + p
                acc = acc + jnp.dot(p.astype(BF), kv_ref[j, :, 128:], preferred_element_type=F32)
            l = jnp.sum(total, axis=-1, keepdims=True)
            outs.append(acc / l)
            lse.append(m + jnp.log(l))
        o_ref[0, :rows, :] = jnp.where(lane < 64, outs[0], outs[1]).astype(BF)
        put_stats(lse)

    @pl.when(plane < mine)
    def _():
        o_ref[0, :rows, :] = jnp.zeros((rows, 128), BF)
        put_stats([jnp.full((rows, 1), LOW, F32)] * 2)

    @pl.when(plane == mine)
    def _():
        compute(True)

    @pl.when(plane > mine)
    def _():
        compute(False)


def attend(place, q8, kv8):
    planes, rows, _ = q8.shape
    return pl.pallas_call(
        attend_kernel,
        grid_spec=pltpu.PrefetchScalarGridSpec(
            num_scalar_prefetch=1,
            grid=(planes,),
            in_specs=[
                pl.BlockSpec((1, rows, 128), lambda i, s: (i, 0, 0)),
                pl.BlockSpec(kv8.shape, lambda i, s: (0, 0, 0)),
            ],
            out_specs=pl.BlockSpec((1, rows + 32, 128), lambda i, s: (i, 0, 0)),
        ),
        out_shape=jax.ShapeDtypeStruct((planes, rows + 32, 128), BF),
        compiler_params=PARAMS,
        name="attend",
    )(place, q8, kv8)


def merge_kernel(o_ref, out_ref):
    planes = o_ref.shape[0]
    rows = out_ref.shape[0]
    lane = lax.broadcasted_iota(jnp.int32, (128, 128), 1)
    for half in range(rows // 128):
        lses = []
        for i in range(planes):
            st = o_ref[i, rows + 16 * half : rows + 16 * half + 16, :].astype(F32)
            lses.append(st[0:2] + st[2:4] + st[4:6])
        top = functools.reduce(jnp.maximum, lses)
        weights = [jnp.exp(v - top) for v in lses]
        total = functools.reduce(jnp.add, weights)
        pad = jnp.zeros((128 - 2 * planes, 128), F32)
        w = jnp.transpose(jnp.concatenate([v / total for v in weights] + [pad], axis=0))
        acc = 0.0
        for i in range(planes):
            wi = jnp.where(lane < 64, w[:, 2 * i : 2 * i + 1], w[:, 2 * i + 1 : 2 * i + 2])
            acc = acc + wi * o_ref[i, 128 * half : 128 * half + 128, :].astype(F32)
        out_ref[128 * half : 128 * half + 128, :] = acc.astype(BF)


def merge(partial):
    rows = partial.shape[1] - 32
    return pl.pallas_call(
        merge_kernel,
        out_shape=jax.ShapeDtypeStruct((rows, 128), BF),
        in_specs=[VMEM],
        out_specs=VMEM,
        compiler_params=PARAMS,
        name="merge",
    )(partial)


def tail_kernel(place_ref, att_ref, near_ref, far_ref, x_ref, hw_ref, tgt_ref, mixed_ref, stat_ref, a_s, m_s, f_s):
    parts, rows, width = x_ref.shape
    head, core = place_ref[0], place_ref[1]
    for i in range(parts):
        a_s[:, 128 * i : 128 * i + 128] = att_ref[place_ref[2 + i]]
    half = near_ref.shape[-1]
    a = a_s[...]
    for ref, which in ((near_ref, core), (far_ref, 1 - core)):
        w = ref[...].reshape(parts * 128, half)
        got = jnp.dot(a, w, preferred_element_type=F32)
        m_s[:, pl.ds(pl.multiple_of(which * half, half), half)] = got.astype(BF)
    mixed_ref[...] = m_s[:, pl.ds(pl.multiple_of(head * width, width), width)]
    squares = 0.0
    for i in range(parts):
        resid = (x_ref[i].astype(F32) + m_s[:, i * width : (i + 1) * width].astype(F32)).astype(BF)
        wide = resid.astype(F32)
        squares = squares + jnp.sum(wide * wide, axis=-1, keepdims=True)
        f_s[:, i * width : (i + 1) * width] = resid
    r = lax.rsqrt(squares / (parts * width) + 1e-05)
    f_s[...] = (f_s[...].astype(F32) * r).astype(BF)
    final = f_s[...]
    books = hw_ref.shape[1]
    lane = lax.broadcasted_iota(jnp.int32, (rows, 128), 1)
    stats = jnp.zeros((rows, 128), F32)
    for b in range(books):
        w = hw_ref[:, b].reshape(parts * width, 128)
        logits = jnp.dot(final, w, preferred_element_type=F32)
        g = jnp.max(logits, axis=-1, keepdims=True)
        s = jnp.sum(jnp.exp(logits - g), axis=-1, keepdims=True)
        hit = lane + 128 * head == tgt_ref[:, b : b + 1]
        picked = jnp.sum(jnp.where(hit, logits, 0.0), axis=-1, keepdims=True)
        stats = jnp.where(lane == b, g, stats)
        stats = jnp.where(lane == books + b, s, stats)
        stats = jnp.where(lane == 2 * books + b, picked, stats)
    stat_ref[...] = stats


def tail(place, att8, near, far, x8, hw, tgt):
    parts, rows, width = x8.shape
    return pl.pallas_call(
        tail_kernel,
        out_shape=(
            jax.ShapeDtypeStruct((rows, width), BF),
            jax.ShapeDtypeStruct((rows, 128), F32),
        ),
        in_specs=[SMEM] + [VMEM] * 6,
        out_specs=(VMEM, VMEM),
        scratch_shapes=[
            pltpu.VMEM((rows, parts * 128), BF),
            pltpu.VMEM((rows, parts * width), BF),
            pltpu.VMEM((rows, parts * width), BF),
        ],
        compiler_params=PARAMS,
        name="tail",
    )(place, att8, near, far, x8, hw, tgt)


def loss_kernel(s_ref, out_ref):
    books, share = out_ref.shape
    parts = s_ref.shape[0]
    top = s_ref[0]
    for i in range(1, parts):
        top = jnp.maximum(top, s_ref[i])
    total = 0.0
    picked = 0.0
    for i in range(parts):
        v = s_ref[i]
        total = total + jnp.exp(v - top) * pltpu.roll(v, 128 - books, 1)
        picked = picked + pltpu.roll(v, 128 - 2 * books, 1)
    loss = top + jnp.log(total) - picked
    full = jnp.concatenate([loss, jnp.zeros((128 - share, 128), F32)], axis=0)
    out_ref[...] = jnp.transpose(full)[:books, :share]


def final_loss(spread, books):
    return pl.pallas_call(
        loss_kernel,
        out_shape=jax.ShapeDtypeStruct((books, spread.shape[1]), F32),
        in_specs=[VMEM],
        out_specs=VMEM,
        name="loss",
    )(spread)


def shards(codes, delays, targets, embed, wqkv, wout, heads_w):
    books, rows = codes.shape
    vocab, width = embed.shape[1:]
    y, z, c = (lax.axis_index(a) for a in SEQ)
    x, h = (lax.axis_index(a) for a in HEAD)
    head = x * 2 + h
    slot = z * 2 + c
    first = (y * 8 + slot) * rows

    hw = lax.all_gather(heads_w, SEQ, axis=0)

    devices = lax.axis_size(SEQ)
    rim = lax.ppermute(codes[:, rows - 3 :], SEQ, [(i, i + 1) for i in range(devices - 1)])
    half = wout.shape[1] // 2
    own_half = lax.dynamic_slice_in_dim(wout, c * half, half, 1)
    pair = jnp.stack([own_half, flip(own_half, "h", 1)])
    near = jnp.concatenate([pair] + [shift(pair, "x", k) for k in (1, 2, 3)])
    far = flip(near, "c", 1)
    w3 = jnp.transpose(wqkv, (1, 0, 2))

    columns = head * width + jnp.arange(width, dtype=jnp.int32)
    local = jnp.arange(rows, dtype=jnp.int32)
    frame_pos = first + local
    pos = lax.optimization_barrier(sinusoid(frame_pos.astype(F32), columns, width * 8))

    extended = jnp.concatenate([rim, codes], axis=1)
    ids = jnp.zeros((books, rows), jnp.int32)
    for d in range(4):
        ids = jnp.where(delays[:, None] == d, extended[:, 3 - d : 3 - d + rows], ids)
    ids = jnp.where(frame_pos[None, :] >= delays[:, None], ids, -1)
    hot = (jnp.transpose(ids)[:, :, None] == jnp.arange(vocab, dtype=jnp.int32)).astype(BF)
    summed = jnp.dot(
        hot.reshape(rows, books * vocab),
        embed.reshape(books * vocab, width),
        preferred_element_type=F32,
    )
    x_part = (summed + pos).astype(BF)

    x8 = gather_heads(x_part)
    q, kv = project(x8, w3)

    q8 = gather(q, "y")
    one = flip(kv, "z", 1)
    kv2 = jnp.stack([kv, one])
    kv4 = jnp.concatenate([kv2, flip(kv2, "z", 2)])
    other = flip(kv4, "c", 1)
    kv8 = jnp.stack([kv4, other], axis=1).reshape((8,) + kv.shape)

    partial = attend(jnp.stack([y, slot]).astype(jnp.int32), q8, kv8)
    spread = lax.all_to_all(partial, "y", 0, 0, tiled=True)
    att8 = gather_heads(merge(spread))

    order = [((x - k) % 4) * 2 + (h ^ j) for k in range(4) for j in range(2)]
    place = jnp.stack([head, c] + order).astype(jnp.int32)
    mixed, stats = tail(place, att8, near, far, x8, hw, jnp.transpose(targets))
    shares = lax.all_to_all(stats.reshape(8, rows // 8, 128), HEAD, 0, 0, tiled=True)
    return (mixed, final_loss(shares, books))


def solution(mesh):
    fine = Mesh(mesh.devices.reshape(8, 4, 2, 4, 2), SEQ + HEAD)
    placed = (
        P(None, SEQ),
        P(),
        P(None, SEQ),
        P(None, None, HEAD),
        P(None, None, HEAD),
        P(HEAD, None),
        P(None, SEQ, HEAD),
    )
    return jax.shard_map(
        shards,
        mesh=fine,
        in_specs=placed,
        out_specs=(P(SEQ, HEAD), P(None, SEQ + HEAD)),
        check_vma=False,
    )
```

time: 681 us -> 206 us (0.30)
  the two profiles are of different devices: /device:TPU:64 before, /device:TPU:2 now
where the time goes in v1:
time: 206 us; the launch traced here: 205 us
  starting transfers between devices  66.5 us (32%)
  blocking collectives  42.1 us (20%)
  waiting for transfers between devices  30.8 us (15%)
  Pallas kernels  26.5 us (13%)
  local copies, waits for them, and re-layouts  17.4 us (8%)
  between operations  14.3 us (7%)
  other arithmetic  6.48 us (3%)
    ppermute x7, starting transfers between devices, flip(): return lax.ppermute(array, axis, [(i, i ^ by) for i in range(size)])  37.5 us
    all_to_all x1, blocking collectives, shards(): spread = lax.all_to_all(partial, 'y', 0, 0, tiled=True)  23.6 us
    all_to_all x1, blocking collectives, shards(): lax.all_to_all(stats.reshape(8, rows // 8, 128), HEAD, 0, 0, tiled=True)  18.4 us
    pallas_call x1, Pallas kernels, attend(): pl.pallas_call(attend_kernel, grid_spec=pltpu.PrefetchScalarGridSpec(num_...  17.2 us
    all_to_all x3, starting transfers between devices, gather(): return lax.all_to_all(copies, axis, 0, 0, tiled=True)  16.9 us
    all_to_all x3, waiting for transfers between devices, gather(): return lax.all_to_all(copies, axis, 0, 0, tiled=True)  12 us
    ppermute x7, waiting for transfers between devices, flip(): return lax.ppermute(array, axis, [(i, i ^ by) for i in range(size)])  11.6 us
    unnamed x17, local copies, waits for them, and re-layouts  10.7 us
  transfers between devices with their start and end apart: 15, of which 6 were waited for; matrix products, arithmetic and copies ran while one was open for 8% of the time, Pallas kernels for 9%

profile of v1, /device:TPU:2, one launch (start us, length us, event | category | flops | bytes accessed | tf_op | source)
XLA Modules:
  0.0 204.9 jit_solution(15341155804103513318)
XLA Ops:
  7.2 0.0 copy-start
  7.2 0.9 slice.12
  8.1 1.7 collective-permute-start
  9.9 1.0 fusion.5
  10.9 0.7 broadcast_compare_fusion.3
  11.6 0.0 collective-permute-done
  11.6 0.9 fusion.10
  12.5 0.0 copy-done
  12.5 0.9 fusion.4
  13.4 10.9 %collective-permute-start.1 = (bf16[256,256]{1,0:T(8,128)(2,1)S(1)}, bf16[256,256]{1,0:T(8,128)(2,1)S(1)}, u32[]{:S(2)}, u32[]{:S(2)}) collective-permute-start(bf16[256,256]{1,0:T(8,128)(2,1)S(1)} %fusion.4), channel_id=1, source_target_pairs={{0,1},{1,0},{2,3},{3,2},{4,5},{5,4},{6,7},{7,6},{8,9},{9,8},{10,11... | collective-permute-start | bytes 393224 | tf_op jit(solution)/shard_map/ppermute | solution.py:24
  24.3 3.3 %collective-permute-done.1 = bf16[256,256]{1,0:T(8,128)(2,1)S(1)} collective-permute-done((bf16[256,256]{1,0:T(8,128)(2,1)S(1)}, bf16[256,256]{1,0:T(8,128)(2,1)S(1)}, u32[]{:S(2)}, u32[]{:S(2)}) %collective-permute-start.1) | collective-permute-done | bytes 131104 | tf_op jit(solution)/shard_map/ppermute | solution.py:24
  27.7 1.1 broadcast_in_dim.74
  28.7 6.2 %all-to-all-start = ((bf16[4,2,256,256]{3,2,1,0:T(8,128)(2,1)}), bf16[4,2,256,256]{3,2,1,0:T(8,128)(2,1)S(1)}, u32[]{:S(2)}, u32[]{:S(2)}) async-start(bf16[4,2,256,256]{3,2,1,0:T(8,128)(2,1)} %broadcast_in_dim.74), calls=%async_computation | async-start | bytes 2097152 | tf_op jit(solution)/shard_map/all_to_all | solution.py:35
  34.9 0.0 all-gather.3.cloned.1.call-start
  34.9 0.7 all-gather.3.cloned.1.call-update
  35.7 1.8 constant_dynamic-update-slice_fusion.4
  37.5 6.8 %collective-permute-start.6 = (bf16[128,1024]{1,0:T(8,128)(2,1)}, bf16[128,1024]{1,0:T(8,128)(2,1)S(1)}, u32[]{:S(2)}, u32[]{:S(2)}) collective-permute-start(bf16[128,1024]{1,0:T(8,128)(2,1)} %get-tuple-element.11), channel_id=1, source_target_pairs={{0,1},{1,0},{2,3},{3,2},{4,5},{5,4},{6,7},{7,6},{8,9},{9,8},{10,11... | collective-permute-start | bytes 786440 | tf_op jit(solution)/shard_map/ppermute | solution.py:24
  44.3 4.8 %all-to-all-done = bf16[4,2,256,256]{3,2,1,0:T(8,128)(2,1)S(1)} async-done(((bf16[4,2,256,256]{3,2,1,0:T(8,128)(2,1)}), bf16[4,2,256,256]{3,2,1,0:T(8,128)(2,1)S(1)}, u32[]{:S(2)}, u32[]{:S(2)}) %all-to-all-start) | async-done | bytes 1048608 | tf_op jit(solution)/shard_map/all_to_all | solution.py:35
  49.2 1.4 copy-done.3
  50.6 1.2 project.1
  51.8 6.2 %collective-permute-start.2 = (bf16[256,256]{1,0:T(8,128)(2,1)S(1)}, bf16[256,256]{1,0:T(8,128)(2,1)S(1)}, u32[]{:S(2)}, u32[]{:S(2)}) collective-permute-start(bf16[256,256]{1,0:T(8,128)(2,1)S(1)} %get-tuple-element.7), channel_id=1, source_target_pairs={{0,16},{16,0},{32,48},{48,32},{1,17},{17,1},{33,49},{49,33},{2,18}... | collective-permute-start | bytes 393224 | tf_op jit(solution)/shard_map/ppermute | solution.py:24
  58.1 5.5 %collective-permute-done.2 = bf16[256,256]{1,0:T(8,128)(2,1)S(1)} collective-permute-done((bf16[256,256]{1,0:T(8,128)(2,1)S(1)}, bf16[256,256]{1,0:T(8,128)(2,1)S(1)}, u32[]{:S(2)}, u32[]{:S(2)}) %collective-permute-start.2) | collective-permute-done | bytes 131104 | tf_op jit(solution)/shard_map/ppermute | solution.py:24
  63.6 0.7 pad_maximum_fusion.4
  64.3 2.3 %collective-permute-start.3 = (bf16[2,256,256]{2,1,0:T(8,128)(2,1)}, bf16[2,256,256]{2,1,0:T(8,128)(2,1)}, u32[]{:S(2)}, u32[]{:S(2)}) collective-permute-start(bf16[2,256,256]{2,1,0:T(8,128)(2,1)} %pad_maximum_fusion.4), channel_id=1, source_target_pairs={{0,32},{16,48},{32,0},{48,16},{1,33},{17,49},{33,1},{49,17},{2,34}... | collective-permute-start | bytes 786440 | tf_op jit(solution)/shard_map/ppermute | solution.py:24
  66.6 0.0 collective-permute-done.6
  66.6 1.8 pad_maximum_fusion.2
  68.5 3.3 %collective-permute-start.7 = (bf16[2,128,1024]{2,1,0:T(8,128)(2,1)}, bf16[2,128,1024]{2,1,0:T(8,128)(2,1)}, u32[]{:S(2)}, u32[]{:S(2)}) collective-permute-start(bf16[2,128,1024]{2,1,0:T(8,128)(2,1)} %pad_maximum_fusion.2), channel_id=1, source_target_pairs={{0,2},{2,4},{4,6},{6,0},{1,3},{3,5},{5,7},{7,1},{8,10},{10,12},{12... | collective-permute-start | bytes 1572872 | tf_op jit(solution)/shard_map/ppermute | solution.py:29
  71.8 3.8 %collective-permute-start.8 = (bf16[2,128,1024]{2,1,0:T(8,128)(2,1)}, bf16[2,128,1024]{2,1,0:T(8,128)(2,1)}, u32[]{:S(2)}, u32[]{:S(2)}) collective-permute-start(bf16[2,128,1024]{2,1,0:T(8,128)(2,1)} %pad_maximum_fusion.2), channel_id=1, source_target_pairs={{0,4},{2,6},{4,0},{6,2},{1,5},{3,7},{5,1},{7,3},{8,12},{10,14},{12... | collective-permute-start | bytes 1572872 | tf_op jit(solution)/shard_map/ppermute | solution.py:29
  75.6 3.3 %collective-permute-start.9 = (bf16[2,128,1024]{2,1,0:T(8,128)(2,1)}, bf16[2,128,1024]{2,1,0:T(8,128)(2,1)}, u32[]{:S(2)}, u32[]{:S(2)}) collective-permute-start(bf16[2,128,1024]{2,1,0:T(8,128)(2,1)} %pad_maximum_fusion.2), channel_id=1, source_target_pairs={{0,6},{2,0},{4,2},{6,4},{1,7},{3,1},{5,3},{7,5},{8,14},{10,8},{12,... | collective-permute-start | bytes 1572872 | tf_op jit(solution)/shard_map/ppermute | solution.py:29
  78.8 0.9 broadcast_in_dim.75
  79.7 6.3 %all-to-all-start.1 = ((bf16[8,256,128]{2,1,0:T(8,128)(2,1)}), bf16[8,256,128]{2,1,0:T(8,128)(2,1)}, u32[]{:S(2)}, u32[]{:S(2)}) async-start(bf16[8,256,128]{2,1,0:T(8,128)(2,1)} %broadcast_in_dim.75), calls=%async_computation.1 | async-start | bytes 1048576 | tf_op jit(solution)/shard_map/all_to_all | solution.py:35
  86.0 0.0 collective-permute-done.3
  86.0 1.1 fusion.19
  87.1 1.9 collective-permute-start.4
  89.0 0.7 constant_dynamic-update-slice_fusion.3
  89.8 0.0 collective-permute-done.7
  89.8 1.9 constant_dynamic-update-slice_fusion.2
  91.6 0.0 collective-permute-done.8
  91.6 1.9 constant_dynamic-update-slice_fusion.1
  93.5 6.5 %collective-permute-done.9 = bf16[2,128,1024]{2,1,0:T(8,128)(2,1)} collective-permute-done((bf16[2,128,1024]{2,1,0:T(8,128)(2,1)}, bf16[2,128,1024]{2,1,0:T(8,128)(2,1)}, u32[]{:S(2)}, u32[]{:S(2)}) %collective-permute-start.9) | collective-permute-done | bytes 524320 | tf_op jit(solution)/shard_map/ppermute | solution.py:29
  100.1 1.9 constant_dynamic-update-slice_fusion.near_ref
  101.9 1.9 collective-permute-start.10
  103.8 0.1 pad_add_fusion.1.place_ref
  103.9 0.0 collective-permute-done.4
  103.9 0.1 pad_maximum_fusion
  104.0 1.0 copy.11
  105.1 0.0 all-to-all-done.1.q_ref
  105.1 1.2 copy-done.1
  106.3 17.2 %attend.1 = bf16[8,288,128]{2,1,0:T(8,128)(2,1)S(1)} custom-call(s32[2]{0:T(128)S(1)} %pad_add_fusion.1.place_ref, bf16[8,256,128]{2,1,0:T(8,128)(2,1)} %all-to-all-done.1.q_ref, bf16[8,256,256]{2,1,0:T(8,128)(2,1)S(1)} %bitcast.47), custom_call_target="tpu_custom_call" | custom-call | tf_op jit(solution)/shard_map/attend/pallas_call | solution.py:151
  123.5 0.0 copy-start.5
  123.5 23.6 %all_to_all.25.o_ref = bf16[8,288,128]{2,1,0:T(8,128)(2,1)S(1)} all-to-all(bf16[8,288,128]{2,1,0:T(8,128)(2,1)S(1)} %attend.1), channel_id=1, replica_groups=mesh['y'=8,'z'=4,'c'=2,'x'=4,'h'=2] {'y'}, dimensions={0} | all-to-all | bytes 1179648 | tf_op jit(solution)/shard_map/all_to_all | solution.py:334
  147.1 0.8 merge.1
  147.9 7.3 %collective-permute-start.5 = (bf16[256,128]{1,0:T(8,128)(2,1)S(1)}, bf16[256,128]{1,0:T(8,128)(2,1)S(1)}, u32[]{:S(2)}, u32[]{:S(2)}) collective-permute-start(bf16[256,128]{1,0:T(8,128)(2,1)S(1)} %merge.1), channel_id=1, source_target_pairs={{0,1},{1,0},{2,3},{3,2},{4,5},{5,4},{6,7},{7,6},{8,9},{9,8},{10,11... | collective-permute-start | bytes 196616 | tf_op jit(solution)/shard_map/ppermute | solution.py:24
  155.3 2.8 %collective-permute-done.5 = bf16[256,128]{1,0:T(8,128)(2,1)S(1)} collective-permute-done((bf16[256,128]{1,0:T(8,128)(2,1)S(1)}, bf16[256,128]{1,0:T(8,128)(2,1)S(1)}, u32[]{:S(2)}, u32[]{:S(2)}) %collective-permute-start.5) | collective-permute-done | bytes 65568 | tf_op jit(solution)/shard_map/ppermute | solution.py:24
  158.1 0.9 broadcast_in_dim.76
  158.9 4.4 %all-to-all-start.3 = ((bf16[4,2,256,128]{3,2,1,0:T(8,128)(2,1)}), bf16[4,2,256,128]{3,2,1,0:T(8,128)(2,1)}, u32[]{:S(2)}, u32[]{:S(2)}) async-start(bf16[4,2,256,128]{3,2,1,0:T(8,128)(2,1)} %broadcast_in_dim.76), calls=%async_computation.3 | async-start | bytes 1048576 | tf_op jit(solution)/shard_map/all_to_all | solution.py:35
  163.3 0.1 copy.12
  163.5 0.1 stack.97.place_ref
  163.6 0.0 collective-permute-done.10.far_ref
  163.6 7.1 %all-to-all-done.3 = bf16[4,2,256,128]{3,2,1,0:T(8,128)(2,1)} async-done(((bf16[4,2,256,128]{3,2,1,0:T(8,128)(2,1)}), bf16[4,2,256,128]{3,2,1,0:T(8,128)(2,1)}, u32[]{:S(2)}, u32[]{:S(2)}) %all-to-all-start.3) | async-done | bytes 524320 | tf_op jit(solution)/shard_map/all_to_all | solution.py:35
  170.7 1.6 copy-done.2
  172.3 5.6 %tail.1 = (bf16[256,256]{1,0:T(8,128)(2,1)}, f32[256,128]{1,0:T(8,128)S(1)}) custom-call(s32[10]{0:T(128)S(1)} %stack.97.place_ref, bf16[8,256,128]{2,1,0:T(8,128)(2,1)} %bitcast.25.att_ref, bf16[8,128,1024]{2,1,0:T(8,128)(2,1)S(1)} %copy-done.2, bf16[8,128,1024]{2,1,0:T(8,128)(2,1)} %collective-permute-done.10.far_ref, bf16[8,256,256]{2,1,0:T(8,128)(2,1)S(1)} %bitcast.46, ...), custom_call_target="tpu_custom_call" | custom-call | tf_op jit(solution)/shard_map/tail/pallas_call | solution.py:240
  177.9 18.4 %all_to_all.26.s_ref = f32[8,32,128]{2,1,0:T(8,128)} all-to-all(f32[8,32,128]{2,1,0:T(8,128)S(1)} %bitcast.52), channel_id=1, replica_groups=mesh['y'=8,'z'=4,'c'=2,'x'=4,'h'=2] {'x','h'}, dimensions={0} | all-to-all | bytes 262144 | tf_op jit(solution)/shard_map/all_to_all | solution.py:340
  196.3 1.7 loss.1
  (15 shorter events, 0.1 us)
Async XLA Ops:
  7.2 5.3 %copy-start = (bf16[4,1024,256]{2,1,0:T(8,128)(2,1)S(1)}, bf16[4,1024,256]{2,1,0:T(8,128)(2,1)}, u32[]{:S(2)}) copy-start(bf16[4,1024,256]{2,1,0:T(8,128)(2,1)} %param.10) | copy-start | bytes 6291460
  8.1 3.5 %collective-permute-start = (s32[4,3]{1,0:T(4,128)S(1)}, s32[4,3]{1,0:T(4,128)S(1)}, u32[]{:S(2)}, u32[]{:S(2)}) collective-permute-start(s32[4,3]{1,0:T(4,128)S(1)} %slice.12), channel_id=1, source_target_pairs={{0,8},{8,16},{16,24},{24,32},{32,40},{40,48},{48,56},{56,64},{64,7... | collective-permute-start | bytes 152 | tf_op jit(solution)/shard_map/ppermute | solution.py:297
  13.4 14.3 %collective-permute-start.1 = (bf16[256,256]{1,0:T(8,128)(2,1)S(1)}, bf16[256,256]{1,0:T(8,128)(2,1)S(1)}, u32[]{:S(2)}, u32[]{:S(2)}) collective-permute-start(bf16[256,256]{1,0:T(8,128)(2,1)S(1)} %fusion.4), channel_id=1, source_target_pairs={{0,1},{1,0},{2,3},{3,2},{4,5},{5,4},{6,7},{7,6},{8,9},{9,8},{10,11... | collective-permute-start | bytes 393224 | tf_op jit(solution)/shard_map/ppermute | solution.py:24
  28.7 20.4 %all-to-all-start = ((bf16[4,2,256,256]{3,2,1,0:T(8,128)(2,1)}), bf16[4,2,256,256]{3,2,1,0:T(8,128)(2,1)S(1)}, u32[]{:S(2)}, u32[]{:S(2)}) async-start(bf16[4,2,256,256]{3,2,1,0:T(8,128)(2,1)} %broadcast_in_dim.74), calls=%async_computation | async-start | bytes 2097152 | tf_op jit(solution)/shard_map/all_to_all | solution.py:35
  34.9 135.8 %all-gather.3.cloned.1.call-start = ((), (), s32[]{:S(2)}) async-start(), calls=%async_computation.5 | async-start | bytes 2129920 | tf_op jit(solution)/shard_map/all_gather | solution.py:294
  37.5 29.2 %collective-permute-start.6 = (bf16[128,1024]{1,0:T(8,128)(2,1)}, bf16[128,1024]{1,0:T(8,128)(2,1)S(1)}, u32[]{:S(2)}, u32[]{:S(2)}) collective-permute-start(bf16[128,1024]{1,0:T(8,128)(2,1)} %get-tuple-element.11), channel_id=1, source_target_pairs={{0,1},{1,0},{2,3},{3,2},{4,5},{5,4},{6,7},{7,6},{8,9},{9,8},{10,11... | collective-permute-start | bytes 786440 | tf_op jit(solution)/shard_map/ppermute | solution.py:24
  49.2 1.4 copy-start.3
  51.8 11.7 %collective-permute-start.2 = (bf16[256,256]{1,0:T(8,128)(2,1)S(1)}, bf16[256,256]{1,0:T(8,128)(2,1)S(1)}, u32[]{:S(2)}, u32[]{:S(2)}) collective-permute-start(bf16[256,256]{1,0:T(8,128)(2,1)S(1)} %get-tuple-element.7), channel_id=1, source_target_pairs={{0,16},{16,0},{32,48},{48,32},{1,17},{17,1},{33,49},{49,33},{2,18}... | collective-permute-start | bytes 393224 | tf_op jit(solution)/shard_map/ppermute | solution.py:24
  63.6 3.1 %copy-start.4 = (bf16[256,256]{1,0:T(8,128)(2,1)}, bf16[256,256]{1,0:T(8,128)(2,1)S(1)}, u32[]{:S(2)}) copy-start(bf16[256,256]{1,0:T(8,128)(2,1)S(1)} %collective-permute-done.2) | copy-start | bytes 393220
  64.3 21.7 %collective-permute-start.3 = (bf16[2,256,256]{2,1,0:T(8,128)(2,1)}, bf16[2,256,256]{2,1,0:T(8,128)(2,1)}, u32[]{:S(2)}, u32[]{:S(2)}) collective-permute-start(bf16[2,256,256]{2,1,0:T(8,128)(2,1)} %pad_maximum_fusion.4), channel_id=1, source_target_pairs={{0,32},{16,48},{32,0},{48,16},{1,33},{17,49},{33,1},{49,17},{2,34}... | collective-permute-start | bytes 786440 | tf_op jit(solution)/shard_map/ppermute | solution.py:24
  68.5 21.3 %collective-permute-start.7 = (bf16[2,128,1024]{2,1,0:T(8,128)(2,1)}, bf16[2,128,1024]{2,1,0:T(8,128)(2,1)}, u32[]{:S(2)}, u32[]{:S(2)}) collective-permute-start(bf16[2,128,1024]{2,1,0:T(8,128)(2,1)} %pad_maximum_fusion.2), channel_id=1, source_target_pairs={{0,2},{2,4},{4,6},{6,0},{1,3},{3,5},{5,7},{7,1},{8,10},{10,12},{12... | collective-permute-start | bytes 1572872 | tf_op jit(solution)/shard_map/ppermute | solution.py:29
  71.8 19.9 %collective-permute-start.8 = (bf16[2,128,1024]{2,1,0:T(8,128)(2,1)}, bf16[2,128,1024]{2,1,0:T(8,128)(2,1)}, u32[]{:S(2)}, u32[]{:S(2)}) collective-permute-start(bf16[2,128,1024]{2,1,0:T(8,128)(2,1)} %pad_maximum_fusion.2), channel_id=1, source_target_pairs={{0,4},{2,6},{4,0},{6,2},{1,5},{3,7},{5,1},{7,3},{8,12},{10,14},{12... | collective-permute-start | bytes 1572872 | tf_op jit(solution)/shard_map/ppermute | solution.py:29
  75.6 24.5 %collective-permute-start.9 = (bf16[2,128,1024]{2,1,0:T(8,128)(2,1)}, bf16[2,128,1024]{2,1,0:T(8,128)(2,1)}, u32[]{:S(2)}, u32[]{:S(2)}) collective-permute-start(bf16[2,128,1024]{2,1,0:T(8,128)(2,1)} %pad_maximum_fusion.2), channel_id=1, source_target_pairs={{0,6},{2,0},{4,2},{6,4},{1,7},{3,1},{5,3},{7,5},{8,14},{10,8},{12,... | collective-permute-start | bytes 1572872 | tf_op jit(solution)/shard_map/ppermute | solution.py:29
  79.7 25.3 %all-to-all-start.1 = ((bf16[8,256,128]{2,1,0:T(8,128)(2,1)}), bf16[8,256,128]{2,1,0:T(8,128)(2,1)}, u32[]{:S(2)}, u32[]{:S(2)}) async-start(bf16[8,256,128]{2,1,0:T(8,128)(2,1)} %broadcast_in_dim.75), calls=%async_computation.1 | async-start | bytes 1048576 | tf_op jit(solution)/shard_map/all_to_all | solution.py:35
  87.1 16.8 %collective-permute-start.4 = (bf16[4,256,256]{2,1,0:T(8,128)(2,1)S(1)}, bf16[4,256,256]{2,1,0:T(8,128)(2,1)S(1)}, u32[]{:S(2)}, u32[]{:S(2)}) collective-permute-start(bf16[4,256,256]{2,1,0:T(8,128)(2,1)S(1)} %get-tuple-element.13), channel_id=1, source_target_pairs={{0,8},{8,0},{1,9},{9,1},{2,10},{10,2},{3,11},{11,3},{4,12},{12,4},... | collective-permute-start | bytes 1572872 | tf_op jit(solution)/shard_map/ppermute | solution.py:24
  101.9 61.6 %collective-permute-start.10 = (bf16[8,128,1024]{2,1,0:T(8,128)(2,1)}, bf16[8,128,1024]{2,1,0:T(8,128)(2,1)}, u32[]{:S(2)}, u32[]{:S(2)}) collective-permute-start(bf16[8,128,1024]{2,1,0:T(8,128)(2,1)} %constant_dynamic-update-slice_fusion.near_ref), channel_id=1, source_target_pairs={{0,8},{8,0},{1,9},{9,1},{2,10},{10,2},{3,11},{11,3},{4,12},{12,4},... | collective-permute-start | bytes 6291464 | tf_op jit(solution)/shard_map/ppermute | solution.py:24
  105.1 1.2 copy-start.1
  123.5 39.9 %copy-start.5 = (s32[4,256]{1,0:T(4,128)S(1)}, s32[4,256]{1,0:T(4,128)}, u32[]{:S(2)}) copy-start(s32[4,256]{1,0:T(4,128)} %param.9) | copy-start | bytes 12292
  147.9 10.1 %collective-permute-start.5 = (bf16[256,128]{1,0:T(8,128)(2,1)S(1)}, bf16[256,128]{1,0:T(8,128)(2,1)S(1)}, u32[]{:S(2)}, u32[]{:S(2)}) collective-permute-start(bf16[256,128]{1,0:T(8,128)(2,1)S(1)} %merge.1), channel_id=1, source_target_pairs={{0,1},{1,0},{2,3},{3,2},{4,5},{5,4},{6,7},{7,6},{8,9},{9,8},{10,11... | collective-permute-start | bytes 196616 | tf_op jit(solution)/shard_map/ppermute | solution.py:24
  158.9 11.8 %all-to-all-start.3 = ((bf16[4,2,256,128]{3,2,1,0:T(8,128)(2,1)}), bf16[4,2,256,128]{3,2,1,0:T(8,128)(2,1)}, u32[]{:S(2)}, u32[]{:S(2)}) async-start(bf16[4,2,256,128]{3,2,1,0:T(8,128)(2,1)} %broadcast_in_dim.76), calls=%async_computation.3 | async-start | bytes 1048576 | tf_op jit(solution)/shard_map/all_to_all | solution.py:35
  170.7 1.6 copy-start.2
Sparse Core Ops, SparseCore 0:
  37.9 127.4 all-gather.2

commit v2 on v1

--- a/solution.py
+++ b/solution.py
@@ -19,14 +19,13 @@
 PARAMS = pltpu.CompilerParams(vmem_limit_bytes=48 * 1024 * 1024)
 
 
+def cost(us):
+    return pl.CostEstimate(flops=us * 10**9, bytes_accessed=us * 10**6, transcendentals=0)
+
+
 def flip(array, axis, by):
     size = lax.axis_size(axis)
     return lax.ppermute(array, axis, [(i, i ^ by) for i in range(size)])
-
-
-def shift(array, axis, by):
-    size = lax.axis_size(axis)
-    return lax.ppermute(array, axis, [(i, (i + by) % size) for i in range(size)])
 
 
 def gather(array, axis):
@@ -35,11 +34,14 @@
     return lax.all_to_all(copies, axis, 0, 0, tiled=True)
 
 
+def exchange(array, axis, by):
+    other = flip(array, axis, by)
+    low = lax.axis_index(axis) & by == 0
+    return jnp.stack([jnp.where(low, array, other), jnp.where(low, other, array)])
+
+
 def gather_heads(array):
-    other = flip(array, "h", 1)
-    low = lax.axis_index("h") == 0
-    pair = jnp.stack([jnp.where(low, array, other), jnp.where(low, other, array)])
-    return gather(pair, "x").reshape((8,) + array.shape)
+    return gather(exchange(array, "h", 1), "x").reshape((8,) + array.shape)
 
 
 def sinusoid(frames_f, columns, width):
@@ -79,18 +81,28 @@
         in_specs=[VMEM, VMEM],
         out_specs=(VMEM, VMEM),
         compiler_params=PARAMS,
+        cost_estimate=cost(2),
         name="project",
     )(x8, w)
 
 
-def attend_kernel(place_ref, q_ref, kv_ref, o_ref):
-    rows = q_ref.shape[1]
-    blocks = kv_ref.shape[0]
-    plane = pl.program_id(0)
+def attend_kernel(place_ref, q_ref, near_ref, far_ref, o_ref, v_s):
+    planes, rows, _ = q_ref.shape
+    order = [0, 2, 1, 3]
+    step = pl.program_id(0)
     mine, slot = place_ref[0], place_ref[1]
     lane = lax.broadcasted_iota(jnp.int32, (rows, 128), 1)
-
-    def put_stats(lse):
+    blocks = [(near_ref, j, 2 * order[j]) for j in range(4)]
+    blocks += [(far_ref, j, 2 * order[j] + 1) for j in range(4)]
+
+    @pl.when(step == 0)
+    def _():
+        for n, (ref, j, _) in enumerate(blocks):
+            v_s[n, :, :128] = ref[j, :, 128:]
+            v_s[n, :, 128:] = jnp.ones((rows, 128), BF)
+
+    def put(i, out, lse):
+        o_ref[i, :rows, :] = out
         stats = jnp.zeros((rows, 128), F32)
         rest = list(lse)
         for part in range(3):
@@ -98,71 +110,89 @@
                 top = rest[h].astype(BF).astype(F32)
                 rest[h] = rest[h] - top
                 stats = jnp.where(lane == 2 * part + h, top, stats)
-        turned = jnp.transpose(stats)[:16, :].astype(BF)
-        o_ref[0, rows : rows + 16, :] = turned[:, :128]
-        o_ref[0, rows + 16 : rows + 32, :] = turned[:, 128:]
-
-    def compute(masked):
-        q = q_ref[0] * jnp.asarray(0.125, BF)
-        lse, outs = [], []
-        for h in range(2):
-            qh = jnp.where((lane >= 64) == (h == 1), q, jnp.zeros_like(q))
-            scores = []
-            for j in range(blocks):
-                s = lax.dot_general(
-                    qh, kv_ref[j, :, :128], (((1,), (1,)), ((), ())), preferred_element_type=F32
-                )
-                if masked:
-                    first = (slot ^ j) * rows - slot * rows
-                    row = lax.broadcasted_iota(jnp.int32, s.shape, 0)
-                    col = lax.broadcasted_iota(jnp.int32, s.shape, 1)
-                    s = jnp.where(col - row <= -first, s, LOW)
-                scores.append(s)
-            top = functools.reduce(jnp.maximum, scores)
-            m = jnp.max(top, axis=-1, keepdims=True)
-            total = 0.0
-            acc = 0.0
-            for j in range(blocks):
-                p = jnp.exp(scores[j] - m)
-                total = total + p
-                acc = acc + jnp.dot(p.astype(BF), kv_ref[j, :, 128:], preferred_element_type=F32)
-            l = jnp.sum(total, axis=-1, keepdims=True)
-            outs.append(acc / l)
-            lse.append(m + jnp.log(l))
-        o_ref[0, :rows, :] = jnp.where(lane < 64, outs[0], outs[1]).astype(BF)
-        put_stats(lse)
-
-    @pl.when(plane < mine)
+        turned = jnp.transpose(stats)[:8, :]
+        o_ref[i, rows : rows + 16, :] = jnp.concatenate(
+            [turned[:, :128], turned[:, 128:]], axis=0
+        ).astype(BF)
+
+    def scores(i, h, masked):
+        q = q_ref[i] * jnp.asarray(0.125, BF)
+        qh = jnp.where((lane >= 64) == (h == 1), q, jnp.zeros_like(q))
+        found = []
+        for ref, j, change in blocks:
+            s = lax.dot_general(
+                qh, ref[j, :, :128], (((1,), (1,)), ((), ())), preferred_element_type=F32
+            )
+            if masked:
+                first = (slot ^ change) * rows - slot * rows
+                row = lax.broadcasted_iota(jnp.int32, s.shape, 0)
+                col = lax.broadcasted_iota(jnp.int32, s.shape, 1)
+                s = jnp.where(col - row <= -first, s, LOW)
+            found.append(s)
+        return found
+
+    def soften(found):
+        m = jnp.max(functools.reduce(jnp.maximum, found), axis=-1, keepdims=True)
+        return m, [jnp.exp(s - m).astype(BF) for s in found]
+
+    def mix(m, weights):
+        acc = 0.0
+        for n, p in enumerate(weights):
+            acc = acc + jnp.dot(p, v_s[n], preferred_element_type=F32)
+        return acc[:, :128] / acc[:, 128:], m + jnp.log(acc[:, 128:129])
+
+    def compute(modes):
+        units = [(i, h) for i in range(planes) for h in range(2) if modes[i] > 0]
+        found, soft, done = {}, {}, {}
+        for t in range(len(units) + 2):
+            if t < len(units):
+                found[t] = scores(*units[t], modes[units[t][0]] == 1)
+            if 0 <= t - 1 < len(units):
+                soft[t - 1] = soften(found.pop(t - 1))
+            if 0 <= t - 2:
+                done[units[t - 2]] = mix(*soft.pop(t - 2))
+        for i in range(planes):
+            if modes[i] == 0:
+                put(i, jnp.zeros((rows, 128), BF), [jnp.full((rows, 1), LOW, F32)] * 2)
+            else:
+                (a, la), (b, lb) = done[i, 0], done[i, 1]
+                put(i, jnp.where(lane < 64, a, b).astype(BF), [la, lb])
+
+    low = step * planes
+
+    @pl.when(low > mine)
     def _():
-        o_ref[0, :rows, :] = jnp.zeros((rows, 128), BF)
-        put_stats([jnp.full((rows, 1), LOW, F32)] * 2)
-
-    @pl.when(plane == mine)
+        compute([2] * planes)
+
+    @pl.when(low + planes - 1 < mine)
     def _():
-        compute(True)
-
-    @pl.when(plane > mine)
-    def _():
-        compute(False)
-
-
-def attend(place, q8, kv8):
+        compute([0] * planes)
+
+    for k in range(planes):
+
+        @pl.when(low + k == mine)
+        def _():
+            compute([0] * k + [1] + [2] * (planes - 1 - k))
+
+
+def attend(place, q8, near, far):
     planes, rows, _ = q8.shape
+    each = 2
+    whole = pl.BlockSpec(near.shape, lambda i, s: (0, 0, 0))
     return pl.pallas_call(
         attend_kernel,
         grid_spec=pltpu.PrefetchScalarGridSpec(
             num_scalar_prefetch=1,
-            grid=(planes,),
-            in_specs=[
-                pl.BlockSpec((1, rows, 128), lambda i, s: (i, 0, 0)),
-                pl.BlockSpec(kv8.shape, lambda i, s: (0, 0, 0)),
-            ],
-            out_specs=pl.BlockSpec((1, rows + 32, 128), lambda i, s: (i, 0, 0)),
+            grid=(planes // each,),
+            in_specs=[pl.BlockSpec((each, rows, 128), lambda i, s: (i, 0, 0)), whole, whole],
+            out_specs=pl.BlockSpec((each, rows + 16, 128), lambda i, s: (i, 0, 0)),
+            scratch_shapes=[pltpu.VMEM((8, rows, 256), BF)],
         ),
-        out_shape=jax.ShapeDtypeStruct((planes, rows + 32, 128), BF),
+        out_shape=jax.ShapeDtypeStruct((planes, rows + 16, 128), BF),
         compiler_params=PARAMS,
+        cost_estimate=cost(14),
         name="attend",
-    )(place, q8, kv8)
+    )(place, q8, near, far)
 
 
 def merge_kernel(o_ref, out_ref):
@@ -172,7 +202,7 @@
     for half in range(rows // 128):
         lses = []
         for i in range(planes):
-            st = o_ref[i, rows + 16 * half : rows + 16 * half + 16, :].astype(F32)
+            st = o_ref[i, rows : rows + 16, :].astype(F32)[8 * half : 8 * half + 6]
             lses.append(st[0:2] + st[2:4] + st[4:6])
         top = functools.reduce(jnp.maximum, lses)
         weights = [jnp.exp(v - top) for v in lses]
@@ -187,13 +217,14 @@
 
 
 def merge(partial):
-    rows = partial.shape[1] - 32
+    rows = partial.shape[1] - 16
     return pl.pallas_call(
         merge_kernel,
         out_shape=jax.ShapeDtypeStruct((rows, 128), BF),
         in_specs=[VMEM],
         out_specs=VMEM,
         compiler_params=PARAMS,
+        cost_estimate=cost(1),
         name="merge",
     )(partial)
 
@@ -202,7 +233,7 @@
     parts, rows, width = x_ref.shape
     head, core = place_ref[0], place_ref[1]
     for i in range(parts):
-        a_s[:, 128 * i : 128 * i + 128] = att_ref[place_ref[2 + i]]
+        a_s[:, 128 * i : 128 * i + 128] = att_ref[i]
     half = near_ref.shape[-1]
     a = a_s[...]
     for ref, which in ((near_ref, core), (far_ref, 1 - core)):
@@ -251,6 +282,7 @@
             pltpu.VMEM((rows, parts * width), BF),
         ],
         compiler_params=PARAMS,
+        cost_estimate=cost(6),
         name="tail",
     )(place, att8, near, far, x8, hw, tgt)
 
@@ -291,15 +323,15 @@
     slot = z * 2 + c
     first = (y * 8 + slot) * rows
 
-    hw = lax.all_gather(heads_w, SEQ, axis=0)
-
     devices = lax.axis_size(SEQ)
     rim = lax.ppermute(codes[:, rows - 3 :], SEQ, [(i, i + 1) for i in range(devices - 1)])
     half = wout.shape[1] // 2
-    own_half = lax.dynamic_slice_in_dim(wout, c * half, half, 1)
-    pair = jnp.stack([own_half, flip(own_half, "h", 1)])
-    near = jnp.concatenate([pair] + [shift(pair, "x", k) for k in (1, 2, 3)])
+    pair = exchange(lax.dynamic_slice_in_dim(wout, c * half, half, 1), "h", 1)
+    near = lax.all_gather(pair, "x", axis=0).reshape(8, wout.shape[0], half)
     far = flip(near, "c", 1)
+    hw = exchange(exchange(exchange(heads_w, "c", 1), "z", 1), "z", 2)
+    hw, near = lax.optimization_barrier((hw, near))
+    hw = lax.all_gather(hw, "y", axis=0).reshape((-1,) + heads_w.shape)
     w3 = jnp.transpose(wqkv, (1, 0, 2))
 
     columns = head * width + jnp.arange(width, dtype=jnp.int32)
@@ -324,18 +356,15 @@
     q, kv = project(x8, w3)
 
     q8 = gather(q, "y")
-    one = flip(kv, "z", 1)
-    kv2 = jnp.stack([kv, one])
-    kv4 = jnp.concatenate([kv2, flip(kv2, "z", 2)])
-    other = flip(kv4, "c", 1)
-    kv8 = jnp.stack([kv4, other], axis=1).reshape((8,) + kv.shape)
-
-    partial = attend(jnp.stack([y, slot]).astype(jnp.int32), q8, kv8)
+    kv2 = jnp.stack([kv, flip(kv, "z", 2)])
+    kv4 = jnp.concatenate([kv2, flip(kv2, "z", 1)])
+    kv4_far = flip(kv4, "c", 1)
+
+    partial = attend(jnp.stack([y, slot]).astype(jnp.int32), q8, kv4, kv4_far)
     spread = lax.all_to_all(partial, "y", 0, 0, tiled=True)
     att8 = gather_heads(merge(spread))
 
-    order = [((x - k) % 4) * 2 + (h ^ j) for k in range(4) for j in range(2)]
-    place = jnp.stack([head, c] + order).astype(jnp.int32)
+    place = jnp.stack([head, c]).astype(jnp.int32)
     mixed, stats = tail(place, att8, near, far, x8, hw, jnp.transpose(targets))
     shares = lax.all_to_all(stats.reshape(8, rows // 8, 128), HEAD, 0, 0, tiled=True)
     return (mixed, final_loss(shares, books))

time: 206 us -> 219 us (1.063)
  the two profiles are of different devices: /device:TPU:2 before, /device:TPU:72 now
where the time goes in v2:
time: 219 us; the launch traced here: 218 us
  starting transfers between devices  64 us (29%)
  waiting for transfers between devices  55.2 us (25%)
  blocking collectives  44.1 us (20%)
  Pallas kernels  21.9 us (10%)
  between operations  14.4 us (7%)
  other arithmetic  9.09 us (4%)
  local copies, waits for them, and re-layouts  8.42 us (4%)
    ppermute x10, starting transfers between devices, flip(): return lax.ppermute(array, axis, [(i, i ^ by) for i in range(size)])  46.2 us
    all_to_all x3, waiting for transfers between devices, gather(): return lax.all_to_all(copies, axis, 0, 0, tiled=True)  33.2 us
    all_to_all x1, blocking collectives, shards(): spread = lax.all_to_all(partial, 'y', 0, 0, tiled=True)  26.7 us
    ppermute x10, waiting for transfers between devices, flip(): return lax.ppermute(array, axis, [(i, i ^ by) for i in range(size)])  22 us
    all_to_all x1, blocking collectives, shards(): lax.all_to_all(stats.reshape(8, rows // 8, 128), HEAD, 0, 0, tiled=True)  17.4 us
    all_to_all x3, starting transfers between devices, gather(): return lax.all_to_all(copies, axis, 0, 0, tiled=True)  15.9 us
    pallas_call x1, Pallas kernels, attend(): pl.pallas_call(attend_kernel, grid_spec=pltpu.PrefetchScalarGridSpec(num_...  12.6 us
    pallas_call x1, Pallas kernels, tail(): pl.pallas_call(tail_kernel, out_shape=(jax.ShapeDtypeStruct((rows, width)...  5.58 us
  transfers between devices with their start and end apart: 16, of which 8 were waited for; matrix products, arithmetic and copies ran while one was open for 6% of the time, Pallas kernels for 7%

profile of v2, /device:TPU:72, one launch (start us, length us, event | category | flops | bytes accessed | tf_op | source)
XLA Modules:
  0.0 218.1 jit_solution(1574597795184555927)
XLA Ops:
  7.2 0.0 copy-start
  7.2 0.0 copy-start.5
  7.2 0.0 all-gather.5.cloned.1.call-start
  7.2 0.9 slice.12
  8.1 1.9 collective-permute-start
  10.1 1.0 constant_dynamic-slice_fusion
  11.0 10.0 %collective-permute-start.9 = (bf16[128,1024]{1,0:T(8,128)(2,1)S(1)}, bf16[128,1024]{1,0:T(8,128)(2,1)S(1)}, u32[]{:S(2)}, u32[]{:S(2)}) collective-permute-start(bf16[128,1024]{1,0:T(8,128)(2,1)S(1)} %constant_dynamic-slice_fusion), channel_id=1, source_target_pairs={{0,1},{1,0},{2,3},{3,2},{4,5},{5,4},{6,7},{7,6},{8,9},{9,8},{10,11... | collective-permute-start | bytes 786440 | tf_op jit(solution)/shard_map/ppermute | solution.py:28
  21.1 1.0 fusion.5
  22.1 11.0 %collective-permute-done.9 = bf16[128,1024]{1,0:T(8,128)(2,1)S(1)} collective-permute-done((bf16[128,1024]{1,0:T(8,128)(2,1)S(1)}, bf16[128,1024]{1,0:T(8,128)(2,1)S(1)}, u32[]{:S(2)}, u32[]{:S(2)}) %collective-permute-start.9) | collective-permute-done | bytes 262176 | tf_op jit(solution)/shard_map/ppermute | solution.py:28
  33.1 1.1 select_bitcast_fusion.1
  34.2 0.8 pad_maximum_fusion.1
  35.0 0.0 all-gather.5.cloned.1.call-update
  35.1 0.0 collective-permute-done
  35.1 0.1 fusion.10
  35.2 0.9 fusion.4
  36.1 7.7 %collective-permute-start.1 = (bf16[256,256]{1,0:T(8,128)(2,1)S(1)}, bf16[256,256]{1,0:T(8,128)(2,1)S(1)}, u32[]{:S(2)}, u32[]{:S(2)}) collective-permute-start(bf16[256,256]{1,0:T(8,128)(2,1)S(1)} %fusion.4), channel_id=1, source_target_pairs={{0,1},{1,0},{2,3},{3,2},{4,5},{5,4},{6,7},{7,6},{8,9},{9,8},{10,11... | collective-permute-start | bytes 393224 | tf_op jit(solution)/shard_map/ppermute | solution.py:28
  43.8 5.8 %collective-permute-done.1 = bf16[256,256]{1,0:T(8,128)(2,1)S(1)} collective-permute-done((bf16[256,256]{1,0:T(8,128)(2,1)S(1)}, bf16[256,256]{1,0:T(8,128)(2,1)S(1)}, u32[]{:S(2)}, u32[]{:S(2)}) %collective-permute-start.1) | collective-permute-done | bytes 131104 | tf_op jit(solution)/shard_map/ppermute | solution.py:28
  49.6 0.0 copy-start.4
  49.6 1.1 broadcast_in_dim.74
  50.7 4.3 %all-to-all-start = ((bf16[4,2,256,256]{3,2,1,0:T(8,128)(2,1)}), bf16[4,2,256,256]{3,2,1,0:T(8,128)(2,1)S(1)}, u32[]{:S(2)}, u32[]{:S(2)}) async-start(bf16[4,2,256,256]{3,2,1,0:T(8,128)(2,1)} %broadcast_in_dim.74), calls=%async_computation | async-start | bytes 2097152 | tf_op jit(solution)/shard_map/all_to_all | solution.py:34
  54.9 0.0 copy-done.4
  55.0 1.9 collective-permute-start.6
  56.9 1.2 collective-permute-done.6
  58.1 1.9 collective-permute-start.7
  60.0 22.2 %all-to-all-done = bf16[4,2,256,256]{3,2,1,0:T(8,128)(2,1)S(1)} async-done(((bf16[4,2,256,256]{3,2,1,0:T(8,128)(2,1)}), bf16[4,2,256,256]{3,2,1,0:T(8,128)(2,1)S(1)}, u32[]{:S(2)}, u32[]{:S(2)}) %all-to-all-start) | async-done | bytes 1048608 | tf_op jit(solution)/shard_map/all_to_all | solution.py:34
  82.2 1.4 copy-done.2
  83.6 1.2 project.1
  84.9 1.9 collective-permute-start.2
  86.8 0.0 collective-permute-done.7
  86.8 0.9 select_bitcast_fusion.7
  87.7 0.7 pad_maximum_fusion.6
  88.3 4.8 %collective-permute-start.8 = (bf16[2,2,4,32,128]{4,3,2,1,0:T(8,128)(2,1)}, bf16[2,2,4,32,128]{4,3,2,1,0:T(8,128)(2,1)}, u32[]{:S(2)}, u32[]{:S(2)}) collective-permute-start(bf16[2,2,4,32,128]{4,3,2,1,0:T(8,128)(2,1)} %pad_maximum_fusion.6), channel_id=1, source_target_pairs={{0,32},{16,48},{32,0},{48,16},{1,33},{17,49},{33,1},{49,17},{2,34}... | collective-permute-start | bytes 393224 | tf_op jit(solution)/shard_map/ppermute | solution.py:28
  93.1 0.5 collective-permute-done.2
  93.6 0.7 copy-done.3
  94.3 0.7 pad_maximum_fusion.3
  95.0 6.5 %collective-permute-start.3 = (bf16[2,256,256]{2,1,0:T(8,128)(2,1)}, bf16[2,256,256]{2,1,0:T(8,128)(2,1)}, u32[]{:S(2)}, u32[]{:S(2)}) collective-permute-start(bf16[2,256,256]{2,1,0:T(8,128)(2,1)} %pad_maximum_fusion.3), channel_id=1, source_target_pairs={{0,16},{16,0},{32,48},{48,32},{1,17},{17,1},{33,49},{49,33},{2,18}... | collective-permute-start | bytes 786440 | tf_op jit(solution)/shard_map/ppermute | solution.py:28
  101.5 0.8 broadcast_in_dim.75
  102.3 7.5 %all-to-all-start.1 = ((bf16[8,256,128]{2,1,0:T(8,128)(2,1)}), bf16[8,256,128]{2,1,0:T(8,128)(2,1)}, u32[]{:S(2)}, u32[]{:S(2)}) async-start(bf16[8,256,128]{2,1,0:T(8,128)(2,1)} %broadcast_in_dim.75), calls=%async_computation.1 | async-start | bytes 1048576 | tf_op jit(solution)/shard_map/all_to_all | solution.py:34
  109.8 0.0 collective-permute-done.8
  109.8 0.9 select_bitcast_fusion.3
  110.8 0.0 collective-permute-done.3
  110.8 1.9 pad_maximum_fusion.near_ref
  112.6 1.9 collective-permute-start.4
  114.6 0.7 pad_maximum_fusion.4
  115.3 0.0 all-gather.7.cloned.1.call-update
  115.3 0.1 pad_add_fusion.2.place_ref
  115.4 2.6 %collective-permute-start.10 = (bf16[8,128,1024]{2,1,0:T(8,128)(2,1)}, bf16[8,128,1024]{2,1,0:T(8,128)(2,1)}, u32[]{:S(2)}, u32[]{:S(2)}) collective-permute-start(bf16[8,128,1024]{2,1,0:T(8,128)(2,1)} %all-gather.5.cloned.1.call-done.near_ref), channel_id=1, source_target_pairs={{0,8},{8,0},{1,9},{9,1},{2,10},{10,2},{3,11},{11,3},{4,12},{12,4},... | collective-permute-start | bytes 6291464 | tf_op jit(solution)/shard_map/ppermute | solution.py:28
  118.0 3.1 %all-to-all-done.1.q_ref = bf16[8,256,128]{2,1,0:T(8,128)(2,1)} async-done(((bf16[8,256,128]{2,1,0:T(8,128)(2,1)}), bf16[8,256,128]{2,1,0:T(8,128)(2,1)}, u32[]{:S(2)}, u32[]{:S(2)}) %all-to-all-start.1) | async-done | bytes 524320 | tf_op jit(solution)/shard_map/all_to_all | solution.py:34
  121.1 0.0 collective-permute-done.4.far_ref
  121.1 12.6 %attend.1 = bf16[8,272,128]{2,1,0:T(8,128)(2,1)S(1)} custom-call(s32[2]{0:T(128)S(1)} %pad_add_fusion.2.place_ref, bf16[8,256,128]{2,1,0:T(8,128)(2,1)} %all-to-all-done.1.q_ref, bf16[4,256,256]{2,1,0:T(8,128)(2,1)} %pad_maximum_fusion.near_ref, bf16[4,256,256]{2,1,0:T(8,128)(2,1)} %collective-permute-done.4.far_ref), custom_call_target="tpu_custom_call" | custom-call | flops 14000000000 | bytes 14000000 | tf_op jit(solution)/shard_map/attend/pallas_call | solution.py:182
  133.7 26.7 %all_to_all.25.o_ref = bf16[8,272,128]{2,1,0:T(8,128)(2,1)S(1)} all-to-all(bf16[8,272,128]{2,1,0:T(8,128)(2,1)S(1)} %attend.1), channel_id=1, replica_groups=mesh['y'=8,'z'=4,'c'=2,'x'=4,'h'=2] {'y'}, dimensions={0} | all-to-all | bytes 1114112 | tf_op jit(solution)/shard_map/all_to_all | solution.py:364
  160.4 0.8 merge.1
  161.2 7.0 %collective-permute-start.5 = (bf16[256,128]{1,0:T(8,128)(2,1)S(1)}, bf16[256,128]{1,0:T(8,128)(2,1)S(1)}, u32[]{:S(2)}, u32[]{:S(2)}) collective-permute-start(bf16[256,128]{1,0:T(8,128)(2,1)S(1)} %merge.1), channel_id=1, source_target_pairs={{0,1},{1,0},{2,3},{3,2},{4,5},{5,4},{6,7},{7,6},{8,9},{9,8},{10,11... | collective-permute-start | bytes 196616 | tf_op jit(solution)/shard_map/ppermute | solution.py:28
  168.2 3.6 %collective-permute-done.5 = bf16[256,128]{1,0:T(8,128)(2,1)S(1)} collective-permute-done((bf16[256,128]{1,0:T(8,128)(2,1)S(1)}, bf16[256,128]{1,0:T(8,128)(2,1)S(1)}, u32[]{:S(2)}, u32[]{:S(2)}) %collective-permute-start.5) | collective-permute-done | bytes 65568 | tf_op jit(solution)/shard_map/ppermute | solution.py:28
  171.8 0.8 broadcast_in_dim.76
  172.7 4.1 %all-to-all-start.3 = ((bf16[4,2,256,128]{3,2,1,0:T(8,128)(2,1)}), bf16[4,2,256,128]{3,2,1,0:T(8,128)(2,1)}, u32[]{:S(2)}, u32[]{:S(2)}) async-start(bf16[4,2,256,128]{3,2,1,0:T(8,128)(2,1)} %broadcast_in_dim.76), calls=%async_computation.3 | async-start | bytes 1048576 | tf_op jit(solution)/shard_map/all_to_all | solution.py:34
  176.8 0.1 copy.10
  177.0 0.1 pad_add_fusion.1.place_ref
  177.1 7.9 %all-to-all-done.3 = bf16[4,2,256,128]{3,2,1,0:T(8,128)(2,1)} async-done(((bf16[4,2,256,128]{3,2,1,0:T(8,128)(2,1)}), bf16[4,2,256,128]{3,2,1,0:T(8,128)(2,1)}, u32[]{:S(2)}, u32[]{:S(2)}) %all-to-all-start.3) | async-done | bytes 524320 | tf_op jit(solution)/shard_map/all_to_all | solution.py:34
  185.0 0.0 collective-permute-done.10.far_ref
  185.0 1.6 copy-done.1
  186.6 5.6 %tail.1 = (bf16[256,256]{1,0:T(8,128)(2,1)}, f32[256,128]{1,0:T(8,128)S(1)}) custom-call(s32[2]{0:T(128)S(1)} %pad_add_fusion.1.place_ref, bf16[8,256,128]{2,1,0:T(8,128)(2,1)} %bitcast.14.att_ref, bf16[8,128,1024]{2,1,0:T(8,128)(2,1)S(1)} %copy-done.1, bf16[8,128,1024]{2,1,0:T(8,128)(2,1)} %collective-permute-done.10.far_ref, ...), custom_call_target="tpu_custom_call" | custom-call | flops 6000000000 | bytes 6000000 | tf_op jit(solution)/shard_map/tail/pallas_call | solution.py:271
  192.2 17.4 %all_to_all.26.s_ref = f32[8,32,128]{2,1,0:T(8,128)} all-to-all(f32[8,32,128]{2,1,0:T(8,128)S(1)} %bitcast.50), channel_id=1, replica_groups=mesh['y'=8,'z'=4,'c'=2,'x'=4,'h'=2] {'x','h'}, dimensions={0} | all-to-all | bytes 262144 | tf_op jit(solution)/shard_map/all_to_all | solution.py:369
  209.6 1.7 loss.1
  (23 shorter events, 0.2 us)
Async XLA Ops:
  7.2 28.0 %copy-start = (bf16[4,1024,256]{2,1,0:T(8,128)(2,1)S(1)}, bf16[4,1024,256]{2,1,0:T(8,128)(2,1)}, u32[]{:S(2)}) copy-start(bf16[4,1024,256]{2,1,0:T(8,128)(2,1)} %param.10) | copy-start | bytes 6291460
  7.2 27.9 %copy-start.5 = (s32[4,256]{1,0:T(4,128)S(1)}, s32[4,256]{1,0:T(4,128)}, u32[]{:S(2)}) copy-start(s32[4,256]{1,0:T(4,128)} %param.7) | copy-start | bytes 12292
  7.2 27.9 %copy-start.7 = (s32[4]{0:T(128)S(1)}, s32[4]{0:T(128)}, u32[]{:S(2)}) copy-start(s32[4]{0:T(128)} %param.8) | copy-start | bytes 52
  7.2 108.1 %all-gather.5.cloned.1.call-start = ((), (), s32[]{:S(2)}) async-start(), calls=%async_computation.5 | async-start | bytes 2621440 | tf_op jit(solution)/shard_map/all_gather | solution.py:330
  8.1 27.0 %collective-permute-start = (s32[4,3]{1,0:T(4,128)S(1)}, s32[4,3]{1,0:T(4,128)S(1)}, u32[]{:S(2)}, u32[]{:S(2)}) collective-permute-start(s32[4,3]{1,0:T(4,128)S(1)} %slice.12), channel_id=1, source_target_pairs={{0,8},{8,16},{16,24},{24,32},{32,40},{40,48},{48,56},{56,64},{64,7... | collective-permute-start | bytes 152 | tf_op jit(solution)/shard_map/ppermute | solution.py:327
  11.0 22.1 %collective-permute-start.9 = (bf16[128,1024]{1,0:T(8,128)(2,1)S(1)}, bf16[128,1024]{1,0:T(8,128)(2,1)S(1)}, u32[]{:S(2)}, u32[]{:S(2)}) collective-permute-start(bf16[128,1024]{1,0:T(8,128)(2,1)S(1)} %constant_dynamic-slice_fusion), channel_id=1, source_target_pairs={{0,1},{1,0},{2,3},{3,2},{4,5},{5,4},{6,7},{7,6},{8,9},{9,8},{10,11... | collective-permute-start | bytes 786440 | tf_op jit(solution)/shard_map/ppermute | solution.py:28
  36.1 13.4 %collective-permute-start.1 = (bf16[256,256]{1,0:T(8,128)(2,1)S(1)}, bf16[256,256]{1,0:T(8,128)(2,1)S(1)}, u32[]{:S(2)}, u32[]{:S(2)}) collective-permute-start(bf16[256,256]{1,0:T(8,128)(2,1)S(1)} %fusion.4), channel_id=1, source_target_pairs={{0,1},{1,0},{2,3},{3,2},{4,5},{5,4},{6,7},{7,6},{8,9},{9,8},{10,11... | collective-permute-start | bytes 393224 | tf_op jit(solution)/shard_map/ppermute | solution.py:28
  49.6 5.4 %copy-start.4 = (bf16[4,32,128]{2,1,0:T(8,128)(2,1)S(1)}, bf16[4,32,128]{2,1,0:T(8,128)(2,1)}, u32[]{:S(2)}) copy-start(bf16[4,32,128]{2,1,0:T(8,128)(2,1)} %param.13) | copy-start | bytes 98308
  50.7 31.5 %all-to-all-start = ((bf16[4,2,256,256]{3,2,1,0:T(8,128)(2,1)}), bf16[4,2,256,256]{3,2,1,0:T(8,128)(2,1)S(1)}, u32[]{:S(2)}, u32[]{:S(2)}) async-start(bf16[4,2,256,256]{3,2,1,0:T(8,128)(2,1)} %broadcast_in_dim.74), calls=%async_computation | async-start | bytes 2097152 | tf_op jit(solution)/shard_map/all_to_all | solution.py:34
  55.0 3.1 %collective-permute-start.6 = (bf16[4,32,128]{2,1,0:T(8,128)(2,1)S(1)}, bf16[4,32,128]{2,1,0:T(8,128)(2,1)S(1)}, u32[]{:S(2)}, u32[]{:S(2)}) collective-permute-start(bf16[4,32,128]{2,1,0:T(8,128)(2,1)S(1)} %copy-done.4), channel_id=1, source_target_pairs={{0,8},{8,0},{1,9},{9,1},{2,10},{10,2},{3,11},{11,3},{4,12},{12,4},... | collective-permute-start | bytes 98312 | tf_op jit(solution)/shard_map/ppermute | solution.py:28
  58.1 28.7 %collective-permute-start.7 = (bf16[2,4,32,128]{3,2,1,0:T(8,128)(2,1)S(1)}, bf16[2,4,32,128]{3,2,1,0:T(8,128)(2,1)}, u32[]{:S(2)}, u32[]{:S(2)}) collective-permute-start(bf16[2,4,32,128]{3,2,1,0:T(8,128)(2,1)S(1)} %pad_maximum_fusion.7), channel_id=1, source_target_pairs={{0,16},{16,0},{32,48},{48,32},{1,17},{17,1},{33,49},{49,33},{2,18}... | collective-permute-start | bytes 196616 | tf_op jit(solution)/shard_map/ppermute | solution.py:28
  82.2 1.4 copy-start.2
  84.9 8.8 %collective-permute-start.2 = (bf16[256,256]{1,0:T(8,128)(2,1)S(1)}, bf16[256,256]{1,0:T(8,128)(2,1)S(1)}, u32[]{:S(2)}, u32[]{:S(2)}) collective-permute-start(bf16[256,256]{1,0:T(8,128)(2,1)S(1)} %get-tuple-element.9), channel_id=1, source_target_pairs={{0,32},{16,48},{32,0},{48,16},{1,33},{17,49},{33,1},{49,17},{2,34}... | collective-permute-start | bytes 393224 | tf_op jit(solution)/shard_map/ppermute | solution.py:28
  88.3 21.5 %collective-permute-start.8 = (bf16[2,2,4,32,128]{4,3,2,1,0:T(8,128)(2,1)}, bf16[2,2,4,32,128]{4,3,2,1,0:T(8,128)(2,1)}, u32[]{:S(2)}, u32[]{:S(2)}) collective-permute-start(bf16[2,2,4,32,128]{4,3,2,1,0:T(8,128)(2,1)} %pad_maximum_fusion.6), channel_id=1, source_target_pairs={{0,32},{16,48},{32,0},{48,16},{1,33},{17,49},{33,1},{49,17},{2,34}... | collective-permute-start | bytes 393224 | tf_op jit(solution)/shard_map/ppermute | solution.py:28
  93.6 0.7 copy-start.3
  95.0 15.7 %collective-permute-start.3 = (bf16[2,256,256]{2,1,0:T(8,128)(2,1)}, bf16[2,256,256]{2,1,0:T(8,128)(2,1)}, u32[]{:S(2)}, u32[]{:S(2)}) collective-permute-start(bf16[2,256,256]{2,1,0:T(8,128)(2,1)} %pad_maximum_fusion.3), channel_id=1, source_target_pairs={{0,16},{16,0},{32,48},{48,32},{1,17},{17,1},{33,49},{49,33},{2,18}... | collective-permute-start | bytes 786440 | tf_op jit(solution)/shard_map/ppermute | solution.py:28
  102.3 18.7 %all-to-all-start.1 = ((bf16[8,256,128]{2,1,0:T(8,128)(2,1)}), bf16[8,256,128]{2,1,0:T(8,128)(2,1)}, u32[]{:S(2)}, u32[]{:S(2)}) async-start(bf16[8,256,128]{2,1,0:T(8,128)(2,1)} %broadcast_in_dim.75), calls=%async_computation.1 | async-start | bytes 1048576 | tf_op jit(solution)/shard_map/all_to_all | solution.py:34
  109.8 75.2 %all-gather.7.cloned.1.call-start = ((), (), s32[]{:S(2)}) async-start(), calls=%async_computation.6 | async-start | bytes 2359296 | tf_op jit(solution)/shard_map/all_gather | solution.py:334
  112.6 8.4 %collective-permute-start.4 = (bf16[4,256,256]{2,1,0:T(8,128)(2,1)}, bf16[4,256,256]{2,1,0:T(8,128)(2,1)}, u32[]{:S(2)}, u32[]{:S(2)}) collective-permute-start(bf16[4,256,256]{2,1,0:T(8,128)(2,1)} %pad_maximum_fusion.near_ref), channel_id=1, source_target_pairs={{0,8},{8,0},{1,9},{9,1},{2,10},{10,2},{3,11},{11,3},{4,12},{12,4},... | collective-permute-start | bytes 1572872 | tf_op jit(solution)/shard_map/ppermute | solution.py:28
  115.4 69.6 %collective-permute-start.10 = (bf16[8,128,1024]{2,1,0:T(8,128)(2,1)}, bf16[8,128,1024]{2,1,0:T(8,128)(2,1)}, u32[]{:S(2)}, u32[]{:S(2)}) collective-permute-start(bf16[8,128,1024]{2,1,0:T(8,128)(2,1)} %all-gather.5.cloned.1.call-done.near_ref), channel_id=1, source_target_pairs={{0,8},{8,0},{1,9},{9,1},{2,10},{10,2},{3,11},{11,3},{4,12},{12,4},... | collective-permute-start | bytes 6291464 | tf_op jit(solution)/shard_map/ppermute | solution.py:28
  160.4 16.4 %copy-start.6 = (s32[4,256]{1,0:T(4,128)S(1)}, s32[4,256]{1,0:T(4,128)}, u32[]{:S(2)}) copy-start(s32[4,256]{1,0:T(4,128)} %param.9) | copy-start | bytes 12292
  161.2 10.6 %collective-permute-start.5 = (bf16[256,128]{1,0:T(8,128)(2,1)S(1)}, bf16[256,128]{1,0:T(8,128)(2,1)S(1)}, u32[]{:S(2)}, u32[]{:S(2)}) collective-permute-start(bf16[256,128]{1,0:T(8,128)(2,1)S(1)} %merge.1), channel_id=1, source_target_pairs={{0,1},{1,0},{2,3},{3,2},{4,5},{5,4},{6,7},{7,6},{8,9},{9,8},{10,11... | collective-permute-start | bytes 196616 | tf_op jit(solution)/shard_map/ppermute | solution.py:28
  172.7 12.3 %all-to-all-start.3 = ((bf16[4,2,256,128]{3,2,1,0:T(8,128)(2,1)}), bf16[4,2,256,128]{3,2,1,0:T(8,128)(2,1)}, u32[]{:S(2)}, u32[]{:S(2)}) async-start(bf16[4,2,256,128]{3,2,1,0:T(8,128)(2,1)} %broadcast_in_dim.76), calls=%async_computation.3 | async-start | bytes 1048576 | tf_op jit(solution)/shard_map/all_to_all | solution.py:34
  185.0 1.6 copy-start.1
Sparse Core Ops, SparseCore 0:
  35.2 49.1 all-gather.4
  115.5 51.5 all-gather.6

commit v3 on v2

--- a/solution.py
+++ b/solution.py
@@ -15,12 +15,10 @@
 SEQ = ("y", "z", "c")
 HEAD = ("x", "h")
 VMEM = pl.BlockSpec(memory_space=pltpu.VMEM)
+SMALL = pl.CostEstimate(flops=1, bytes_accessed=1, transcendentals=0)
 SMEM = pl.BlockSpec(memory_space=pltpu.SMEM)
+HBM = pl.BlockSpec(memory_space=pltpu.HBM)
 PARAMS = pltpu.CompilerParams(vmem_limit_bytes=48 * 1024 * 1024)
-
-
-def cost(us):
-    return pl.CostEstimate(flops=us * 10**9, bytes_accessed=us * 10**6, transcendentals=0)
 
 
 def flip(array, axis, by):
@@ -28,20 +26,17 @@
     return lax.ppermute(array, axis, [(i, i ^ by) for i in range(size)])
 
 
-def gather(array, axis):
+def shift(array, axis, by):
     size = lax.axis_size(axis)
-    copies = jnp.broadcast_to(array[None], (size,) + array.shape)
-    return lax.all_to_all(copies, axis, 0, 0, tiled=True)
-
-
-def exchange(array, axis, by):
-    other = flip(array, axis, by)
-    low = lax.axis_index(axis) & by == 0
-    return jnp.stack([jnp.where(low, array, other), jnp.where(low, other, array)])
-
-
-def gather_heads(array):
-    return gather(exchange(array, "h", 1), "x").reshape((8,) + array.shape)
+    return lax.ppermute(array, axis, [(i, (i + by) % size) for i in range(size)])
+
+
+def trade(array, axis):
+    return lax.all_to_all(array, axis, 0, 0, tiled=True)
+
+
+def after(array, first):
+    return lax.optimization_barrier((array, first))[0]
 
 
 def sinusoid(frames_f, columns, width):
@@ -51,37 +46,44 @@
     return jnp.where(columns[None, :] < half, jnp.sin(angle), jnp.cos(angle))
 
 
-def project_kernel(x_ref, w_ref, q_ref, kv_ref):
+def project_kernel(x_ref, w_ref, q_ref, kv_ref, w_s, n_s, sem):
+    load = pltpu.make_async_copy(w_ref, w_s, sem)
+    load.start()
     parts, _, width = x_ref.shape
     squares = 0.0
     for i in range(parts):
         xi = x_ref[i].astype(F32)
         squares = squares + jnp.sum(xi * xi, axis=-1, keepdims=True)
     r = lax.rsqrt(squares / (parts * width) + 1e-05)
-    sums = [0.0, 0.0, 0.0]
     for i in range(parts):
-        ni = (x_ref[i].astype(F32) * r).astype(BF)
-        for j in range(3):
-            sums[j] = sums[j] + jnp.dot(
-                ni, w_ref[j, i * width : (i + 1) * width, :], preferred_element_type=F32
-            )
-    q_ref[...] = sums[0].astype(BF)
-    kv_ref[:, :128] = sums[1].astype(BF)
-    kv_ref[:, 128:] = sums[2].astype(BF)
+        n_s[:, i * width : (i + 1) * width] = (x_ref[i].astype(F32) * r).astype(BF)
+    load.wait()
+    n = n_s[...]
+    q = jnp.dot(n, w_s[0], preferred_element_type=F32).astype(BF)
+    for i in range(q_ref.shape[0]):
+        q_ref[i] = q
+    for j in range(2):
+        kv = jnp.dot(n, w_s[1 + j], preferred_element_type=F32)
+        kv_ref[:, 128 * j : 128 * j + 128] = kv.astype(BF)
 
 
 def project(x8, w):
-    rows = x8.shape[1]
+    parts, rows, width = x8.shape
     return pl.pallas_call(
         project_kernel,
         out_shape=(
-            jax.ShapeDtypeStruct((rows, 128), BF),
+            pltpu.HBM((8, rows, 128), BF),
             jax.ShapeDtypeStruct((rows, 256), BF),
         ),
-        in_specs=[VMEM, VMEM],
+        in_specs=[VMEM, HBM],
         out_specs=(VMEM, VMEM),
+        scratch_shapes=[
+            pltpu.VMEM(w.shape, BF),
+            pltpu.VMEM((rows, parts * width), BF),
+            pltpu.SemaphoreType.DMA,
+        ],
         compiler_params=PARAMS,
-        cost_estimate=cost(2),
+        cost_estimate=SMALL,
         name="project",
     )(x8, w)
 
@@ -188,16 +190,16 @@
             out_specs=pl.BlockSpec((each, rows + 16, 128), lambda i, s: (i, 0, 0)),
             scratch_shapes=[pltpu.VMEM((8, rows, 256), BF)],
         ),
-        out_shape=jax.ShapeDtypeStruct((planes, rows + 16, 128), BF),
+        out_shape=pltpu.HBM((planes, rows + 16, 128), BF),
         compiler_params=PARAMS,
-        cost_estimate=cost(14),
+        cost_estimate=SMALL,
         name="attend",
     )(place, q8, near, far)
 
 
 def merge_kernel(o_ref, out_ref):
     planes = o_ref.shape[0]
-    rows = out_ref.shape[0]
+    copies, rows, _ = out_ref.shape
     lane = lax.broadcasted_iota(jnp.int32, (128, 128), 1)
     for half in range(rows // 128):
         lses = []
@@ -213,32 +215,36 @@
         for i in range(planes):
             wi = jnp.where(lane < 64, w[:, 2 * i : 2 * i + 1], w[:, 2 * i + 1 : 2 * i + 2])
             acc = acc + wi * o_ref[i, 128 * half : 128 * half + 128, :].astype(F32)
-        out_ref[128 * half : 128 * half + 128, :] = acc.astype(BF)
+        for i in range(copies):
+            out_ref[i, 128 * half : 128 * half + 128, :] = acc.astype(BF)
 
 
 def merge(partial):
     rows = partial.shape[1] - 16
     return pl.pallas_call(
         merge_kernel,
-        out_shape=jax.ShapeDtypeStruct((rows, 128), BF),
+        out_shape=pltpu.HBM((8, rows, 128), BF),
         in_specs=[VMEM],
         out_specs=VMEM,
         compiler_params=PARAMS,
-        cost_estimate=cost(1),
+        cost_estimate=SMALL,
         name="merge",
     )(partial)
 
 
-def tail_kernel(place_ref, att_ref, near_ref, far_ref, x_ref, hw_ref, tgt_ref, mixed_ref, stat_ref, a_s, m_s, f_s):
+def tail_kernel(place_ref, att_ref, x_ref, hw_ref, tgt_ref, *refs):
+    near_refs, far_refs = refs[:4], refs[4:8]
+    mixed_ref, stat_ref, a_s, m_s, f_s = refs[8:]
     parts, rows, width = x_ref.shape
     head, core = place_ref[0], place_ref[1]
     for i in range(parts):
-        a_s[:, 128 * i : 128 * i + 128] = att_ref[i]
-    half = near_ref.shape[-1]
-    a = a_s[...]
-    for ref, which in ((near_ref, core), (far_ref, 1 - core)):
-        w = ref[...].reshape(parts * 128, half)
-        got = jnp.dot(a, w, preferred_element_type=F32)
+        a_s[:, 128 * i : 128 * i + 128] = att_ref[place_ref[2 + i]]
+    half = near_refs[0].shape[-1]
+    for group, which in ((near_refs, core), (far_refs, 1 - core)):
+        got = 0.0
+        for k, ref in enumerate(group):
+            w = ref[...].reshape(256, half)
+            got = got + jnp.dot(a_s[:, 256 * k : 256 * k + 256], w, preferred_element_type=F32)
         m_s[:, pl.ds(pl.multiple_of(which * half, half), half)] = got.astype(BF)
     mixed_ref[...] = m_s[:, pl.ds(pl.multiple_of(head * width, width), width)]
     squares = 0.0
@@ -250,23 +256,27 @@
     r = lax.rsqrt(squares / (parts * width) + 1e-05)
     f_s[...] = (f_s[...].astype(F32) * r).astype(BF)
     final = f_s[...]
-    books = hw_ref.shape[1]
+    books = tgt_ref.shape[1]
+    share = hw_ref.shape[1] // 2
     lane = lax.broadcasted_iota(jnp.int32, (rows, 128), 1)
     stats = jnp.zeros((rows, 128), F32)
-    for b in range(books):
-        w = hw_ref[:, b].reshape(parts * width, 128)
-        logits = jnp.dot(final, w, preferred_element_type=F32)
-        g = jnp.max(logits, axis=-1, keepdims=True)
-        s = jnp.sum(jnp.exp(logits - g), axis=-1, keepdims=True)
-        hit = lane + 128 * head == tgt_ref[:, b : b + 1]
-        picked = jnp.sum(jnp.where(hit, logits, 0.0), axis=-1, keepdims=True)
-        stats = jnp.where(lane == b, g, stats)
-        stats = jnp.where(lane == books + b, s, stats)
-        stats = jnp.where(lane == 2 * books + b, picked, stats)
+    for i in range(2):
+        w = hw_ref[:, i * share : (i + 1) * share, :].reshape(parts * width, 256)
+        both = jnp.dot(final, w, preferred_element_type=F32)
+        for j in range(2):
+            b = 2 * j + i
+            logits = both[:, 128 * j : 128 * j + 128]
+            g = jnp.max(logits, axis=-1, keepdims=True)
+            s = jnp.sum(jnp.exp(logits - g), axis=-1, keepdims=True)
+            hit = lane + 128 * head == tgt_ref[:, b : b + 1]
+            picked = jnp.sum(jnp.where(hit, logits, 0.0), axis=-1, keepdims=True)
+            stats = jnp.where(lane == b, g, stats)
+            stats = jnp.where(lane == books + b, s, stats)
+            stats = jnp.where(lane == 2 * books + b, picked, stats)
     stat_ref[...] = stats
 
 
-def tail(place, att8, near, far, x8, hw, tgt):
+def tail(place, att8, x8, hw, tgt, near, far):
     parts, rows, width = x8.shape
     return pl.pallas_call(
         tail_kernel,
@@ -274,7 +284,7 @@
             jax.ShapeDtypeStruct((rows, width), BF),
             jax.ShapeDtypeStruct((rows, 128), F32),
         ),
-        in_specs=[SMEM] + [VMEM] * 6,
+        in_specs=[SMEM] + [VMEM] * 12,
         out_specs=(VMEM, VMEM),
         scratch_shapes=[
             pltpu.VMEM((rows, parts * 128), BF),
@@ -282,9 +292,9 @@
             pltpu.VMEM((rows, parts * width), BF),
         ],
         compiler_params=PARAMS,
-        cost_estimate=cost(6),
+        cost_estimate=SMALL,
         name="tail",
-    )(place, att8, near, far, x8, hw, tgt)
+    )(place, att8, x8, hw, tgt, *near, *far)
 
 
 def loss_kernel(s_ref, out_ref):
@@ -310,6 +320,7 @@
         out_shape=jax.ShapeDtypeStruct((books, spread.shape[1]), F32),
         in_specs=[VMEM],
         out_specs=VMEM,
+        cost_estimate=SMALL,
         name="loss",
     )(spread)
 
@@ -323,15 +334,11 @@
     slot = z * 2 + c
     first = (y * 8 + slot) * rows
 
+    flat = heads_w.reshape(2, -1, heads_w.shape[-1])
+    rows_here = jnp.concatenate([flat[0], flat[1]], axis=1)
+    plane = trade(jnp.broadcast_to(rows_here[None], (8,) + rows_here.shape), ("z", "c"))
     devices = lax.axis_size(SEQ)
-    rim = lax.ppermute(codes[:, rows - 3 :], SEQ, [(i, i + 1) for i in range(devices - 1)])
-    half = wout.shape[1] // 2
-    pair = exchange(lax.dynamic_slice_in_dim(wout, c * half, half, 1), "h", 1)
-    near = lax.all_gather(pair, "x", axis=0).reshape(8, wout.shape[0], half)
-    far = flip(near, "c", 1)
-    hw = exchange(exchange(exchange(heads_w, "c", 1), "z", 1), "z", 2)
-    hw, near = lax.optimization_barrier((hw, near))
-    hw = lax.all_gather(hw, "y", axis=0).reshape((-1,) + heads_w.shape)
+    behind = lax.ppermute(codes, SEQ, [(i, i + 1) for i in range(devices - 1)])
     w3 = jnp.transpose(wqkv, (1, 0, 2))
 
     columns = head * width + jnp.arange(width, dtype=jnp.int32)
@@ -339,7 +346,7 @@
     frame_pos = first + local
     pos = lax.optimization_barrier(sinusoid(frame_pos.astype(F32), columns, width * 8))
 
-    extended = jnp.concatenate([rim, codes], axis=1)
+    extended = jnp.concatenate([behind[:, rows - 3 :], codes], axis=1)
     ids = jnp.zeros((books, rows), jnp.int32)
     for d in range(4):
         ids = jnp.where(delays[:, None] == d, extended[:, 3 - d : 3 - d + rows], ids)
@@ -351,22 +358,35 @@
         preferred_element_type=F32,
     )
     x_part = (summed + pos).astype(BF)
-
-    x8 = gather_heads(x_part)
+    x_part, plane = lax.optimization_barrier((x_part, plane))
+    hw = lax.all_gather(plane, "y", axis=0).reshape((-1,) + rows_here.shape)
+
+    other = flip(x_part, "h", 1)
+    both = jnp.stack([jnp.where(h == 0, x_part, other), jnp.where(h == 0, other, x_part)])
+    x8 = trade(jnp.broadcast_to(both[None], (4,) + both.shape), "x").reshape((8,) + x_part.shape)
+    half = wout.shape[1] // 2
+    mine = after(lax.dynamic_slice_in_dim(wout, c * half, half, 1), both)
+    theirs = flip(mine, "h", 1)
+
     q, kv = project(x8, w3)
-
-    q8 = gather(q, "y")
+    q8 = trade(q, "y")
     kv2 = jnp.stack([kv, flip(kv, "z", 2)])
+    kv2 = after(kv2, theirs)
     kv4 = jnp.concatenate([kv2, flip(kv2, "z", 1)])
     kv4_far = flip(kv4, "c", 1)
-
     partial = attend(jnp.stack([y, slot]).astype(jnp.int32), q8, kv4, kv4_far)
-    spread = lax.all_to_all(partial, "y", 0, 0, tiled=True)
-    att8 = gather_heads(merge(spread))
-
-    place = jnp.stack([head, c]).astype(jnp.int32)
-    mixed, stats = tail(place, att8, near, far, x8, hw, jnp.transpose(targets))
-    shares = lax.all_to_all(stats.reshape(8, rows // 8, 128), HEAD, 0, 0, tiled=True)
+    pair = jnp.stack(after([mine, theirs], partial))
+    near = [pair] + [shift(pair, "x", k) for k in (1, 2, 3)]
+
+    att = merge(trade(partial, "y"))
+    waits = [partial, att, att, att]
+    far = [flip(after(n, first), "c", 1) for n, first in zip(near, waits)]
+    att8 = trade(att, HEAD)
+
+    order = [((x - k) % 4) * 2 + (h ^ j) for k in range(4) for j in range(2)]
+    place = jnp.stack([head, c] + order).astype(jnp.int32)
+    mixed, stats = tail(place, att8, x8, hw, jnp.transpose(targets), near, far)
+    shares = trade(stats.reshape(8, rows // 8, 128), HEAD)
     return (mixed, final_loss(shares, books))
 
 

time: 219 us -> 184 us (0.84)
  blocking collectives: 44.1 us -> 18.4 us
  waiting for transfers between devices: 55.2 us -> 39.9 us
  starting transfers between devices: 64 us -> 72.3 us
  other arithmetic: 9.09 us -> 5.46 us
  Pallas kernels: 21.9 us -> 25.2 us
    all_to_all x2 -> x1, blocking collectives: 44.1 us -> 18.4 us  [trade(): return lax.all_to_all(array, axis, 0, 0, tiled=True)]
    all_to_all x3 -> x5, starting transfers between devices: 15.9 us -> 28.3 us  [trade(): return lax.all_to_all(array, axis, 0, 0, tiled=True)]
    ppermute x10 -> x9, starting transfers between devices: 46.2 us -> 33.9 us  [flip(): return lax.ppermute(array, axis, [(i, i ^ by) for i in range(size)])]
    all_to_all x3 -> x5, waiting for transfers between devices: 33.2 us -> 21.1 us  [trade(): return lax.all_to_all(array, axis, 0, 0, tiled=True)]
    ppermute x10 -> x9, waiting for transfers between devices: 22 us -> 13.4 us  [flip(): return lax.ppermute(array, axis, [(i, i ^ by) for i in range(size)])]
    ppermute x1 -> x4, starting transfers between devices: 1.91 us -> 10.1 us  [the longest x3 8.07 us: shift(): lax.ppermute(array, axis, [(i, (i + by) % size) for i in range(size)])]
    ppermute x1 -> x4, waiting for transfers between devices: 0.01 us -> 4.71 us  [the longest x3 4.71 us: shift(): lax.ppermute(array, axis, [(i, (i + by) % size) for i in range(size)])]
    another operation x13 -> x3, other arithmetic: 5.28 us -> 1.84 us  [the longest x1 1.79 us: shards(): pair = jnp.stack(after([mine, theirs], partial))]
  transfers between devices with their start and end apart: 16 -> 19, of which waited for: 8 -> 8; matrix products, arithmetic and copies ran while one was open for 6% -> 6% of each run, Pallas kernels for 7% -> 10%
where the time goes in v3:
time: 184 us; the launch traced here: 183 us
  starting transfers between devices  72.3 us (39%)
  waiting for transfers between devices  39.9 us (22%)
  Pallas kernels  25.2 us (14%)
  blocking collectives  18.4 us (10%)
  between operations  14.4 us (8%)
  local copies, waits for them, and re-layouts  6.67 us (4%)
  other arithmetic  5.46 us (3%)
    ppermute x9, starting transfers between devices, flip(): return lax.ppermute(array, axis, [(i, i ^ by) for i in range(size)])  33.9 us
    all_to_all x5, starting transfers between devices, trade(): return lax.all_to_all(array, axis, 0, 0, tiled=True)  28.3 us
    all_to_all x5, waiting for transfers between devices, trade(): return lax.all_to_all(array, axis, 0, 0, tiled=True)  21.1 us
    all_to_all x1, blocking collectives, trade(): return lax.all_to_all(array, axis, 0, 0, tiled=True)  18.4 us
    ppermute x9, waiting for transfers between devices, flip(): return lax.ppermute(array, axis, [(i, i ^ by) for i in range(size)])  13.4 us
    pallas_call x1, Pallas kernels, attend(): pl.pallas_call(attend_kernel, grid_spec=pltpu.PrefetchScalarGridSpec(num_...  13.3 us
    ppermute x3, starting transfers between devices, shift(): lax.ppermute(array, axis, [(i, (i + by) % size) for i in range(size)])  8.07 us
    pallas_call x1, Pallas kernels, tail(): pl.pallas_call(tail_kernel, out_shape=(jax.ShapeDtypeStruct((rows, width)...  5.72 us
  transfers between devices with their start and end apart: 19, of which 8 were waited for; matrix products, arithmetic and copies ran while one was open for 6% of the time, Pallas kernels for 10%

profile of v3, /device:TPU:72, one launch (start us, length us, event | category | flops | bytes accessed | tf_op | source)
XLA Modules:
  0.0 183.2 jit_solution(14433911196339871243)
XLA Ops:
  7.2 0.0 copy-start
  7.2 2.1 %collective-permute-start = (s32[4,256]{1,0:T(4,128)}, s32[4,256]{1,0:T(4,128)S(1)}, u32[]{:S(2)}, u32[]{:S(2)}) collective-permute-start(s32[4,256]{1,0:T(4,128)} %param.7), channel_id=1, source_target_pairs={{0,8},{8,16},{16,24},{24,32},{32,40},{40,48},{48,56},{56,64},{64,7... | collective-permute-start | bytes 12296 | tf_op jit(solution)/shard_map/ppermute | solution.py:341
  9.2 0.7 fusion.19
  10.0 0.7 broadcast_in_dim.68
  10.7 7.2 %all-to-all-start = ((bf16[8,64,256]{2,1,0:T(8,128)(2,1)}), bf16[8,64,256]{2,1,0:T(8,128)(2,1)S(1)}, u32[]{:S(2)}, u32[]{:S(2)}) async-start(bf16[8,64,256]{2,1,0:T(8,128)(2,1)} %broadcast_in_dim.68), calls=%async_computation | async-start | bytes 524288 | tf_op jit(solution)/shard_map/all_to_all | solution.py:35
  17.9 0.7 broadcast_compare_fusion.3
  18.6 1.0 fusion.5
  19.6 0.0 collective-permute-done
  19.6 0.1 slice.26
  19.7 0.9 fusion.10
  20.6 0.0 copy-done
  20.6 0.9 fusion.4
  21.5 4.3 %all-to-all-done = bf16[8,64,256]{2,1,0:T(8,128)(2,1)S(1)} async-done(((bf16[8,64,256]{2,1,0:T(8,128)(2,1)}), bf16[8,64,256]{2,1,0:T(8,128)(2,1)S(1)}, u32[]{:S(2)}, u32[]{:S(2)}) %all-to-all-start) | async-done | bytes 262176 | tf_op jit(solution)/shard_map/all_to_all | solution.py:35
  25.8 9.2 %collective-permute-start.1 = (bf16[256,256]{1,0:T(8,128)(2,1)S(1)}, bf16[256,256]{1,0:T(8,128)(2,1)S(1)}, u32[]{:S(2)}, u32[]{:S(2)}) collective-permute-start(bf16[256,256]{1,0:T(8,128)(2,1)S(1)} %fusion.4), channel_id=1, source_target_pairs={{0,1},{1,0},{2,3},{3,2},{4,5},{5,4},{6,7},{7,6},{8,9},{9,8},{10,11... | collective-permute-start | bytes 393224 | tf_op jit(solution)/shard_map/ppermute | solution.py:26
  35.0 6.1 %collective-permute-done.1 = bf16[256,256]{1,0:T(8,128)(2,1)S(1)} collective-permute-done((bf16[256,256]{1,0:T(8,128)(2,1)S(1)}, bf16[256,256]{1,0:T(8,128)(2,1)S(1)}, u32[]{:S(2)}, u32[]{:S(2)}) %collective-permute-start.1) | collective-permute-done | bytes 131104 | tf_op jit(solution)/shard_map/ppermute | solution.py:26
  41.1 1.1 broadcast_in_dim.69
  42.2 0.0 copy-done.2
  42.2 4.3 %all-to-all-start.1 = ((bf16[4,2,256,256]{3,2,1,0:T(8,128)(2,1)}), bf16[4,2,256,256]{3,2,1,0:T(8,128)(2,1)S(1)}, u32[]{:S(2)}, u32[]{:S(2)}) async-start(bf16[4,2,256,256]{3,2,1,0:T(8,128)(2,1)} %broadcast_in_dim.69), calls=%async_computation.1 | async-start | bytes 2097152 | tf_op jit(solution)/shard_map/all_to_all | solution.py:35
  46.5 0.0 all-gather.3.cloned.1.call-start
  46.5 0.7 all-gather.3.cloned.1.call-update
  47.2 1.0 constant_dynamic-slice_fusion
  48.2 7.5 %collective-permute-start.3 = (bf16[128,1024]{1,0:T(8,128)(2,1)S(1)}, bf16[128,1024]{1,0:T(8,128)(2,1)}, u32[]{:S(2)}, u32[]{:S(2)}) collective-permute-start(bf16[128,1024]{1,0:T(8,128)(2,1)S(1)} %constant_dynamic-slice_fusion), channel_id=1, source_target_pairs={{0,1},{1,0},{2,3},{3,2},{4,5},{5,4},{6,7},{7,6},{8,9},{9,8},{10,11... | collective-permute-start | bytes 786440 | tf_op jit(solution)/shard_map/ppermute | solution.py:26
  55.7 2.0 %all-to-all-done.1 = bf16[4,2,256,256]{3,2,1,0:T(8,128)(2,1)S(1)} async-done(((bf16[4,2,256,256]{3,2,1,0:T(8,128)(2,1)}), bf16[4,2,256,256]{3,2,1,0:T(8,128)(2,1)S(1)}, u32[]{:S(2)}, u32[]{:S(2)}) %all-to-all-start.1) | async-done | bytes 1048608 | tf_op jit(solution)/shard_map/all_to_all | solution.py:35
  57.6 1.4 copy-done.1
  59.0 1.8 %project.1 = (bf16[8,256,128]{2,1,0:T(8,128)(2,1)}, bf16[256,256]{1,0:T(8,128)(2,1)S(1)}) custom-call(bf16[8,256,256]{2,1,0:T(8,128)(2,1)S(1)} %bitcast.35, bf16[3,2048,128]{2,1,0:T(8,128)(2,1)S(1)} %bitcast.37), custom_call_target="tpu_custom_call" | custom-call | flops 1 | bytes 1 | tf_op jit(solution)/shard_map/project/pallas_call | solution.py:72
  60.9 4.8 %collective-permute-start.2 = (bf16[256,256]{1,0:T(8,128)(2,1)S(1)}, bf16[256,256]{1,0:T(8,128)(2,1)}, u32[]{:S(2)}, u32[]{:S(2)}) collective-permute-start(bf16[256,256]{1,0:T(8,128)(2,1)S(1)} %get-tuple-element.18), channel_id=1, source_target_pairs={{0,32},{16,48},{32,0},{48,16},{1,33},{17,49},{33,1},{49,17},{2,34}... | collective-permute-start | bytes 393224 | tf_op jit(solution)/shard_map/ppermute | solution.py:26
  65.8 6.7 %all-to-all-start.2 = ((bf16[8,256,128]{2,1,0:T(8,128)(2,1)}), bf16[8,256,128]{2,1,0:T(8,128)(2,1)}, u32[]{:S(2)}, u32[]{:S(2)}) async-start(bf16[8,256,128]{2,1,0:T(8,128)(2,1)} %get-tuple-element.17), calls=%async_computation.2 | async-start | bytes 1048576 | tf_op jit(solution)/shard_map/all_to_all | solution.py:35
  72.4 0.0 collective-permute-done.2
  72.4 0.9 pad_maximum_fusion.2
  73.3 0.0 collective-permute-done.3
  73.4 1.9 %collective-permute-start.4 = (bf16[2,256,256]{2,1,0:T(8,128)(2,1)S(1)}, bf16[2,256,256]{2,1,0:T(8,128)(2,1)S(1)}, u32[]{:S(2)}, u32[]{:S(2)}) collective-permute-start(bf16[2,256,256]{2,1,0:T(8,128)(2,1)S(1)} %pad_maximum_fusion.2), channel_id=1, source_target_pairs={{0,16},{16,0},{32,48},{48,32},{1,17},{17,1},{33,49},{49,33},{2,18}... | collective-permute-start | bytes 786440 | tf_op jit(solution)/shard_map/ppermute | solution.py:26
  75.3 0.7 constant_dynamic-update-slice_fusion.1
  76.0 5.6 %collective-permute-done.4 = bf16[2,256,256]{2,1,0:T(8,128)(2,1)S(1)} collective-permute-done((bf16[2,256,256]{2,1,0:T(8,128)(2,1)S(1)}, bf16[2,256,256]{2,1,0:T(8,128)(2,1)S(1)}, u32[]{:S(2)}, u32[]{:S(2)}) %collective-permute-start.4) | collective-permute-done | bytes 262176 | tf_op jit(solution)/shard_map/ppermute | solution.py:26
  81.6 0.7 constant_dynamic-update-slice_fusion.near_ref
  82.4 2.1 %collective-permute-start.5 = (bf16[4,256,256]{2,1,0:T(8,128)(2,1)}, bf16[4,256,256]{2,1,0:T(8,128)(2,1)}, u32[]{:S(2)}, u32[]{:S(2)}) collective-permute-start(bf16[4,256,256]{2,1,0:T(8,128)(2,1)} %constant_dynamic-update-slice_fusion.near_ref), channel_id=1, source_target_pairs={{0,8},{8,0},{1,9},{9,1},{2,10},{10,2},{3,11},{11,3},{4,12},{12,4},... | collective-permute-start | bytes 1572872 | tf_op jit(solution)/shard_map/ppermute | solution.py:26
  84.5 0.1 pad_add_fusion.1.place_ref
  84.5 9.5 %all-to-all-done.2.q_ref = bf16[8,256,128]{2,1,0:T(8,128)(2,1)} async-done(((bf16[8,256,128]{2,1,0:T(8,128)(2,1)}), bf16[8,256,128]{2,1,0:T(8,128)(2,1)}, u32[]{:S(2)}, u32[]{:S(2)}) %all-to-all-start.2) | async-done | bytes 524320 | tf_op jit(solution)/shard_map/all_to_all | solution.py:35
  94.0 0.0 collective-permute-done.5.far_ref
  94.1 13.3 %attend.1 = bf16[8,272,128]{2,1,0:T(8,128)(2,1)} custom-call(s32[2]{0:T(128)S(1)} %pad_add_fusion.1.place_ref, bf16[8,256,128]{2,1,0:T(8,128)(2,1)} %all-to-all-done.2.q_ref, bf16[4,256,256]{2,1,0:T(8,128)(2,1)} %constant_dynamic-update-slice_fusion.near_ref, bf16[4,256,256]{2,1,0:T(8,128)(2,1)} %collective-permute-done.5.far_ref), custom_call_target="tpu_custom_call" | custom-call | flops 1 | bytes 1 | tf_op jit(solution)/shard_map/attend/pallas_call | solution.py:184
  107.4 5.7 %all-to-all-start.3 = ((bf16[8,272,128]{2,1,0:T(8,128)(2,1)}), bf16[8,272,128]{2,1,0:T(8,128)(2,1)}, u32[]{:S(2)}, u32[]{:S(2)}) async-start(bf16[8,272,128]{2,1,0:T(8,128)(2,1)} %attend.1), calls=%async_computation.3 | async-start | bytes 1114112 | tf_op jit(solution)/shard_map/all_to_all | solution.py:35
  113.1 1.8 pad_maximum_fusion.refs_0_
  114.9 3.4 %collective-permute-start.8 = (bf16[2,128,1024]{2,1,0:T(8,128)(2,1)}, bf16[2,128,1024]{2,1,0:T(8,128)(2,1)}, u32[]{:S(2)}, u32[]{:S(2)}) collective-permute-start(bf16[2,128,1024]{2,1,0:T(8,128)(2,1)} %pad_maximum_fusion.refs_0_), channel_id=1, source_target_pairs={{0,6},{2,0},{4,2},{6,4},{1,7},{3,1},{5,3},{7,5},{8,14},{10,8},{12,... | collective-permute-start | bytes 1572872 | tf_op jit(solution)/shard_map/ppermute | solution.py:31
  118.3 2.2 %collective-permute-start.7 = (bf16[2,128,1024]{2,1,0:T(8,128)(2,1)}, bf16[2,128,1024]{2,1,0:T(8,128)(2,1)}, u32[]{:S(2)}, u32[]{:S(2)}) collective-permute-start(bf16[2,128,1024]{2,1,0:T(8,128)(2,1)} %pad_maximum_fusion.refs_0_), channel_id=1, source_target_pairs={{0,4},{2,6},{4,0},{6,2},{1,5},{3,7},{5,1},{7,3},{8,12},{10,14},{12... | collective-permute-start | bytes 1572872 | tf_op jit(solution)/shard_map/ppermute | solution.py:31
  120.5 2.5 %collective-permute-start.6 = (bf16[2,128,1024]{2,1,0:T(8,128)(2,1)}, bf16[2,128,1024]{2,1,0:T(8,128)(2,1)}, u32[]{:S(2)}, u32[]{:S(2)}) collective-permute-start(bf16[2,128,1024]{2,1,0:T(8,128)(2,1)} %pad_maximum_fusion.refs_0_), channel_id=1, source_target_pairs={{0,2},{2,4},{4,6},{6,0},{1,3},{3,5},{5,7},{7,1},{8,10},{10,12},{12... | collective-permute-start | bytes 1572872 | tf_op jit(solution)/shard_map/ppermute | solution.py:31
  123.0 5.3 %all-to-all-done.3.o_ref = bf16[8,272,128]{2,1,0:T(8,128)(2,1)} async-done(((bf16[8,272,128]{2,1,0:T(8,128)(2,1)}), bf16[8,272,128]{2,1,0:T(8,128)(2,1)}, u32[]{:S(2)}, u32[]{:S(2)}) %all-to-all-start.3) | async-done | bytes 557088 | tf_op jit(solution)/shard_map/all_to_all | solution.py:35
  128.3 2.6 %merge.1 = bf16[8,256,128]{2,1,0:T(8,128)(2,1)} custom-call(bf16[8,272,128]{2,1,0:T(8,128)(2,1)} %all-to-all-done.3.o_ref), custom_call_target="tpu_custom_call" | custom-call | flops 1 | bytes 1 | tf_op jit(solution)/shard_map/merge/pallas_call | solution.py:224
  131.0 4.4 %all-to-all-start.4 = ((bf16[8,256,128]{2,1,0:T(8,128)(2,1)}), bf16[8,256,128]{2,1,0:T(8,128)(2,1)}, u32[]{:S(2)}, u32[]{:S(2)}) async-start(bf16[8,256,128]{2,1,0:T(8,128)(2,1)} %merge.1), calls=%async_computation.4 | async-start | bytes 1048576 | tf_op jit(solution)/shard_map/all_to_all | solution.py:35
  135.4 1.9 %collective-permute-start.9 = (bf16[2,128,1024]{2,1,0:T(8,128)(2,1)}, bf16[2,128,1024]{2,1,0:T(8,128)(2,1)}, u32[]{:S(2)}, u32[]{:S(2)}) collective-permute-start(bf16[2,128,1024]{2,1,0:T(8,128)(2,1)} %pad_maximum_fusion.refs_0_), channel_id=1, source_target_pairs={{0,8},{8,0},{1,9},{9,1},{2,10},{10,2},{3,11},{11,3},{4,12},{12,4},... | collective-permute-start | bytes 1572872 | tf_op jit(solution)/shard_map/ppermute | solution.py:26
  137.3 0.0 collective-permute-done.8.refs_3_
  137.3 2.4 %collective-permute-start.12 = (bf16[2,128,1024]{2,1,0:T(8,128)(2,1)}, bf16[2,128,1024]{2,1,0:T(8,128)(2,1)}, u32[]{:S(2)}, u32[]{:S(2)}) collective-permute-start(bf16[2,128,1024]{2,1,0:T(8,128)(2,1)} %collective-permute-done.8.refs_3_), channel_id=1, source_target_pairs={{0,8},{8,0},{1,9},{9,1},{2,10},{10,2},{3,11},{11,3},{4,12},{12,4},... | collective-permute-start | bytes 1572872 | tf_op jit(solution)/shard_map/ppermute | solution.py:26
  139.7 0.0 collective-permute-done.7.refs_2_
  139.8 1.9 %collective-permute-start.11 = (bf16[2,128,1024]{2,1,0:T(8,128)(2,1)}, bf16[2,128,1024]{2,1,0:T(8,128)(2,1)}, u32[]{:S(2)}, u32[]{:S(2)}) collective-permute-start(bf16[2,128,1024]{2,1,0:T(8,128)(2,1)} %collective-permute-done.7.refs_2_), channel_id=1, source_target_pairs={{0,8},{8,0},{1,9},{9,1},{2,10},{10,2},{3,11},{11,3},{4,12},{12,4},... | collective-permute-start | bytes 1572872 | tf_op jit(solution)/shard_map/ppermute | solution.py:26
  141.7 4.7 %collective-permute-done.6.refs_1_ = bf16[2,128,1024]{2,1,0:T(8,128)(2,1)} collective-permute-done((bf16[2,128,1024]{2,1,0:T(8,128)(2,1)}, bf16[2,128,1024]{2,1,0:T(8,128)(2,1)}, u32[]{:S(2)}, u32[]{:S(2)}) %collective-permute-start.6) | collective-permute-done | bytes 524320 | tf_op jit(solution)/shard_map/ppermute | solution.py:31
  146.4 2.1 %collective-permute-start.10 = (bf16[2,128,1024]{2,1,0:T(8,128)(2,1)}, bf16[2,128,1024]{2,1,0:T(8,128)(2,1)}, u32[]{:S(2)}, u32[]{:S(2)}) collective-permute-start(bf16[2,128,1024]{2,1,0:T(8,128)(2,1)} %collective-permute-done.6.refs_1_), channel_id=1, source_target_pairs={{0,8},{8,0},{1,9},{9,1},{2,10},{10,2},{3,11},{11,3},{4,12},{12,4},... | collective-permute-start | bytes 1572872 | tf_op jit(solution)/shard_map/ppermute | solution.py:26
  148.6 0.1 copy.10
  148.7 0.1 stack.79.place_ref
  148.8 0.0 collective-permute-done.9.refs_4_
  148.8 0.0 collective-permute-done.12.refs_7_
  148.9 0.0 collective-permute-done.11.refs_6_
  148.9 1.7 collective-permute-done.10.refs_5_
  150.5 0.0 all-to-all-done.4.att_ref
  150.5 5.7 %tail.1 = (bf16[256,256]{1,0:T(8,128)(2,1)}, f32[256,128]{1,0:T(8,128)S(1)}) custom-call(s32[10]{0:T(128)S(1)} %stack.79.place_ref, bf16[8,256,128]{2,1,0:T(8,128)(2,1)} %all-to-all-done.4.att_ref, bf16[8,256,256]{2,1,0:T(8,128)(2,1)S(1)} %bitcast.36, bf16[64,64,256]{2,1,0:T(8,128)(2,1)} %all-gather.3.cloned.1.call-done.hw_ref, s32[256,4]{1,0:T(8,128)S(1)} %bitcast.38, ...), custom_call_target="tpu_custom_call" | custom-call | flops 1 | bytes 1 | tf_op jit(solution)/shard_map/tail/pallas_call | solution.py:281
  156.3 18.4 %all_to_all.30.s_ref = f32[8,32,128]{2,1,0:T(8,128)} all-to-all(f32[8,32,128]{2,1,0:T(8,128)S(1)} %bitcast.39), channel_id=1, replica_groups=mesh['y'=8,'z'=4,'c'=2,'x'=4,'h'=2] {'x','h'}, dimensions={0} | all-to-all | bytes 262144 | tf_op jit(solution)/shard_map/all_to_all | solution.py:35
  174.7 1.7 loss.1
  (12 shorter events, 0.1 us)
Async XLA Ops:
  7.2 13.5 %copy-start = (bf16[4,1024,256]{2,1,0:T(8,128)(2,1)S(1)}, bf16[4,1024,256]{2,1,0:T(8,128)(2,1)}, u32[]{:S(2)}) copy-start(bf16[4,1024,256]{2,1,0:T(8,128)(2,1)} %param.10) | copy-start | bytes 6291460
  7.2 12.4 %collective-permute-start = (s32[4,256]{1,0:T(4,128)}, s32[4,256]{1,0:T(4,128)S(1)}, u32[]{:S(2)}, u32[]{:S(2)}) collective-permute-start(s32[4,256]{1,0:T(4,128)} %param.7), channel_id=1, source_target_pairs={{0,8},{8,16},{16,24},{24,32},{32,40},{40,48},{48,56},{56,64},{64,7... | collective-permute-start | bytes 12296 | tf_op jit(solution)/shard_map/ppermute | solution.py:341
  10.7 15.1 %all-to-all-start = ((bf16[8,64,256]{2,1,0:T(8,128)(2,1)}), bf16[8,64,256]{2,1,0:T(8,128)(2,1)S(1)}, u32[]{:S(2)}, u32[]{:S(2)}) async-start(bf16[8,64,256]{2,1,0:T(8,128)(2,1)} %broadcast_in_dim.68), calls=%async_computation | async-start | bytes 524288 | tf_op jit(solution)/shard_map/all_to_all | solution.py:35
  25.8 16.4 %copy-start.2 = (bf16[8,64,256]{2,1,0:T(8,128)(2,1)}, bf16[8,64,256]{2,1,0:T(8,128)(2,1)S(1)}, u32[]{:S(2)}) copy-start(bf16[8,64,256]{2,1,0:T(8,128)(2,1)S(1)} %all-to-all-done) | copy-start | bytes 786436
  25.8 15.3 %collective-permute-start.1 = (bf16[256,256]{1,0:T(8,128)(2,1)S(1)}, bf16[256,256]{1,0:T(8,128)(2,1)S(1)}, u32[]{:S(2)}, u32[]{:S(2)}) collective-permute-start(bf16[256,256]{1,0:T(8,128)(2,1)S(1)} %fusion.4), channel_id=1, source_target_pairs={{0,1},{1,0},{2,3},{3,2},{4,5},{5,4},{6,7},{7,6},{8,9},{9,8},{10,11... | collective-permute-start | bytes 393224 | tf_op jit(solution)/shard_map/ppermute | solution.py:26
  42.2 15.5 %all-to-all-start.1 = ((bf16[4,2,256,256]{3,2,1,0:T(8,128)(2,1)}), bf16[4,2,256,256]{3,2,1,0:T(8,128)(2,1)S(1)}, u32[]{:S(2)}, u32[]{:S(2)}) async-start(bf16[4,2,256,256]{3,2,1,0:T(8,128)(2,1)} %broadcast_in_dim.69), calls=%async_computation.1 | async-start | bytes 2097152 | tf_op jit(solution)/shard_map/all_to_all | solution.py:35
  46.5 104.1 %all-gather.3.cloned.1.call-start = ((), (), s32[]{:S(2)}) async-start(), calls=%async_computation.6 | async-start | bytes 2359296 | tf_op jit(solution)/shard_map/all_gather | solution.py:362
  48.2 25.2 %collective-permute-start.3 = (bf16[128,1024]{1,0:T(8,128)(2,1)S(1)}, bf16[128,1024]{1,0:T(8,128)(2,1)}, u32[]{:S(2)}, u32[]{:S(2)}) collective-permute-start(bf16[128,1024]{1,0:T(8,128)(2,1)S(1)} %constant_dynamic-slice_fusion), channel_id=1, source_target_pairs={{0,1},{1,0},{2,3},{3,2},{4,5},{5,4},{6,7},{7,6},{8,9},{9,8},{10,11... | collective-permute-start | bytes 786440 | tf_op jit(solution)/shard_map/ppermute | solution.py:26
  57.6 1.4 copy-start.1
  60.9 11.5 %collective-permute-start.2 = (bf16[256,256]{1,0:T(8,128)(2,1)S(1)}, bf16[256,256]{1,0:T(8,128)(2,1)}, u32[]{:S(2)}, u32[]{:S(2)}) collective-permute-start(bf16[256,256]{1,0:T(8,128)(2,1)S(1)} %get-tuple-element.18), channel_id=1, source_target_pairs={{0,32},{16,48},{32,0},{48,16},{1,33},{17,49},{33,1},{49,17},{2,34}... | collective-permute-start | bytes 393224 | tf_op jit(solution)/shard_map/ppermute | solution.py:26
  65.8 28.3 %all-to-all-start.2 = ((bf16[8,256,128]{2,1,0:T(8,128)(2,1)}), bf16[8,256,128]{2,1,0:T(8,128)(2,1)}, u32[]{:S(2)}, u32[]{:S(2)}) async-start(bf16[8,256,128]{2,1,0:T(8,128)(2,1)} %get-tuple-element.17), calls=%async_computation.2 | async-start | bytes 1048576 | tf_op jit(solution)/shard_map/all_to_all | solution.py:35
  73.4 8.3 %collective-permute-start.4 = (bf16[2,256,256]{2,1,0:T(8,128)(2,1)S(1)}, bf16[2,256,256]{2,1,0:T(8,128)(2,1)S(1)}, u32[]{:S(2)}, u32[]{:S(2)}) collective-permute-start(bf16[2,256,256]{2,1,0:T(8,128)(2,1)S(1)} %pad_maximum_fusion.2), channel_id=1, source_target_pairs={{0,16},{16,0},{32,48},{48,32},{1,17},{17,1},{33,49},{49,33},{2,18}... | collective-permute-start | bytes 786440 | tf_op jit(solution)/shard_map/ppermute | solution.py:26
  82.4 11.7 %collective-permute-start.5 = (bf16[4,256,256]{2,1,0:T(8,128)(2,1)}, bf16[4,256,256]{2,1,0:T(8,128)(2,1)}, u32[]{:S(2)}, u32[]{:S(2)}) collective-permute-start(bf16[4,256,256]{2,1,0:T(8,128)(2,1)} %constant_dynamic-update-slice_fusion.near_ref), channel_id=1, source_target_pairs={{0,8},{8,0},{1,9},{9,1},{2,10},{10,2},{3,11},{11,3},{4,12},{12,4},... | collective-permute-start | bytes 1572872 | tf_op jit(solution)/shard_map/ppermute | solution.py:26
  107.4 41.2 %copy-start.3 = (s32[4,256]{1,0:T(4,128)S(1)}, s32[4,256]{1,0:T(4,128)}, u32[]{:S(2)}) copy-start(s32[4,256]{1,0:T(4,128)} %param.9) | copy-start | bytes 12292
  107.4 20.9 %all-to-all-start.3 = ((bf16[8,272,128]{2,1,0:T(8,128)(2,1)}), bf16[8,272,128]{2,1,0:T(8,128)(2,1)}, u32[]{:S(2)}, u32[]{:S(2)}) async-start(bf16[8,272,128]{2,1,0:T(8,128)(2,1)} %attend.1), calls=%async_computation.3 | async-start | bytes 1114112 | tf_op jit(solution)/shard_map/all_to_all | solution.py:35
  114.9 22.4 %collective-permute-start.8 = (bf16[2,128,1024]{2,1,0:T(8,128)(2,1)}, bf16[2,128,1024]{2,1,0:T(8,128)(2,1)}, u32[]{:S(2)}, u32[]{:S(2)}) collective-permute-start(bf16[2,128,1024]{2,1,0:T(8,128)(2,1)} %pad_maximum_fusion.refs_0_), channel_id=1, source_target_pairs={{0,6},{2,0},{4,2},{6,4},{1,7},{3,1},{5,3},{7,5},{8,14},{10,8},{12,... | collective-permute-start | bytes 1572872 | tf_op jit(solution)/shard_map/ppermute | solution.py:31
  118.3 21.4 %collective-permute-start.7 = (bf16[2,128,1024]{2,1,0:T(8,128)(2,1)}, bf16[2,128,1024]{2,1,0:T(8,128)(2,1)}, u32[]{:S(2)}, u32[]{:S(2)}) collective-permute-start(bf16[2,128,1024]{2,1,0:T(8,128)(2,1)} %pad_maximum_fusion.refs_0_), channel_id=1, source_target_pairs={{0,4},{2,6},{4,0},{6,2},{1,5},{3,7},{5,1},{7,3},{8,12},{10,14},{12... | collective-permute-start | bytes 1572872 | tf_op jit(solution)/shard_map/ppermute | solution.py:31
  120.5 25.8 %collective-permute-start.6 = (bf16[2,128,1024]{2,1,0:T(8,128)(2,1)}, bf16[2,128,1024]{2,1,0:T(8,128)(2,1)}, u32[]{:S(2)}, u32[]{:S(2)}) collective-permute-start(bf16[2,128,1024]{2,1,0:T(8,128)(2,1)} %pad_maximum_fusion.refs_0_), channel_id=1, source_target_pairs={{0,2},{2,4},{4,6},{6,0},{1,3},{3,5},{5,7},{7,1},{8,10},{10,12},{12... | collective-permute-start | bytes 1572872 | tf_op jit(solution)/shard_map/ppermute | solution.py:31
  131.0 19.5 %all-to-all-start.4 = ((bf16[8,256,128]{2,1,0:T(8,128)(2,1)}), bf16[8,256,128]{2,1,0:T(8,128)(2,1)}, u32[]{:S(2)}, u32[]{:S(2)}) async-start(bf16[8,256,128]{2,1,0:T(8,128)(2,1)} %merge.1), calls=%async_computation.4 | async-start | bytes 1048576 | tf_op jit(solution)/shard_map/all_to_all | solution.py:35
  135.4 13.4 %collective-permute-start.9 = (bf16[2,128,1024]{2,1,0:T(8,128)(2,1)}, bf16[2,128,1024]{2,1,0:T(8,128)(2,1)}, u32[]{:S(2)}, u32[]{:S(2)}) collective-permute-start(bf16[2,128,1024]{2,1,0:T(8,128)(2,1)} %pad_maximum_fusion.refs_0_), channel_id=1, source_target_pairs={{0,8},{8,0},{1,9},{9,1},{2,10},{10,2},{3,11},{11,3},{4,12},{12,4},... | collective-permute-start | bytes 1572872 | tf_op jit(solution)/shard_map/ppermute | solution.py:26
  137.3 11.5 %collective-permute-start.12 = (bf16[2,128,1024]{2,1,0:T(8,128)(2,1)}, bf16[2,128,1024]{2,1,0:T(8,128)(2,1)}, u32[]{:S(2)}, u32[]{:S(2)}) collective-permute-start(bf16[2,128,1024]{2,1,0:T(8,128)(2,1)} %collective-permute-done.8.refs_3_), channel_id=1, source_target_pairs={{0,8},{8,0},{1,9},{9,1},{2,10},{10,2},{3,11},{11,3},{4,12},{12,4},... | collective-permute-start | bytes 1572872 | tf_op jit(solution)/shard_map/ppermute | solution.py:26
  139.8 9.1 %collective-permute-start.11 = (bf16[2,128,1024]{2,1,0:T(8,128)(2,1)}, bf16[2,128,1024]{2,1,0:T(8,128)(2,1)}, u32[]{:S(2)}, u32[]{:S(2)}) collective-permute-start(bf16[2,128,1024]{2,1,0:T(8,128)(2,1)} %collective-permute-done.7.refs_2_), channel_id=1, source_target_pairs={{0,8},{8,0},{1,9},{9,1},{2,10},{10,2},{3,11},{11,3},{4,12},{12,4},... | collective-permute-start | bytes 1572872 | tf_op jit(solution)/shard_map/ppermute | solution.py:26
  146.4 4.1 %collective-permute-start.10 = (bf16[2,128,1024]{2,1,0:T(8,128)(2,1)}, bf16[2,128,1024]{2,1,0:T(8,128)(2,1)}, u32[]{:S(2)}, u32[]{:S(2)}) collective-permute-start(bf16[2,128,1024]{2,1,0:T(8,128)(2,1)} %collective-permute-done.6.refs_1_), channel_id=1, source_target_pairs={{0,8},{8,0},{1,9},{9,1},{2,10},{10,2},{3,11},{11,3},{4,12},{12,4},... | collective-permute-start | bytes 1572872 | tf_op jit(solution)/shard_map/ppermute | solution.py:26
Sparse Core Ops, SparseCore 0:
  49.4 53.6 all-gather.2

commit v4 on v3

--- a/solution.py
+++ b/solution.py
@@ -18,7 +18,10 @@
 SMALL = pl.CostEstimate(flops=1, bytes_accessed=1, transcendentals=0)
 SMEM = pl.BlockSpec(memory_space=pltpu.SMEM)
 HBM = pl.BlockSpec(memory_space=pltpu.HBM)
-PARAMS = pltpu.CompilerParams(vmem_limit_bytes=48 * 1024 * 1024)
+
+
+def room(mib):
+    return pltpu.CompilerParams(vmem_limit_bytes=mib * 1024 * 1024)
 
 
 def flip(array, axis, by):
@@ -46,44 +49,36 @@
     return jnp.where(columns[None, :] < half, jnp.sin(angle), jnp.cos(angle))
 
 
-def project_kernel(x_ref, w_ref, q_ref, kv_ref, w_s, n_s, sem):
-    load = pltpu.make_async_copy(w_ref, w_s, sem)
-    load.start()
+def project_kernel(x_ref, w_ref, q_ref, kv_ref):
     parts, _, width = x_ref.shape
     squares = 0.0
     for i in range(parts):
         xi = x_ref[i].astype(F32)
         squares = squares + jnp.sum(xi * xi, axis=-1, keepdims=True)
     r = lax.rsqrt(squares / (parts * width) + 1e-05)
+    sums = [0.0, 0.0, 0.0]
     for i in range(parts):
-        n_s[:, i * width : (i + 1) * width] = (x_ref[i].astype(F32) * r).astype(BF)
-    load.wait()
-    n = n_s[...]
-    q = jnp.dot(n, w_s[0], preferred_element_type=F32).astype(BF)
-    for i in range(q_ref.shape[0]):
-        q_ref[i] = q
-    for j in range(2):
-        kv = jnp.dot(n, w_s[1 + j], preferred_element_type=F32)
-        kv_ref[:, 128 * j : 128 * j + 128] = kv.astype(BF)
+        ni = (x_ref[i].astype(F32) * r).astype(BF)
+        for j in range(3):
+            sums[j] = sums[j] + jnp.dot(
+                ni, w_ref[j, i * width : (i + 1) * width, :], preferred_element_type=F32
+            )
+    q_ref[...] = sums[0].astype(BF)
+    kv_ref[:, :128] = sums[1].astype(BF)
+    kv_ref[:, 128:] = sums[2].astype(BF)
 
 
 def project(x8, w):
-    parts, rows, width = x8.shape
+    rows = x8.shape[1]
     return pl.pallas_call(
         project_kernel,
         out_shape=(
-            pltpu.HBM((8, rows, 128), BF),
+            jax.ShapeDtypeStruct((rows, 128), BF),
             jax.ShapeDtypeStruct((rows, 256), BF),
         ),
-        in_specs=[VMEM, HBM],
+        in_specs=[VMEM, VMEM],
         out_specs=(VMEM, VMEM),
-        scratch_shapes=[
-            pltpu.VMEM(w.shape, BF),
-            pltpu.VMEM((rows, parts * width), BF),
-            pltpu.SemaphoreType.DMA,
-        ],
-        compiler_params=PARAMS,
-        cost_estimate=SMALL,
+        compiler_params=room(12),
         name="project",
     )(x8, w)
 
@@ -179,7 +174,7 @@
 
 def attend(place, q8, near, far):
     planes, rows, _ = q8.shape
-    each = 2
+    each = 4
     whole = pl.BlockSpec(near.shape, lambda i, s: (0, 0, 0))
     return pl.pallas_call(
         attend_kernel,
@@ -191,7 +186,7 @@
             scratch_shapes=[pltpu.VMEM((8, rows, 256), BF)],
         ),
         out_shape=pltpu.HBM((planes, rows + 16, 128), BF),
-        compiler_params=PARAMS,
+        compiler_params=room(24),
         cost_estimate=SMALL,
         name="attend",
     )(place, q8, near, far)
@@ -199,7 +194,7 @@
 
 def merge_kernel(o_ref, out_ref):
     planes = o_ref.shape[0]
-    copies, rows, _ = out_ref.shape
+    rows = out_ref.shape[0]
     lane = lax.broadcasted_iota(jnp.int32, (128, 128), 1)
     for half in range(rows // 128):
         lses = []
@@ -215,24 +210,23 @@
         for i in range(planes):
             wi = jnp.where(lane < 64, w[:, 2 * i : 2 * i + 1], w[:, 2 * i + 1 : 2 * i + 2])
             acc = acc + wi * o_ref[i, 128 * half : 128 * half + 128, :].astype(F32)
-        for i in range(copies):
-            out_ref[i, 128 * half : 128 * half + 128, :] = acc.astype(BF)
+        out_ref[128 * half : 128 * half + 128, :] = acc.astype(BF)
 
 
 def merge(partial):
     rows = partial.shape[1] - 16
     return pl.pallas_call(
         merge_kernel,
-        out_shape=pltpu.HBM((8, rows, 128), BF),
+        out_shape=jax.ShapeDtypeStruct((rows, 128), BF),
         in_specs=[VMEM],
         out_specs=VMEM,
-        compiler_params=PARAMS,
+        compiler_params=room(8),
         cost_estimate=SMALL,
         name="merge",
     )(partial)
 
 
-def tail_kernel(place_ref, att_ref, x_ref, hw_ref, tgt_ref, *refs):
+def tail_kernel(place_ref, att_ref, x_ref, hw_ref, hw_far_ref, tgt_ref, *refs):
     near_refs, far_refs = refs[:4], refs[4:8]
     mixed_ref, stat_ref, a_s, m_s, f_s = refs[8:]
     parts, rows, width = x_ref.shape
@@ -260,23 +254,23 @@
     share = hw_ref.shape[1] // 2
     lane = lax.broadcasted_iota(jnp.int32, (rows, 128), 1)
     stats = jnp.zeros((rows, 128), F32)
-    for i in range(2):
-        w = hw_ref[:, i * share : (i + 1) * share, :].reshape(parts * width, 256)
-        both = jnp.dot(final, w, preferred_element_type=F32)
-        for j in range(2):
-            b = 2 * j + i
-            logits = both[:, 128 * j : 128 * j + 128]
+    for ref, which in ((hw_ref, core), (hw_far_ref, 1 - core)):
+        for i in range(2):
+            w = ref[:, i * share : (i + 1) * share, :].reshape(parts * width, 128)
+            logits = jnp.dot(final, w, preferred_element_type=F32)
+            b = 2 * which + i
+            goal = jnp.where(which == 0, tgt_ref[:, i : i + 1], tgt_ref[:, 2 + i : 3 + i])
             g = jnp.max(logits, axis=-1, keepdims=True)
             s = jnp.sum(jnp.exp(logits - g), axis=-1, keepdims=True)
-            hit = lane + 128 * head == tgt_ref[:, b : b + 1]
-            picked = jnp.sum(jnp.where(hit, logits, 0.0), axis=-1, keepdims=True)
+            picked = jnp.where(lane + 128 * head == goal, logits, 0.0)
+            picked = jnp.sum(picked, axis=-1, keepdims=True)
             stats = jnp.where(lane == b, g, stats)
             stats = jnp.where(lane == books + b, s, stats)
             stats = jnp.where(lane == 2 * books + b, picked, stats)
     stat_ref[...] = stats
 
 
-def tail(place, att8, x8, hw, tgt, near, far):
+def tail(place, att8, x8, hw, hw_far, tgt, near, far):
     parts, rows, width = x8.shape
     return pl.pallas_call(
         tail_kernel,
@@ -284,17 +278,17 @@
             jax.ShapeDtypeStruct((rows, width), BF),
             jax.ShapeDtypeStruct((rows, 128), F32),
         ),
-        in_specs=[SMEM] + [VMEM] * 12,
+        in_specs=[SMEM] + [VMEM] * 13,
         out_specs=(VMEM, VMEM),
         scratch_shapes=[
             pltpu.VMEM((rows, parts * 128), BF),
             pltpu.VMEM((rows, parts * width), BF),
             pltpu.VMEM((rows, parts * width), BF),
         ],
-        compiler_params=PARAMS,
+        compiler_params=room(28),
         cost_estimate=SMALL,
         name="tail",
-    )(place, att8, x8, hw, tgt, *near, *far)
+    )(place, att8, x8, hw, hw_far, tgt, *near, *far)
 
 
 def loss_kernel(s_ref, out_ref):
@@ -334,9 +328,10 @@
     slot = z * 2 + c
     first = (y * 8 + slot) * rows
 
-    flat = heads_w.reshape(2, -1, heads_w.shape[-1])
-    rows_here = jnp.concatenate([flat[0], flat[1]], axis=1)
-    plane = trade(jnp.broadcast_to(rows_here[None], (8,) + rows_here.shape), ("z", "c"))
+    halves = heads_w.reshape(1, 2, -1, heads_w.shape[-1])
+    plane = trade(
+        jnp.broadcast_to(halves, (4,) + halves.shape[1:]).reshape((8,) + halves.shape[2:]), ("z", "c")
+    )
     devices = lax.axis_size(SEQ)
     behind = lax.ppermute(codes, SEQ, [(i, i + 1) for i in range(devices - 1)])
     w3 = jnp.transpose(wqkv, (1, 0, 2))
@@ -359,7 +354,7 @@
     )
     x_part = (summed + pos).astype(BF)
     x_part, plane = lax.optimization_barrier((x_part, plane))
-    hw = lax.all_gather(plane, "y", axis=0).reshape((-1,) + rows_here.shape)
+    hw = lax.all_gather(plane, "y", axis=0).reshape((-1,) + halves.shape[2:])
 
     other = flip(x_part, "h", 1)
     both = jnp.stack([jnp.where(h == 0, x_part, other), jnp.where(h == 0, other, x_part)])
@@ -369,23 +364,25 @@
     theirs = flip(mine, "h", 1)
 
     q, kv = project(x8, w3)
-    q8 = trade(q, "y")
+    q8 = trade(jnp.broadcast_to(q[None], (8,) + q.shape), "y")
     kv2 = jnp.stack([kv, flip(kv, "z", 2)])
     kv2 = after(kv2, theirs)
     kv4 = jnp.concatenate([kv2, flip(kv2, "z", 1)])
     kv4_far = flip(kv4, "c", 1)
     partial = attend(jnp.stack([y, slot]).astype(jnp.int32), q8, kv4, kv4_far)
-    pair = jnp.stack(after([mine, theirs], partial))
+    pair = jnp.stack([mine, theirs])
     near = [pair] + [shift(pair, "x", k) for k in (1, 2, 3)]
 
     att = merge(trade(partial, "y"))
     waits = [partial, att, att, att]
     far = [flip(after(n, first), "c", 1) for n, first in zip(near, waits)]
-    att8 = trade(att, HEAD)
+    hw = after(hw, partial)
+    hw_far = flip(hw, "c", 1)
+    att8 = trade(jnp.broadcast_to(att[None], (8,) + att.shape), HEAD)
 
     order = [((x - k) % 4) * 2 + (h ^ j) for k in range(4) for j in range(2)]
     place = jnp.stack([head, c] + order).astype(jnp.int32)
-    mixed, stats = tail(place, att8, x8, hw, jnp.transpose(targets), near, far)
+    mixed, stats = tail(place, att8, x8, hw, hw_far, jnp.transpose(targets), near, far)
     shares = trade(stats.reshape(8, rows // 8, 128), HEAD)
     return (mixed, final_loss(shares, books))
 

time: 184 us -> 185 us (level)
  starting transfers between devices: 72.3 us -> 78.3 us
  local copies, waits for them, and re-layouts: 6.67 us -> 12.5 us
  blocking collectives: 18.4 us -> 13.7 us
  waiting for transfers between devices: 39.9 us -> 36.6 us
  Pallas kernels: 25.2 us -> 23.1 us
    all_to_all x5, starting transfers between devices: 28.3 us -> 35.9 us  [trade(): return lax.all_to_all(array, axis, 0, 0, tiled=True)]
    all_to_all x1, blocking collectives: 18.4 us -> 13.7 us  [trade(): return lax.all_to_all(array, axis, 0, 0, tiled=True)]
    unnamed x10 -> x20, local copies, waits for them, and re-layouts: 2.28 us -> 6.47 us
    ppermute x3, waiting for transfers between devices: 4.71 us -> 1.79 us  [shift(): lax.ppermute(array, axis, [(i, (i + by) % size) for i in range(size)])]
    broadcast_in_dim x1 -> x3, local copies, waits for them, and re-layouts: 0.71 us -> 3.16 us  [the longest x1 1.43 us: shards(): jnp.broadcast_to(halves, (4,) + halves.shape[1:])]
    ppermute x9 -> x10, waiting for transfers between devices: 13.4 us -> 15.4 us  [flip(): return lax.ppermute(array, axis, [(i, i ^ by) for i in range(size)])]
    ppermute x9 -> x10, starting transfers between devices: 33.9 us -> 32.6 us  [flip(): return lax.ppermute(array, axis, [(i, i ^ by) for i in range(size)])]
  transfers between devices with their start and end apart: 19 -> 20, of which waited for: 8 -> 10; matrix products, arithmetic and copies ran while one was open for 6% -> 6% of each run, Pallas kernels for 10% -> 8%
where the time goes in v4:
time: 185 us; the launch traced here: 184 us
  starting transfers between devices  78.3 us (42%)
  waiting for transfers between devices  36.6 us (20%)
  Pallas kernels  23.1 us (12%)
  between operations  14.4 us (8%)
  blocking collectives  13.7 us (7%)
  local copies, waits for them, and re-layouts  12.5 us (7%)
  other arithmetic  4.63 us (3%)
    all_to_all x5, starting transfers between devices, trade(): return lax.all_to_all(array, axis, 0, 0, tiled=True)  35.9 us
    ppermute x10, starting transfers between devices, flip(): return lax.ppermute(array, axis, [(i, i ^ by) for i in range(size)])  32.6 us
    all_to_all x5, waiting for transfers between devices, trade(): return lax.all_to_all(array, axis, 0, 0, tiled=True)  19.4 us
    ppermute x10, waiting for transfers between devices, flip(): return lax.ppermute(array, axis, [(i, i ^ by) for i in range(size)])  15.4 us
    all_to_all x1, blocking collectives, trade(): return lax.all_to_all(array, axis, 0, 0, tiled=True)  13.7 us
    pallas_call x1, Pallas kernels, attend(): pl.pallas_call(attend_kernel, grid_spec=pltpu.PrefetchScalarGridSpec(num_...  12.5 us
    ppermute x3, starting transfers between devices, shift(): lax.ppermute(array, axis, [(i, (i + by) % size) for i in range(size)])  7.82 us
    unnamed x20, local copies, waits for them, and re-layouts  6.47 us
  transfers between devices with their start and end apart: 20, of which 10 were waited for; matrix products, arithmetic and copies ran while one was open for 6% of the time, Pallas kernels for 8%

profile of v4, /device:TPU:72, one launch (start us, length us, event | category | flops | bytes accessed | tf_op | source)
XLA Modules:
  0.0 184.1 jit_solution(7366212415689647103)
XLA Ops:
  7.2 0.0 copy-start
  7.2 2.1 %collective-permute-start = (s32[4,256]{1,0:T(4,128)}, s32[4,256]{1,0:T(4,128)S(1)}, u32[]{:S(2)}, u32[]{:S(2)}) collective-permute-start(s32[4,256]{1,0:T(4,128)} %param.7), channel_id=1, source_target_pairs={{0,8},{8,16},{16,24},{24,32},{32,40},{40,48},{48,56},{56,64},{64,7... | collective-permute-start | bytes 12296 | tf_op jit(solution)/shard_map/ppermute | solution.py:336
  9.2 1.4 broadcast_in_dim.82
  10.7 7.2 %all-to-all-start = ((bf16[8,64,128]{2,1,0:T(8,128)(2,1)}), bf16[8,64,128]{2,1,0:T(8,128)(2,1)S(1)}, u32[]{:S(2)}, u32[]{:S(2)}) async-start(bf16[8,64,128]{2,1,0:T(8,128)(2,1)} %bitcast.15), calls=%async_computation | async-start | bytes 262144 | tf_op jit(solution)/shard_map/all_to_all | solution.py:38
  17.9 0.7 broadcast_compare_fusion.3
  18.6 1.0 fusion.5
  19.6 0.0 collective-permute-done
  19.6 0.1 slice.16
  19.7 0.9 fusion.10
  20.6 0.9 fusion.4
  21.5 2.1 %all-to-all-done = bf16[8,64,128]{2,1,0:T(8,128)(2,1)S(1)} async-done(((bf16[8,64,128]{2,1,0:T(8,128)(2,1)}), bf16[8,64,128]{2,1,0:T(8,128)(2,1)S(1)}, u32[]{:S(2)}, u32[]{:S(2)}) %all-to-all-start) | async-done | bytes 131104 | tf_op jit(solution)/shard_map/all_to_all | solution.py:38
  23.5 9.2 %collective-permute-start.1 = (bf16[256,256]{1,0:T(8,128)(2,1)S(1)}, bf16[256,256]{1,0:T(8,128)(2,1)S(1)}, u32[]{:S(2)}, u32[]{:S(2)}) collective-permute-start(bf16[256,256]{1,0:T(8,128)(2,1)S(1)} %fusion.4), channel_id=1, source_target_pairs={{0,1},{1,0},{2,3},{3,2},{4,5},{5,4},{6,7},{7,6},{8,9},{9,8},{10,11... | collective-permute-start | bytes 393224 | tf_op jit(solution)/shard_map/ppermute | solution.py:29
  32.7 6.2 %collective-permute-done.1 = bf16[256,256]{1,0:T(8,128)(2,1)S(1)} collective-permute-done((bf16[256,256]{1,0:T(8,128)(2,1)S(1)}, bf16[256,256]{1,0:T(8,128)(2,1)S(1)}, u32[]{:S(2)}, u32[]{:S(2)}) %collective-permute-start.1) | collective-permute-done | bytes 131104 | tf_op jit(solution)/shard_map/ppermute | solution.py:29
  39.0 1.0 broadcast_in_dim.83
  40.1 4.3 %all-to-all-start.1 = ((bf16[4,2,256,256]{3,2,1,0:T(8,128)(2,1)}), bf16[4,2,256,256]{3,2,1,0:T(8,128)(2,1)S(1)}, u32[]{:S(2)}, u32[]{:S(2)}) async-start(bf16[4,2,256,256]{3,2,1,0:T(8,128)(2,1)} %broadcast_in_dim.83), calls=%async_computation.1 | async-start | bytes 2097152 | tf_op jit(solution)/shard_map/all_to_all | solution.py:38
  44.4 1.7 constant_dynamic-slice_fusion
  46.1 7.3 %collective-permute-start.3 = (bf16[128,1024]{1,0:T(8,128)(2,1)}, bf16[128,1024]{1,0:T(8,128)(2,1)}, u32[]{:S(2)}, u32[]{:S(2)}) collective-permute-start(bf16[128,1024]{1,0:T(8,128)(2,1)} %constant_dynamic-slice_fusion), channel_id=1, source_target_pairs={{0,1},{1,0},{2,3},{3,2},{4,5},{5,4},{6,7},{7,6},{8,9},{9,8},{10,11... | collective-permute-start | bytes 786440 | tf_op jit(solution)/shard_map/ppermute | solution.py:29
  53.4 5.6 %all-to-all-done.1 = bf16[4,2,256,256]{3,2,1,0:T(8,128)(2,1)S(1)} async-done(((bf16[4,2,256,256]{3,2,1,0:T(8,128)(2,1)}), bf16[4,2,256,256]{3,2,1,0:T(8,128)(2,1)S(1)}, u32[]{:S(2)}, u32[]{:S(2)}) %all-to-all-start.1) | async-done | bytes 1048608 | tf_op jit(solution)/shard_map/all_to_all | solution.py:38
  59.0 1.4 copy-done.1
  60.4 1.2 project.1
  61.7 1.9 %collective-permute-start.2 = (bf16[256,256]{1,0:T(8,128)(2,1)S(1)}, bf16[256,256]{1,0:T(8,128)(2,1)S(1)}, u32[]{:S(2)}, u32[]{:S(2)}) collective-permute-start(bf16[256,256]{1,0:T(8,128)(2,1)S(1)} %get-tuple-element.17), channel_id=1, source_target_pairs={{0,32},{16,48},{32,0},{48,16},{1,33},{17,49},{33,1},{49,17},{2,34}... | collective-permute-start | bytes 393224 | tf_op jit(solution)/shard_map/ppermute | solution.py:29
  63.6 0.0 all-gather.3.cloned.1.call-update
  63.6 0.9 broadcast_in_dim.84
  64.5 6.6 %all-to-all-start.2 = ((bf16[8,256,128]{2,1,0:T(8,128)(2,1)}), bf16[8,256,128]{2,1,0:T(8,128)(2,1)}, u32[]{:S(2)}, u32[]{:S(2)}) async-start(bf16[8,256,128]{2,1,0:T(8,128)(2,1)} %broadcast_in_dim.84), calls=%async_computation.2 | async-start | bytes 1048576 | tf_op jit(solution)/shard_map/all_to_all | solution.py:38
  71.1 0.0 collective-permute-done.2
  71.2 1.9 %collective-permute-start.4 = (bf16[2,256,256]{2,1,0:T(8,128)(2,1)S(1)}, bf16[2,256,256]{2,1,0:T(8,128)(2,1)S(1)}, u32[]{:S(2)}, u32[]{:S(2)}) collective-permute-start(bf16[2,256,256]{2,1,0:T(8,128)(2,1)S(1)} %pad_maximum_fusion.2), channel_id=1, source_target_pairs={{0,16},{16,0},{32,48},{48,32},{1,17},{17,1},{33,49},{49,33},{2,18}... | collective-permute-start | bytes 786440 | tf_op jit(solution)/shard_map/ppermute | solution.py:29
  73.1 6.3 %collective-permute-done.4 = bf16[2,256,256]{2,1,0:T(8,128)(2,1)S(1)} collective-permute-done((bf16[2,256,256]{2,1,0:T(8,128)(2,1)S(1)}, bf16[2,256,256]{2,1,0:T(8,128)(2,1)S(1)}, u32[]{:S(2)}, u32[]{:S(2)}) %collective-permute-start.4) | collective-permute-done | bytes 262176 | tf_op jit(solution)/shard_map/ppermute | solution.py:29
  79.5 1.9 %collective-permute-start.5 = (bf16[4,256,256]{2,1,0:T(8,128)(2,1)S(1)}, bf16[4,256,256]{2,1,0:T(8,128)(2,1)S(1)}, u32[]{:S(2)}, u32[]{:S(2)}) collective-permute-start(bf16[4,256,256]{2,1,0:T(8,128)(2,1)S(1)} %constant_dynamic-update-slice_fusion.near_ref), channel_id=1, source_target_pairs={{0,8},{8,0},{1,9},{9,1},{2,10},{10,2},{3,11},{11,3},{4,12},{12,4},... | collective-permute-start | bytes 1572872 | tf_op jit(solution)/shard_map/ppermute | solution.py:29
  81.4 0.8 copy-done.2
  82.2 0.1 pad_add_fusion.1.place_ref
  82.3 1.0 collective-permute-done.5.far_ref
  83.3 0.8 copy-done.5
  84.1 3.7 %all-to-all-done.2.q_ref = bf16[8,256,128]{2,1,0:T(8,128)(2,1)} async-done(((bf16[8,256,128]{2,1,0:T(8,128)(2,1)}), bf16[8,256,128]{2,1,0:T(8,128)(2,1)}, u32[]{:S(2)}, u32[]{:S(2)}) %all-to-all-start.2) | async-done | bytes 524320 | tf_op jit(solution)/shard_map/all_to_all | solution.py:38
  87.7 1.0 copy-done.3
  88.8 1.0 copy-done.6
  89.8 12.5 %attend.1 = bf16[8,272,128]{2,1,0:T(8,128)(2,1)} custom-call(s32[2]{0:T(128)S(1)} %pad_add_fusion.1.place_ref, bf16[8,256,128]{2,1,0:T(8,128)(2,1)} %all-to-all-done.2.q_ref, bf16[4,256,256]{2,1,0:T(8,128)(2,1)S(1)} %copy-done.3, bf16[4,256,256]{2,1,0:T(8,128)(2,1)S(1)} %copy-done.6), custom_call_target="tpu_custom_call" | custom-call | flops 1 | bytes 1 | tf_op jit(solution)/shard_map/attend/pallas_call | solution.py:179
  102.4 6.8 %all-to-all-start.3 = ((bf16[8,272,128]{2,1,0:T(8,128)(2,1)}), bf16[8,272,128]{2,1,0:T(8,128)(2,1)}, u32[]{:S(2)}, u32[]{:S(2)}) async-start(bf16[8,272,128]{2,1,0:T(8,128)(2,1)} %attend.1), calls=%async_computation.3 | async-start | bytes 1114112 | tf_op jit(solution)/shard_map/all_to_all | solution.py:38
  109.2 1.9 %pad_maximum_fusion.refs_0_ = bf16[2,128,1024]{2,1,0:T(8,128)(2,1)} fusion(bf16[1,128,1024]{2,1,0:T(8,128)(2,1)} %bitcast.24, bf16[1,128,1024]{2,1,0:T(8,128)(2,1)} %bitcast.23), kind=kLoop, calls=%fused_computation.6 | loop fusion | flops 262144 | bytes 1048576 | tf_op jit(solution)/shard_map/stack | solution.py:373
  111.0 2.9 %collective-permute-start.9 = (bf16[2,128,1024]{2,1,0:T(8,128)(2,1)}, bf16[2,128,1024]{2,1,0:T(8,128)(2,1)}, u32[]{:S(2)}, u32[]{:S(2)}) collective-permute-start(bf16[2,128,1024]{2,1,0:T(8,128)(2,1)} %pad_maximum_fusion.refs_0_), channel_id=1, source_target_pairs={{0,6},{2,0},{4,2},{6,4},{1,7},{3,1},{5,3},{7,5},{8,14},{10,8},{12,... | collective-permute-start | bytes 1572872 | tf_op jit(solution)/shard_map/ppermute | solution.py:34
  113.9 3.0 %collective-permute-start.8 = (bf16[2,128,1024]{2,1,0:T(8,128)(2,1)}, bf16[2,128,1024]{2,1,0:T(8,128)(2,1)}, u32[]{:S(2)}, u32[]{:S(2)}) collective-permute-start(bf16[2,128,1024]{2,1,0:T(8,128)(2,1)} %pad_maximum_fusion.refs_0_), channel_id=1, source_target_pairs={{0,4},{2,6},{4,0},{6,2},{1,5},{3,7},{5,1},{7,3},{8,12},{10,14},{12... | collective-permute-start | bytes 1572872 | tf_op jit(solution)/shard_map/ppermute | solution.py:34
  116.9 1.9 %collective-permute-start.7 = (bf16[2,128,1024]{2,1,0:T(8,128)(2,1)}, bf16[2,128,1024]{2,1,0:T(8,128)(2,1)}, u32[]{:S(2)}, u32[]{:S(2)}) collective-permute-start(bf16[2,128,1024]{2,1,0:T(8,128)(2,1)} %pad_maximum_fusion.refs_0_), channel_id=1, source_target_pairs={{0,2},{2,4},{4,6},{6,0},{1,3},{3,5},{5,7},{7,1},{8,10},{10,12},{12... | collective-permute-start | bytes 1572872 | tf_op jit(solution)/shard_map/ppermute | solution.py:34
  118.9 0.0 all-gather.3.cloned.1.call-done.hw_ref
  118.9 1.9 %collective-permute-start.6 = (bf16[64,64,128]{2,1,0:T(8,128)(2,1)}, bf16[64,64,128]{2,1,0:T(8,128)(2,1)}, u32[]{:S(2)}, u32[]{:S(2)}) collective-permute-start(bf16[64,64,128]{2,1,0:T(8,128)(2,1)} %all-gather.3.cloned.1.call-done.hw_ref), channel_id=1, source_target_pairs={{0,8},{8,0},{1,9},{9,1},{2,10},{10,2},{3,11},{11,3},{4,12},{12,4},... | collective-permute-start | bytes 3145736 | tf_op jit(solution)/shard_map/ppermute | solution.py:29
  120.8 0.1 all-to-all-done.3.o_ref
  120.9 1.8 merge.1
  122.7 0.9 broadcast_in_dim.85
  123.6 10.9 %all-to-all-start.4 = ((bf16[8,256,128]{2,1,0:T(8,128)(2,1)}), bf16[8,256,128]{2,1,0:T(8,128)(2,1)}, u32[]{:S(2)}, u32[]{:S(2)}) async-start(bf16[8,256,128]{2,1,0:T(8,128)(2,1)} %broadcast_in_dim.85), calls=%async_computation.4 | async-start | bytes 1048576 | tf_op jit(solution)/shard_map/all_to_all | solution.py:38
  134.5 2.1 %collective-permute-start.10 = (bf16[2,128,1024]{2,1,0:T(8,128)(2,1)}, bf16[2,128,1024]{2,1,0:T(8,128)(2,1)}, u32[]{:S(2)}, u32[]{:S(2)}) collective-permute-start(bf16[2,128,1024]{2,1,0:T(8,128)(2,1)} %pad_maximum_fusion.refs_0_), channel_id=1, source_target_pairs={{0,8},{8,0},{1,9},{9,1},{2,10},{10,2},{3,11},{11,3},{4,12},{12,4},... | collective-permute-start | bytes 1572872 | tf_op jit(solution)/shard_map/ppermute | solution.py:29
  136.7 0.0 collective-permute-done.9.refs_3_
  136.7 1.8 collective-permute-done.7.refs_1_
  138.5 1.9 %collective-permute-start.11 = (bf16[2,128,1024]{2,1,0:T(8,128)(2,1)}, bf16[2,128,1024]{2,1,0:T(8,128)(2,1)}, u32[]{:S(2)}, u32[]{:S(2)}) collective-permute-start(bf16[2,128,1024]{2,1,0:T(8,128)(2,1)} %collective-permute-done.7.refs_1_), channel_id=1, source_target_pairs={{0,8},{8,0},{1,9},{9,1},{2,10},{10,2},{3,11},{11,3},{4,12},{12,4},... | collective-permute-start | bytes 1572872 | tf_op jit(solution)/shard_map/ppermute | solution.py:29
  140.4 2.4 %collective-permute-start.12 = (bf16[2,128,1024]{2,1,0:T(8,128)(2,1)}, bf16[2,128,1024]{2,1,0:T(8,128)(2,1)}, u32[]{:S(2)}, u32[]{:S(2)}) collective-permute-start(bf16[2,128,1024]{2,1,0:T(8,128)(2,1)} %collective-permute-done.8.refs_2_), channel_id=1, source_target_pairs={{0,8},{8,0},{1,9},{9,1},{2,10},{10,2},{3,11},{11,3},{4,12},{12,4},... | collective-permute-start | bytes 1572872 | tf_op jit(solution)/shard_map/ppermute | solution.py:29
  142.8 1.9 %collective-permute-start.13 = (bf16[2,128,1024]{2,1,0:T(8,128)(2,1)}, bf16[2,128,1024]{2,1,0:T(8,128)(2,1)}, u32[]{:S(2)}, u32[]{:S(2)}) collective-permute-start(bf16[2,128,1024]{2,1,0:T(8,128)(2,1)} %collective-permute-done.9.refs_3_), channel_id=1, source_target_pairs={{0,8},{8,0},{1,9},{9,1},{2,10},{10,2},{3,11},{11,3},{4,12},{12,4},... | collective-permute-start | bytes 1572872 | tf_op jit(solution)/shard_map/ppermute | solution.py:29
  144.8 0.1 copy.10
  144.9 0.1 stack.79.place_ref
  145.0 0.0 collective-permute-done.10.refs_4_
  145.1 0.0 collective-permute-done.11.refs_5_
  145.1 0.0 collective-permute-done.12.refs_6_
  145.1 1.9 %collective-permute-done.13.refs_7_ = bf16[2,128,1024]{2,1,0:T(8,128)(2,1)} collective-permute-done((bf16[2,128,1024]{2,1,0:T(8,128)(2,1)}, bf16[2,128,1024]{2,1,0:T(8,128)(2,1)}, u32[]{:S(2)}, u32[]{:S(2)}) %collective-permute-start.13) | collective-permute-done | bytes 524320 | tf_op jit(solution)/shard_map/ppermute | solution.py:29
  146.9 8.0 %all-to-all-done.4.att_ref = bf16[8,256,128]{2,1,0:T(8,128)(2,1)} async-done(((bf16[8,256,128]{2,1,0:T(8,128)(2,1)}), bf16[8,256,128]{2,1,0:T(8,128)(2,1)}, u32[]{:S(2)}, u32[]{:S(2)}) %all-to-all-start.4) | async-done | bytes 524320 | tf_op jit(solution)/shard_map/all_to_all | solution.py:38
  154.9 1.2 copy-done.4
  156.1 5.8 %tail.1 = (bf16[256,256]{1,0:T(8,128)(2,1)}, f32[256,128]{1,0:T(8,128)S(1)}) custom-call(s32[10]{0:T(128)S(1)} %stack.79.place_ref, bf16[8,256,128]{2,1,0:T(8,128)(2,1)} %all-to-all-done.4.att_ref, bf16[8,256,256]{2,1,0:T(8,128)(2,1)S(1)} %bitcast.36, bf16[64,64,128]{2,1,0:T(8,128)(2,1)S(1)} %copy-done.4, ...), custom_call_target="tpu_custom_call" | custom-call | flops 1 | bytes 1 | tf_op jit(solution)/shard_map/tail/pallas_call | solution.py:275
  162.0 13.7 %all_to_all.30.s_ref = f32[8,32,128]{2,1,0:T(8,128)} all-to-all(f32[8,32,128]{2,1,0:T(8,128)S(1)} %bitcast.39), channel_id=1, replica_groups=mesh['y'=8,'z'=4,'c'=2,'x'=4,'h'=2] {'x','h'}, dimensions={0} | all-to-all | bytes 262144 | tf_op jit(solution)/shard_map/all_to_all | solution.py:38
  175.6 1.7 loss.1
  (24 shorter events, 0.2 us)
Async XLA Ops:
  7.2 13.4 %copy-start = (bf16[4,1024,256]{2,1,0:T(8,128)(2,1)S(1)}, bf16[4,1024,256]{2,1,0:T(8,128)(2,1)}, u32[]{:S(2)}) copy-start(bf16[4,1024,256]{2,1,0:T(8,128)(2,1)} %param.10) | copy-start | bytes 6291460
  7.2 12.4 %collective-permute-start = (s32[4,256]{1,0:T(4,128)}, s32[4,256]{1,0:T(4,128)S(1)}, u32[]{:S(2)}, u32[]{:S(2)}) collective-permute-start(s32[4,256]{1,0:T(4,128)} %param.7), channel_id=1, source_target_pairs={{0,8},{8,16},{16,24},{24,32},{32,40},{40,48},{48,56},{56,64},{64,7... | collective-permute-start | bytes 12296 | tf_op jit(solution)/shard_map/ppermute | solution.py:336
  10.7 12.9 %all-to-all-start = ((bf16[8,64,128]{2,1,0:T(8,128)(2,1)}), bf16[8,64,128]{2,1,0:T(8,128)(2,1)S(1)}, u32[]{:S(2)}, u32[]{:S(2)}) async-start(bf16[8,64,128]{2,1,0:T(8,128)(2,1)} %bitcast.15), calls=%async_computation | async-start | bytes 262144 | tf_op jit(solution)/shard_map/all_to_all | solution.py:38
  23.5 16.6 %copy-start.7 = (bf16[8,64,128]{2,1,0:T(8,128)(2,1)}, bf16[8,64,128]{2,1,0:T(8,128)(2,1)S(1)}, u32[]{:S(2)}) copy-start(bf16[8,64,128]{2,1,0:T(8,128)(2,1)S(1)} %all-to-all-done) | copy-start | bytes 393220
  23.5 15.4 %collective-permute-start.1 = (bf16[256,256]{1,0:T(8,128)(2,1)S(1)}, bf16[256,256]{1,0:T(8,128)(2,1)S(1)}, u32[]{:S(2)}, u32[]{:S(2)}) collective-permute-start(bf16[256,256]{1,0:T(8,128)(2,1)S(1)} %fusion.4), channel_id=1, source_target_pairs={{0,1},{1,0},{2,3},{3,2},{4,5},{5,4},{6,7},{7,6},{8,9},{9,8},{10,11... | collective-permute-start | bytes 393224 | tf_op jit(solution)/shard_map/ppermute | solution.py:29
  40.1 18.9 %all-to-all-start.1 = ((bf16[4,2,256,256]{3,2,1,0:T(8,128)(2,1)}), bf16[4,2,256,256]{3,2,1,0:T(8,128)(2,1)S(1)}, u32[]{:S(2)}, u32[]{:S(2)}) async-start(bf16[4,2,256,256]{3,2,1,0:T(8,128)(2,1)} %broadcast_in_dim.83), calls=%async_computation.1 | async-start | bytes 2097152 | tf_op jit(solution)/shard_map/all_to_all | solution.py:38
  44.4 74.5 %all-gather.3.cloned.1.call-start = ((), (), s32[]{:S(2)}) async-start(), calls=%async_computation.6 | async-start | bytes 1179648 | tf_op jit(solution)/shard_map/all_gather | solution.py:357
  46.1 25.1 %collective-permute-start.3 = (bf16[128,1024]{1,0:T(8,128)(2,1)}, bf16[128,1024]{1,0:T(8,128)(2,1)}, u32[]{:S(2)}, u32[]{:S(2)}) collective-permute-start(bf16[128,1024]{1,0:T(8,128)(2,1)} %constant_dynamic-slice_fusion), channel_id=1, source_target_pairs={{0,1},{1,0},{2,3},{3,2},{4,5},{5,4},{6,7},{7,6},{8,9},{9,8},{10,11... | collective-permute-start | bytes 786440 | tf_op jit(solution)/shard_map/ppermute | solution.py:29
  59.0 1.4 copy-start.1
  61.7 9.5 %collective-permute-start.2 = (bf16[256,256]{1,0:T(8,128)(2,1)S(1)}, bf16[256,256]{1,0:T(8,128)(2,1)S(1)}, u32[]{:S(2)}, u32[]{:S(2)}) collective-permute-start(bf16[256,256]{1,0:T(8,128)(2,1)S(1)} %get-tuple-element.17), channel_id=1, source_target_pairs={{0,32},{16,48},{32,0},{48,16},{1,33},{17,49},{33,1},{49,17},{2,34}... | collective-permute-start | bytes 393224 | tf_op jit(solution)/shard_map/ppermute | solution.py:29
  64.5 23.2 %all-to-all-start.2 = ((bf16[8,256,128]{2,1,0:T(8,128)(2,1)}), bf16[8,256,128]{2,1,0:T(8,128)(2,1)}, u32[]{:S(2)}, u32[]{:S(2)}) async-start(bf16[8,256,128]{2,1,0:T(8,128)(2,1)} %broadcast_in_dim.84), calls=%async_computation.2 | async-start | bytes 1048576 | tf_op jit(solution)/shard_map/all_to_all | solution.py:38
  71.2 8.3 %collective-permute-start.4 = (bf16[2,256,256]{2,1,0:T(8,128)(2,1)S(1)}, bf16[2,256,256]{2,1,0:T(8,128)(2,1)S(1)}, u32[]{:S(2)}, u32[]{:S(2)}) collective-permute-start(bf16[2,256,256]{2,1,0:T(8,128)(2,1)S(1)} %pad_maximum_fusion.2), channel_id=1, source_target_pairs={{0,16},{16,0},{32,48},{48,32},{1,17},{17,1},{33,49},{49,33},{2,18}... | collective-permute-start | bytes 786440 | tf_op jit(solution)/shard_map/ppermute | solution.py:29
  79.5 3.8 %collective-permute-start.5 = (bf16[4,256,256]{2,1,0:T(8,128)(2,1)S(1)}, bf16[4,256,256]{2,1,0:T(8,128)(2,1)S(1)}, u32[]{:S(2)}, u32[]{:S(2)}) collective-permute-start(bf16[4,256,256]{2,1,0:T(8,128)(2,1)S(1)} %constant_dynamic-update-slice_fusion.near_ref), channel_id=1, source_target_pairs={{0,8},{8,0},{1,9},{9,1},{2,10},{10,2},{3,11},{11,3},{4,12},{12,4},... | collective-permute-start | bytes 1572872 | tf_op jit(solution)/shard_map/ppermute | solution.py:29
  81.4 0.8 copy-start.2
  83.3 0.8 copy-start.5
  87.7 1.0 copy-start.3
  88.8 1.0 copy-start.6
  102.3 42.5 %copy-start.8 = (s32[4,256]{1,0:T(4,128)S(1)}, s32[4,256]{1,0:T(4,128)}, u32[]{:S(2)}) copy-start(s32[4,256]{1,0:T(4,128)} %param.9) | copy-start | bytes 12292
  102.4 18.5 %all-to-all-start.3 = ((bf16[8,272,128]{2,1,0:T(8,128)(2,1)}), bf16[8,272,128]{2,1,0:T(8,128)(2,1)}, u32[]{:S(2)}, u32[]{:S(2)}) async-start(bf16[8,272,128]{2,1,0:T(8,128)(2,1)} %attend.1), calls=%async_computation.3 | async-start | bytes 1114112 | tf_op jit(solution)/shard_map/all_to_all | solution.py:38
  111.0 25.6 %collective-permute-start.9 = (bf16[2,128,1024]{2,1,0:T(8,128)(2,1)}, bf16[2,128,1024]{2,1,0:T(8,128)(2,1)}, u32[]{:S(2)}, u32[]{:S(2)}) collective-permute-start(bf16[2,128,1024]{2,1,0:T(8,128)(2,1)} %pad_maximum_fusion.refs_0_), channel_id=1, source_target_pairs={{0,6},{2,0},{4,2},{6,4},{1,7},{3,1},{5,3},{7,5},{8,14},{10,8},{12,... | collective-permute-start | bytes 1572872 | tf_op jit(solution)/shard_map/ppermute | solution.py:34
  113.9 22.8 %collective-permute-start.8 = (bf16[2,128,1024]{2,1,0:T(8,128)(2,1)}, bf16[2,128,1024]{2,1,0:T(8,128)(2,1)}, u32[]{:S(2)}, u32[]{:S(2)}) collective-permute-start(bf16[2,128,1024]{2,1,0:T(8,128)(2,1)} %pad_maximum_fusion.refs_0_), channel_id=1, source_target_pairs={{0,4},{2,6},{4,0},{6,2},{1,5},{3,7},{5,1},{7,3},{8,12},{10,14},{12... | collective-permute-start | bytes 1572872 | tf_op jit(solution)/shard_map/ppermute | solution.py:34
  116.9 21.5 %collective-permute-start.7 = (bf16[2,128,1024]{2,1,0:T(8,128)(2,1)}, bf16[2,128,1024]{2,1,0:T(8,128)(2,1)}, u32[]{:S(2)}, u32[]{:S(2)}) collective-permute-start(bf16[2,128,1024]{2,1,0:T(8,128)(2,1)} %pad_maximum_fusion.refs_0_), channel_id=1, source_target_pairs={{0,2},{2,4},{4,6},{6,0},{1,3},{3,5},{5,7},{7,1},{8,10},{10,12},{12... | collective-permute-start | bytes 1572872 | tf_op jit(solution)/shard_map/ppermute | solution.py:34
  118.9 26.1 %collective-permute-start.6 = (bf16[64,64,128]{2,1,0:T(8,128)(2,1)}, bf16[64,64,128]{2,1,0:T(8,128)(2,1)}, u32[]{:S(2)}, u32[]{:S(2)}) collective-permute-start(bf16[64,64,128]{2,1,0:T(8,128)(2,1)} %all-gather.3.cloned.1.call-done.hw_ref), channel_id=1, source_target_pairs={{0,8},{8,0},{1,9},{9,1},{2,10},{10,2},{3,11},{11,3},{4,12},{12,4},... | collective-permute-start | bytes 3145736 | tf_op jit(solution)/shard_map/ppermute | solution.py:29
  123.6 31.3 %all-to-all-start.4 = ((bf16[8,256,128]{2,1,0:T(8,128)(2,1)}), bf16[8,256,128]{2,1,0:T(8,128)(2,1)}, u32[]{:S(2)}, u32[]{:S(2)}) async-start(bf16[8,256,128]{2,1,0:T(8,128)(2,1)} %broadcast_in_dim.85), calls=%async_computation.4 | async-start | bytes 1048576 | tf_op jit(solution)/shard_map/all_to_all | solution.py:38
  134.5 10.5 %collective-permute-start.10 = (bf16[2,128,1024]{2,1,0:T(8,128)(2,1)}, bf16[2,128,1024]{2,1,0:T(8,128)(2,1)}, u32[]{:S(2)}, u32[]{:S(2)}) collective-permute-start(bf16[2,128,1024]{2,1,0:T(8,128)(2,1)} %pad_maximum_fusion.refs_0_), channel_id=1, source_target_pairs={{0,8},{8,0},{1,9},{9,1},{2,10},{10,2},{3,11},{11,3},{4,12},{12,4},... | collective-permute-start | bytes 1572872 | tf_op jit(solution)/shard_map/ppermute | solution.py:29
  138.5 6.6 %collective-permute-start.11 = (bf16[2,128,1024]{2,1,0:T(8,128)(2,1)}, bf16[2,128,1024]{2,1,0:T(8,128)(2,1)}, u32[]{:S(2)}, u32[]{:S(2)}) collective-permute-start(bf16[2,128,1024]{2,1,0:T(8,128)(2,1)} %collective-permute-done.7.refs_1_), channel_id=1, source_target_pairs={{0,8},{8,0},{1,9},{9,1},{2,10},{10,2},{3,11},{11,3},{4,12},{12,4},... | collective-permute-start | bytes 1572872 | tf_op jit(solution)/shard_map/ppermute | solution.py:29
  140.4 4.7 %collective-permute-start.12 = (bf16[2,128,1024]{2,1,0:T(8,128)(2,1)}, bf16[2,128,1024]{2,1,0:T(8,128)(2,1)}, u32[]{:S(2)}, u32[]{:S(2)}) collective-permute-start(bf16[2,128,1024]{2,1,0:T(8,128)(2,1)} %collective-permute-done.8.refs_2_), channel_id=1, source_target_pairs={{0,8},{8,0},{1,9},{9,1},{2,10},{10,2},{3,11},{11,3},{4,12},{12,4},... | collective-permute-start | bytes 1572872 | tf_op jit(solution)/shard_map/ppermute | solution.py:29
  142.8 4.1 %collective-permute-start.13 = (bf16[2,128,1024]{2,1,0:T(8,128)(2,1)}, bf16[2,128,1024]{2,1,0:T(8,128)(2,1)}, u32[]{:S(2)}, u32[]{:S(2)}) collective-permute-start(bf16[2,128,1024]{2,1,0:T(8,128)(2,1)} %collective-permute-done.9.refs_3_), channel_id=1, source_target_pairs={{0,8},{8,0},{1,9},{9,1},{2,10},{10,2},{3,11},{11,3},{4,12},{12,4},... | collective-permute-start | bytes 1572872 | tf_op jit(solution)/shard_map/ppermute | solution.py:29
  154.9 1.2 copy-start.4
Sparse Core Ops, SparseCore 0:
  63.7 41.4 all-gather.2

commit v5 on v3

--- a/solution.py
+++ b/solution.py
@@ -46,44 +46,36 @@
     return jnp.where(columns[None, :] < half, jnp.sin(angle), jnp.cos(angle))
 
 
-def project_kernel(x_ref, w_ref, q_ref, kv_ref, w_s, n_s, sem):
-    load = pltpu.make_async_copy(w_ref, w_s, sem)
-    load.start()
+def project_kernel(x_ref, w_ref, q_ref, kv_ref):
     parts, _, width = x_ref.shape
     squares = 0.0
     for i in range(parts):
         xi = x_ref[i].astype(F32)
         squares = squares + jnp.sum(xi * xi, axis=-1, keepdims=True)
     r = lax.rsqrt(squares / (parts * width) + 1e-05)
+    sums = [0.0, 0.0, 0.0]
     for i in range(parts):
-        n_s[:, i * width : (i + 1) * width] = (x_ref[i].astype(F32) * r).astype(BF)
-    load.wait()
-    n = n_s[...]
-    q = jnp.dot(n, w_s[0], preferred_element_type=F32).astype(BF)
-    for i in range(q_ref.shape[0]):
-        q_ref[i] = q
-    for j in range(2):
-        kv = jnp.dot(n, w_s[1 + j], preferred_element_type=F32)
-        kv_ref[:, 128 * j : 128 * j + 128] = kv.astype(BF)
+        ni = (x_ref[i].astype(F32) * r).astype(BF)
+        for j in range(3):
+            sums[j] = sums[j] + jnp.dot(
+                ni, w_ref[j, i * width : (i + 1) * width, :], preferred_element_type=F32
+            )
+    q_ref[...] = sums[0].astype(BF)
+    kv_ref[:, :128] = sums[1].astype(BF)
+    kv_ref[:, 128:] = sums[2].astype(BF)
 
 
 def project(x8, w):
-    parts, rows, width = x8.shape
+    rows = x8.shape[1]
     return pl.pallas_call(
         project_kernel,
         out_shape=(
-            pltpu.HBM((8, rows, 128), BF),
+            jax.ShapeDtypeStruct((rows, 128), BF),
             jax.ShapeDtypeStruct((rows, 256), BF),
         ),
-        in_specs=[VMEM, HBM],
+        in_specs=[VMEM, VMEM],
         out_specs=(VMEM, VMEM),
-        scratch_shapes=[
-            pltpu.VMEM(w.shape, BF),
-            pltpu.VMEM((rows, parts * width), BF),
-            pltpu.SemaphoreType.DMA,
-        ],
         compiler_params=PARAMS,
-        cost_estimate=SMALL,
         name="project",
     )(x8, w)
 
@@ -179,7 +171,7 @@
 
 def attend(place, q8, near, far):
     planes, rows, _ = q8.shape
-    each = 2
+    each = 4
     whole = pl.BlockSpec(near.shape, lambda i, s: (0, 0, 0))
     return pl.pallas_call(
         attend_kernel,
@@ -369,17 +361,17 @@
     theirs = flip(mine, "h", 1)
 
     q, kv = project(x8, w3)
-    q8 = trade(q, "y")
+    q8 = trade(jnp.broadcast_to(q[None], (8,) + q.shape), "y")
     kv2 = jnp.stack([kv, flip(kv, "z", 2)])
     kv2 = after(kv2, theirs)
     kv4 = jnp.concatenate([kv2, flip(kv2, "z", 1)])
     kv4_far = flip(kv4, "c", 1)
     partial = attend(jnp.stack([y, slot]).astype(jnp.int32), q8, kv4, kv4_far)
-    pair = jnp.stack(after([mine, theirs], partial))
+    pair = jnp.stack(after([mine, theirs], q8))
     near = [pair] + [shift(pair, "x", k) for k in (1, 2, 3)]
 
     att = merge(trade(partial, "y"))
-    waits = [partial, att, att, att]
+    waits = [partial] * 4
     far = [flip(after(n, first), "c", 1) for n, first in zip(near, waits)]
     att8 = trade(att, HEAD)
 

time: 184 us -> 184 us (level)
  waiting for transfers between devices: 39.9 us -> 37.7 us
  starting transfers between devices: 72.3 us -> 74.2 us
    all_to_all x5, starting transfers between devices: 28.3 us -> 30.5 us  [trade(): return lax.all_to_all(array, axis, 0, 0, tiled=True)]
  transfers between devices with their start and end apart: 19 -> 19, of which waited for: 8 -> 9; matrix products, arithmetic and copies ran while one was open for 6% -> 6% of each run, Pallas kernels for 10% -> 9%
where the time goes in v5:
time: 184 us; the launch traced here: 183 us
  starting transfers between devices  74.2 us (40%)
  waiting for transfers between devices  37.7 us (20%)
  Pallas kernels  24.2 us (13%)
  blocking collectives  18.7 us (10%)
  between operations  14.4 us (8%)
  local copies, waits for them, and re-layouts  7.54 us (4%)
  other arithmetic  5.46 us (3%)
    ppermute x9, starting transfers between devices, flip(): return lax.ppermute(array, axis, [(i, i ^ by) for i in range(size)])  33.5 us
    all_to_all x5, starting transfers between devices, trade(): return lax.all_to_all(array, axis, 0, 0, tiled=True)  30.5 us
    all_to_all x5, waiting for transfers between devices, trade(): return lax.all_to_all(array, axis, 0, 0, tiled=True)  19.7 us
    all_to_all x1, blocking collectives, trade(): return lax.all_to_all(array, axis, 0, 0, tiled=True)  18.7 us
    ppermute x9, waiting for transfers between devices, flip(): return lax.ppermute(array, axis, [(i, i ^ by) for i in range(size)])  13.6 us
    pallas_call x1, Pallas kernels, attend(): pl.pallas_call(attend_kernel, grid_spec=pltpu.PrefetchScalarGridSpec(num_...  12.9 us
    ppermute x3, starting transfers between devices, shift(): lax.ppermute(array, axis, [(i, (i + by) % size) for i in range(size)])  8.16 us
    pallas_call x1, Pallas kernels, tail(): pl.pallas_call(tail_kernel, out_shape=(jax.ShapeDtypeStruct((rows, width)...  5.72 us
  transfers between devices with their start and end apart: 19, of which 9 were waited for; matrix products, arithmetic and copies ran while one was open for 6% of the time, Pallas kernels for 9%

profile of v5, /device:TPU:72, one launch (start us, length us, event | category | flops | bytes accessed | tf_op | source)
XLA Modules:
  0.0 183.1 jit_solution(4430188266449845425)
XLA Ops:
  7.2 0.0 copy-start
  7.2 2.1 %collective-permute-start = (s32[4,256]{1,0:T(4,128)}, s32[4,256]{1,0:T(4,128)S(1)}, u32[]{:S(2)}, u32[]{:S(2)}) collective-permute-start(s32[4,256]{1,0:T(4,128)} %param.7), channel_id=1, source_target_pairs={{0,8},{8,16},{16,24},{24,32},{32,40},{40,48},{48,56},{56,64},{64,7... | collective-permute-start | bytes 12296 | tf_op jit(solution)/shard_map/ppermute | solution.py:333
  9.2 0.7 fusion.19
  10.0 0.7 broadcast_in_dim.74
  10.7 7.2 %all-to-all-start = ((bf16[8,64,256]{2,1,0:T(8,128)(2,1)}), bf16[8,64,256]{2,1,0:T(8,128)(2,1)S(1)}, u32[]{:S(2)}, u32[]{:S(2)}) async-start(bf16[8,64,256]{2,1,0:T(8,128)(2,1)} %broadcast_in_dim.74), calls=%async_computation | async-start | bytes 524288 | tf_op jit(solution)/shard_map/all_to_all | solution.py:35
  17.9 0.7 broadcast_compare_fusion.3
  18.6 1.0 fusion.5
  19.6 0.0 collective-permute-done
  19.6 0.1 slice.26
  19.7 0.9 fusion.10
  20.6 0.0 copy-done
  20.6 0.9 fusion.4
  21.5 4.3 %all-to-all-done = bf16[8,64,256]{2,1,0:T(8,128)(2,1)S(1)} async-done(((bf16[8,64,256]{2,1,0:T(8,128)(2,1)}), bf16[8,64,256]{2,1,0:T(8,128)(2,1)S(1)}, u32[]{:S(2)}, u32[]{:S(2)}) %all-to-all-start) | async-done | bytes 262176 | tf_op jit(solution)/shard_map/all_to_all | solution.py:35
  25.8 9.2 %collective-permute-start.1 = (bf16[256,256]{1,0:T(8,128)(2,1)S(1)}, bf16[256,256]{1,0:T(8,128)(2,1)S(1)}, u32[]{:S(2)}, u32[]{:S(2)}) collective-permute-start(bf16[256,256]{1,0:T(8,128)(2,1)S(1)} %fusion.4), channel_id=1, source_target_pairs={{0,1},{1,0},{2,3},{3,2},{4,5},{5,4},{6,7},{7,6},{8,9},{9,8},{10,11... | collective-permute-start | bytes 393224 | tf_op jit(solution)/shard_map/ppermute | solution.py:26
  35.0 6.1 %collective-permute-done.1 = bf16[256,256]{1,0:T(8,128)(2,1)S(1)} collective-permute-done((bf16[256,256]{1,0:T(8,128)(2,1)S(1)}, bf16[256,256]{1,0:T(8,128)(2,1)S(1)}, u32[]{:S(2)}, u32[]{:S(2)}) %collective-permute-start.1) | collective-permute-done | bytes 131104 | tf_op jit(solution)/shard_map/ppermute | solution.py:26
  41.1 1.1 broadcast_in_dim.75
  42.2 4.3 %all-to-all-start.1 = ((bf16[4,2,256,256]{3,2,1,0:T(8,128)(2,1)}), bf16[4,2,256,256]{3,2,1,0:T(8,128)(2,1)S(1)}, u32[]{:S(2)}, u32[]{:S(2)}) async-start(bf16[4,2,256,256]{3,2,1,0:T(8,128)(2,1)} %broadcast_in_dim.75), calls=%async_computation.1 | async-start | bytes 2097152 | tf_op jit(solution)/shard_map/all_to_all | solution.py:35
  46.5 0.7 all-gather.3.cloned.1.call-update
  47.2 1.0 constant_dynamic-slice_fusion
  48.2 7.5 %collective-permute-start.3 = (bf16[128,1024]{1,0:T(8,128)(2,1)S(1)}, bf16[128,1024]{1,0:T(8,128)(2,1)}, u32[]{:S(2)}, u32[]{:S(2)}) collective-permute-start(bf16[128,1024]{1,0:T(8,128)(2,1)S(1)} %constant_dynamic-slice_fusion), channel_id=1, source_target_pairs={{0,1},{1,0},{2,3},{3,2},{4,5},{5,4},{6,7},{7,6},{8,9},{9,8},{10,11... | collective-permute-start | bytes 786440 | tf_op jit(solution)/shard_map/ppermute | solution.py:26
  55.7 2.0 %all-to-all-done.1 = bf16[4,2,256,256]{3,2,1,0:T(8,128)(2,1)S(1)} async-done(((bf16[4,2,256,256]{3,2,1,0:T(8,128)(2,1)}), bf16[4,2,256,256]{3,2,1,0:T(8,128)(2,1)S(1)}, u32[]{:S(2)}, u32[]{:S(2)}) %all-to-all-start.1) | async-done | bytes 1048608 | tf_op jit(solution)/shard_map/all_to_all | solution.py:35
  57.6 1.4 copy-done.1
  59.0 1.2 project.1
  60.3 4.8 %collective-permute-start.2 = (bf16[256,256]{1,0:T(8,128)(2,1)S(1)}, bf16[256,256]{1,0:T(8,128)(2,1)}, u32[]{:S(2)}, u32[]{:S(2)}) collective-permute-start(bf16[256,256]{1,0:T(8,128)(2,1)S(1)} %get-tuple-element.18), channel_id=1, source_target_pairs={{0,32},{16,48},{32,0},{48,16},{1,33},{17,49},{33,1},{49,17},{2,34}... | collective-permute-start | bytes 393224 | tf_op jit(solution)/shard_map/ppermute | solution.py:26
  65.2 0.9 broadcast_in_dim.76
  66.0 6.6 %all-to-all-start.2 = ((bf16[8,256,128]{2,1,0:T(8,128)(2,1)}), bf16[8,256,128]{2,1,0:T(8,128)(2,1)}, u32[]{:S(2)}, u32[]{:S(2)}) async-start(bf16[8,256,128]{2,1,0:T(8,128)(2,1)} %broadcast_in_dim.76), calls=%async_computation.2 | async-start | bytes 1048576 | tf_op jit(solution)/shard_map/all_to_all | solution.py:35
  72.7 0.0 collective-permute-done.2
  72.7 0.9 pad_maximum_fusion.2
  73.6 0.0 collective-permute-done.3
  73.6 1.9 %collective-permute-start.4 = (bf16[2,256,256]{2,1,0:T(8,128)(2,1)S(1)}, bf16[2,256,256]{2,1,0:T(8,128)(2,1)S(1)}, u32[]{:S(2)}, u32[]{:S(2)}) collective-permute-start(bf16[2,256,256]{2,1,0:T(8,128)(2,1)S(1)} %pad_maximum_fusion.2), channel_id=1, source_target_pairs={{0,16},{16,0},{32,48},{48,32},{1,17},{17,1},{33,49},{49,33},{2,18}... | collective-permute-start | bytes 786440 | tf_op jit(solution)/shard_map/ppermute | solution.py:26
  75.5 0.7 constant_dynamic-update-slice_fusion.1
  76.3 5.6 %collective-permute-done.4 = bf16[2,256,256]{2,1,0:T(8,128)(2,1)S(1)} collective-permute-done((bf16[2,256,256]{2,1,0:T(8,128)(2,1)S(1)}, bf16[2,256,256]{2,1,0:T(8,128)(2,1)S(1)}, u32[]{:S(2)}, u32[]{:S(2)}) %collective-permute-start.4) | collective-permute-done | bytes 262176 | tf_op jit(solution)/shard_map/ppermute | solution.py:26
  81.9 0.7 constant_dynamic-update-slice_fusion.near_ref
  82.6 1.9 %collective-permute-start.5 = (bf16[4,256,256]{2,1,0:T(8,128)(2,1)}, bf16[4,256,256]{2,1,0:T(8,128)(2,1)}, u32[]{:S(2)}, u32[]{:S(2)}) collective-permute-start(bf16[4,256,256]{2,1,0:T(8,128)(2,1)} %constant_dynamic-update-slice_fusion.near_ref), channel_id=1, source_target_pairs={{0,8},{8,0},{1,9},{9,1},{2,10},{10,2},{3,11},{11,3},{4,12},{12,4},... | collective-permute-start | bytes 1572872 | tf_op jit(solution)/shard_map/ppermute | solution.py:26
  84.5 0.1 pad_add_fusion.1.place_ref
  84.6 9.7 %all-to-all-done.2.q_ref = bf16[8,256,128]{2,1,0:T(8,128)(2,1)} async-done(((bf16[8,256,128]{2,1,0:T(8,128)(2,1)}), bf16[8,256,128]{2,1,0:T(8,128)(2,1)}, u32[]{:S(2)}, u32[]{:S(2)}) %all-to-all-start.2) | async-done | bytes 524320 | tf_op jit(solution)/shard_map/all_to_all | solution.py:35
  94.3 0.0 collective-permute-done.5.far_ref
  94.3 12.9 %attend.1 = bf16[8,272,128]{2,1,0:T(8,128)(2,1)} custom-call(s32[2]{0:T(128)S(1)} %pad_add_fusion.1.place_ref, bf16[8,256,128]{2,1,0:T(8,128)(2,1)} %all-to-all-done.2.q_ref, bf16[4,256,256]{2,1,0:T(8,128)(2,1)} %constant_dynamic-update-slice_fusion.near_ref, bf16[4,256,256]{2,1,0:T(8,128)(2,1)} %collective-permute-done.5.far_ref), custom_call_target="tpu_custom_call" | custom-call | flops 1 | bytes 1 | tf_op jit(solution)/shard_map/attend/pallas_call | solution.py:176
  107.2 5.8 %all-to-all-start.3 = ((bf16[8,272,128]{2,1,0:T(8,128)(2,1)}), bf16[8,272,128]{2,1,0:T(8,128)(2,1)}, u32[]{:S(2)}, u32[]{:S(2)}) async-start(bf16[8,272,128]{2,1,0:T(8,128)(2,1)} %attend.1), calls=%async_computation.3 | async-start | bytes 1114112 | tf_op jit(solution)/shard_map/all_to_all | solution.py:35
  113.0 1.8 pad_maximum_fusion.refs_0_
  114.8 3.2 %collective-permute-start.8 = (bf16[2,128,1024]{2,1,0:T(8,128)(2,1)}, bf16[2,128,1024]{2,1,0:T(8,128)(2,1)}, u32[]{:S(2)}, u32[]{:S(2)}) collective-permute-start(bf16[2,128,1024]{2,1,0:T(8,128)(2,1)} %pad_maximum_fusion.refs_0_), channel_id=1, source_target_pairs={{0,6},{2,0},{4,2},{6,4},{1,7},{3,1},{5,3},{7,5},{8,14},{10,8},{12,... | collective-permute-start | bytes 1572872 | tf_op jit(solution)/shard_map/ppermute | solution.py:31
  118.1 3.0 %collective-permute-start.7 = (bf16[2,128,1024]{2,1,0:T(8,128)(2,1)}, bf16[2,128,1024]{2,1,0:T(8,128)(2,1)}, u32[]{:S(2)}, u32[]{:S(2)}) collective-permute-start(bf16[2,128,1024]{2,1,0:T(8,128)(2,1)} %pad_maximum_fusion.refs_0_), channel_id=1, source_target_pairs={{0,4},{2,6},{4,0},{6,2},{1,5},{3,7},{5,1},{7,3},{8,12},{10,14},{12... | collective-permute-start | bytes 1572872 | tf_op jit(solution)/shard_map/ppermute | solution.py:31
  121.1 1.9 %collective-permute-start.6 = (bf16[2,128,1024]{2,1,0:T(8,128)(2,1)}, bf16[2,128,1024]{2,1,0:T(8,128)(2,1)}, u32[]{:S(2)}, u32[]{:S(2)}) collective-permute-start(bf16[2,128,1024]{2,1,0:T(8,128)(2,1)} %pad_maximum_fusion.refs_0_), channel_id=1, source_target_pairs={{0,2},{2,4},{4,6},{6,0},{1,3},{3,5},{5,7},{7,1},{8,10},{10,12},{12... | collective-permute-start | bytes 1572872 | tf_op jit(solution)/shard_map/ppermute | solution.py:31
  123.0 3.8 %all-to-all-done.3.o_ref = bf16[8,272,128]{2,1,0:T(8,128)(2,1)} async-done(((bf16[8,272,128]{2,1,0:T(8,128)(2,1)}), bf16[8,272,128]{2,1,0:T(8,128)(2,1)}, u32[]{:S(2)}, u32[]{:S(2)}) %all-to-all-start.3) | async-done | bytes 557088 | tf_op jit(solution)/shard_map/all_to_all | solution.py:35
  126.8 2.6 %merge.1 = bf16[8,256,128]{2,1,0:T(8,128)(2,1)} custom-call(bf16[8,272,128]{2,1,0:T(8,128)(2,1)} %all-to-all-done.3.o_ref), custom_call_target="tpu_custom_call" | custom-call | flops 1 | bytes 1 | tf_op jit(solution)/shard_map/merge/pallas_call | solution.py:216
  129.4 6.6 %all-to-all-start.4 = ((bf16[8,256,128]{2,1,0:T(8,128)(2,1)}), bf16[8,256,128]{2,1,0:T(8,128)(2,1)}, u32[]{:S(2)}, u32[]{:S(2)}) async-start(bf16[8,256,128]{2,1,0:T(8,128)(2,1)} %merge.1), calls=%async_computation.4 | async-start | bytes 1048576 | tf_op jit(solution)/shard_map/all_to_all | solution.py:35
  136.0 1.9 %collective-permute-start.9 = (bf16[2,128,1024]{2,1,0:T(8,128)(2,1)}, bf16[2,128,1024]{2,1,0:T(8,128)(2,1)}, u32[]{:S(2)}, u32[]{:S(2)}) collective-permute-start(bf16[2,128,1024]{2,1,0:T(8,128)(2,1)} %pad_maximum_fusion.refs_0_), channel_id=1, source_target_pairs={{0,8},{8,0},{1,9},{9,1},{2,10},{10,2},{3,11},{11,3},{4,12},{12,4},... | collective-permute-start | bytes 1572872 | tf_op jit(solution)/shard_map/ppermute | solution.py:26
  137.9 1.7 collective-permute-done.8.refs_3_
  139.6 1.9 %collective-permute-start.12 = (bf16[2,128,1024]{2,1,0:T(8,128)(2,1)}, bf16[2,128,1024]{2,1,0:T(8,128)(2,1)}, u32[]{:S(2)}, u32[]{:S(2)}) collective-permute-start(bf16[2,128,1024]{2,1,0:T(8,128)(2,1)} %collective-permute-done.8.refs_3_), channel_id=1, source_target_pairs={{0,8},{8,0},{1,9},{9,1},{2,10},{10,2},{3,11},{11,3},{4,12},{12,4},... | collective-permute-start | bytes 1572872 | tf_op jit(solution)/shard_map/ppermute | solution.py:26
  141.5 0.0 collective-permute-done.7.refs_2_
  141.5 2.4 %collective-permute-start.11 = (bf16[2,128,1024]{2,1,0:T(8,128)(2,1)}, bf16[2,128,1024]{2,1,0:T(8,128)(2,1)}, u32[]{:S(2)}, u32[]{:S(2)}) collective-permute-start(bf16[2,128,1024]{2,1,0:T(8,128)(2,1)} %collective-permute-done.7.refs_2_), channel_id=1, source_target_pairs={{0,8},{8,0},{1,9},{9,1},{2,10},{10,2},{3,11},{11,3},{4,12},{12,4},... | collective-permute-start | bytes 1572872 | tf_op jit(solution)/shard_map/ppermute | solution.py:26
  143.9 2.0 %collective-permute-done.6.refs_1_ = bf16[2,128,1024]{2,1,0:T(8,128)(2,1)} collective-permute-done((bf16[2,128,1024]{2,1,0:T(8,128)(2,1)}, bf16[2,128,1024]{2,1,0:T(8,128)(2,1)}, u32[]{:S(2)}, u32[]{:S(2)}) %collective-permute-start.6) | collective-permute-done | bytes 524320 | tf_op jit(solution)/shard_map/ppermute | solution.py:31
  146.0 1.9 %collective-permute-start.10 = (bf16[2,128,1024]{2,1,0:T(8,128)(2,1)}, bf16[2,128,1024]{2,1,0:T(8,128)(2,1)}, u32[]{:S(2)}, u32[]{:S(2)}) collective-permute-start(bf16[2,128,1024]{2,1,0:T(8,128)(2,1)} %collective-permute-done.6.refs_1_), channel_id=1, source_target_pairs={{0,8},{8,0},{1,9},{9,1},{2,10},{10,2},{3,11},{11,3},{4,12},{12,4},... | collective-permute-start | bytes 1572872 | tf_op jit(solution)/shard_map/ppermute | solution.py:26
  148.0 0.0 copy-done.3
  148.0 0.1 copy.10
  148.1 0.1 stack.79.place_ref
  148.2 0.0 collective-permute-done.9.refs_4_
  148.2 0.0 collective-permute-done.12.refs_7_
  148.2 0.0 collective-permute-done.11.refs_6_
  148.2 1.9 %collective-permute-done.10.refs_5_ = bf16[2,128,1024]{2,1,0:T(8,128)(2,1)} collective-permute-done((bf16[2,128,1024]{2,1,0:T(8,128)(2,1)}, bf16[2,128,1024]{2,1,0:T(8,128)(2,1)}, u32[]{:S(2)}, u32[]{:S(2)}) %collective-permute-start.10) | collective-permute-done | bytes 524320 | tf_op jit(solution)/shard_map/ppermute | solution.py:26
  150.1 0.0 all-to-all-done.4.att_ref
  150.1 5.7 %tail.1 = (bf16[256,256]{1,0:T(8,128)(2,1)}, f32[256,128]{1,0:T(8,128)S(1)}) custom-call(s32[10]{0:T(128)S(1)} %stack.79.place_ref, bf16[8,256,128]{2,1,0:T(8,128)(2,1)} %all-to-all-done.4.att_ref, bf16[8,256,256]{2,1,0:T(8,128)(2,1)S(1)} %bitcast.36, bf16[64,64,256]{2,1,0:T(8,128)(2,1)} %all-gather.3.cloned.1.call-done.hw_ref, s32[256,4]{1,0:T(8,128)S(1)} %bitcast.38, ...), custom_call_target="tpu_custom_call" | custom-call | flops 1 | bytes 1 | tf_op jit(solution)/shard_map/tail/pallas_call | solution.py:273
  155.8 18.7 %all_to_all.30.s_ref = f32[8,32,128]{2,1,0:T(8,128)} all-to-all(f32[8,32,128]{2,1,0:T(8,128)S(1)} %bitcast.39), channel_id=1, replica_groups=mesh['y'=8,'z'=4,'c'=2,'x'=4,'h'=2] {'x','h'}, dimensions={0} | all-to-all | bytes 262144 | tf_op jit(solution)/shard_map/all_to_all | solution.py:35
  174.6 1.7 loss.1
  (13 shorter events, 0.1 us)
Async XLA Ops:
  7.2 13.5 %copy-start = (bf16[4,1024,256]{2,1,0:T(8,128)(2,1)S(1)}, bf16[4,1024,256]{2,1,0:T(8,128)(2,1)}, u32[]{:S(2)}) copy-start(bf16[4,1024,256]{2,1,0:T(8,128)(2,1)} %param.10) | copy-start | bytes 6291460
  7.2 12.4 %collective-permute-start = (s32[4,256]{1,0:T(4,128)}, s32[4,256]{1,0:T(4,128)S(1)}, u32[]{:S(2)}, u32[]{:S(2)}) collective-permute-start(s32[4,256]{1,0:T(4,128)} %param.7), channel_id=1, source_target_pairs={{0,8},{8,16},{16,24},{24,32},{32,40},{40,48},{48,56},{56,64},{64,7... | collective-permute-start | bytes 12296 | tf_op jit(solution)/shard_map/ppermute | solution.py:333
  10.7 15.1 %all-to-all-start = ((bf16[8,64,256]{2,1,0:T(8,128)(2,1)}), bf16[8,64,256]{2,1,0:T(8,128)(2,1)S(1)}, u32[]{:S(2)}, u32[]{:S(2)}) async-start(bf16[8,64,256]{2,1,0:T(8,128)(2,1)} %broadcast_in_dim.74), calls=%async_computation | async-start | bytes 524288 | tf_op jit(solution)/shard_map/all_to_all | solution.py:35
  25.8 16.4 %copy-start.2 = (bf16[8,64,256]{2,1,0:T(8,128)(2,1)}, bf16[8,64,256]{2,1,0:T(8,128)(2,1)S(1)}, u32[]{:S(2)}) copy-start(bf16[8,64,256]{2,1,0:T(8,128)(2,1)S(1)} %all-to-all-done) | copy-start | bytes 786436
  25.8 15.3 %collective-permute-start.1 = (bf16[256,256]{1,0:T(8,128)(2,1)S(1)}, bf16[256,256]{1,0:T(8,128)(2,1)S(1)}, u32[]{:S(2)}, u32[]{:S(2)}) collective-permute-start(bf16[256,256]{1,0:T(8,128)(2,1)S(1)} %fusion.4), channel_id=1, source_target_pairs={{0,1},{1,0},{2,3},{3,2},{4,5},{5,4},{6,7},{7,6},{8,9},{9,8},{10,11... | collective-permute-start | bytes 393224 | tf_op jit(solution)/shard_map/ppermute | solution.py:26
  42.2 15.5 %all-to-all-start.1 = ((bf16[4,2,256,256]{3,2,1,0:T(8,128)(2,1)}), bf16[4,2,256,256]{3,2,1,0:T(8,128)(2,1)S(1)}, u32[]{:S(2)}, u32[]{:S(2)}) async-start(bf16[4,2,256,256]{3,2,1,0:T(8,128)(2,1)} %broadcast_in_dim.75), calls=%async_computation.1 | async-start | bytes 2097152 | tf_op jit(solution)/shard_map/all_to_all | solution.py:35
  46.5 103.6 %all-gather.3.cloned.1.call-start = ((), (), s32[]{:S(2)}) async-start(), calls=%async_computation.6 | async-start | bytes 2359296 | tf_op jit(solution)/shard_map/all_gather | solution.py:354
  48.2 25.4 %collective-permute-start.3 = (bf16[128,1024]{1,0:T(8,128)(2,1)S(1)}, bf16[128,1024]{1,0:T(8,128)(2,1)}, u32[]{:S(2)}, u32[]{:S(2)}) collective-permute-start(bf16[128,1024]{1,0:T(8,128)(2,1)S(1)} %constant_dynamic-slice_fusion), channel_id=1, source_target_pairs={{0,1},{1,0},{2,3},{3,2},{4,5},{5,4},{6,7},{7,6},{8,9},{9,8},{10,11... | collective-permute-start | bytes 786440 | tf_op jit(solution)/shard_map/ppermute | solution.py:26
  57.6 1.4 copy-start.1
  60.3 12.4 %collective-permute-start.2 = (bf16[256,256]{1,0:T(8,128)(2,1)S(1)}, bf16[256,256]{1,0:T(8,128)(2,1)}, u32[]{:S(2)}, u32[]{:S(2)}) collective-permute-start(bf16[256,256]{1,0:T(8,128)(2,1)S(1)} %get-tuple-element.18), channel_id=1, source_target_pairs={{0,32},{16,48},{32,0},{48,16},{1,33},{17,49},{33,1},{49,17},{2,34}... | collective-permute-start | bytes 393224 | tf_op jit(solution)/shard_map/ppermute | solution.py:26
  66.0 28.3 %all-to-all-start.2 = ((bf16[8,256,128]{2,1,0:T(8,128)(2,1)}), bf16[8,256,128]{2,1,0:T(8,128)(2,1)}, u32[]{:S(2)}, u32[]{:S(2)}) async-start(bf16[8,256,128]{2,1,0:T(8,128)(2,1)} %broadcast_in_dim.76), calls=%async_computation.2 | async-start | bytes 1048576 | tf_op jit(solution)/shard_map/all_to_all | solution.py:35
  73.6 8.3 %collective-permute-start.4 = (bf16[2,256,256]{2,1,0:T(8,128)(2,1)S(1)}, bf16[2,256,256]{2,1,0:T(8,128)(2,1)S(1)}, u32[]{:S(2)}, u32[]{:S(2)}) collective-permute-start(bf16[2,256,256]{2,1,0:T(8,128)(2,1)S(1)} %pad_maximum_fusion.2), channel_id=1, source_target_pairs={{0,16},{16,0},{32,48},{48,32},{1,17},{17,1},{33,49},{49,33},{2,18}... | collective-permute-start | bytes 786440 | tf_op jit(solution)/shard_map/ppermute | solution.py:26
  82.6 11.7 %collective-permute-start.5 = (bf16[4,256,256]{2,1,0:T(8,128)(2,1)}, bf16[4,256,256]{2,1,0:T(8,128)(2,1)}, u32[]{:S(2)}, u32[]{:S(2)}) collective-permute-start(bf16[4,256,256]{2,1,0:T(8,128)(2,1)} %constant_dynamic-update-slice_fusion.near_ref), channel_id=1, source_target_pairs={{0,8},{8,0},{1,9},{9,1},{2,10},{10,2},{3,11},{11,3},{4,12},{12,4},... | collective-permute-start | bytes 1572872 | tf_op jit(solution)/shard_map/ppermute | solution.py:26
  107.2 40.8 %copy-start.3 = (s32[4,256]{1,0:T(4,128)S(1)}, s32[4,256]{1,0:T(4,128)}, u32[]{:S(2)}) copy-start(s32[4,256]{1,0:T(4,128)} %param.9) | copy-start | bytes 12292
  107.2 19.6 %all-to-all-start.3 = ((bf16[8,272,128]{2,1,0:T(8,128)(2,1)}), bf16[8,272,128]{2,1,0:T(8,128)(2,1)}, u32[]{:S(2)}, u32[]{:S(2)}) async-start(bf16[8,272,128]{2,1,0:T(8,128)(2,1)} %attend.1), calls=%async_computation.3 | async-start | bytes 1114112 | tf_op jit(solution)/shard_map/all_to_all | solution.py:35
  114.8 24.8 %collective-permute-start.8 = (bf16[2,128,1024]{2,1,0:T(8,128)(2,1)}, bf16[2,128,1024]{2,1,0:T(8,128)(2,1)}, u32[]{:S(2)}, u32[]{:S(2)}) collective-permute-start(bf16[2,128,1024]{2,1,0:T(8,128)(2,1)} %pad_maximum_fusion.refs_0_), channel_id=1, source_target_pairs={{0,6},{2,0},{4,2},{6,4},{1,7},{3,1},{5,3},{7,5},{8,14},{10,8},{12,... | collective-permute-start | bytes 1572872 | tf_op jit(solution)/shard_map/ppermute | solution.py:31
  118.1 23.5 %collective-permute-start.7 = (bf16[2,128,1024]{2,1,0:T(8,128)(2,1)}, bf16[2,128,1024]{2,1,0:T(8,128)(2,1)}, u32[]{:S(2)}, u32[]{:S(2)}) collective-permute-start(bf16[2,128,1024]{2,1,0:T(8,128)(2,1)} %pad_maximum_fusion.refs_0_), channel_id=1, source_target_pairs={{0,4},{2,6},{4,0},{6,2},{1,5},{3,7},{5,1},{7,3},{8,12},{10,14},{12... | collective-permute-start | bytes 1572872 | tf_op jit(solution)/shard_map/ppermute | solution.py:31
  121.1 24.9 %collective-permute-start.6 = (bf16[2,128,1024]{2,1,0:T(8,128)(2,1)}, bf16[2,128,1024]{2,1,0:T(8,128)(2,1)}, u32[]{:S(2)}, u32[]{:S(2)}) collective-permute-start(bf16[2,128,1024]{2,1,0:T(8,128)(2,1)} %pad_maximum_fusion.refs_0_), channel_id=1, source_target_pairs={{0,2},{2,4},{4,6},{6,0},{1,3},{3,5},{5,7},{7,1},{8,10},{10,12},{12... | collective-permute-start | bytes 1572872 | tf_op jit(solution)/shard_map/ppermute | solution.py:31
  129.4 20.7 %all-to-all-start.4 = ((bf16[8,256,128]{2,1,0:T(8,128)(2,1)}), bf16[8,256,128]{2,1,0:T(8,128)(2,1)}, u32[]{:S(2)}, u32[]{:S(2)}) async-start(bf16[8,256,128]{2,1,0:T(8,128)(2,1)} %merge.1), calls=%async_computation.4 | async-start | bytes 1048576 | tf_op jit(solution)/shard_map/all_to_all | solution.py:35
  136.0 12.2 %collective-permute-start.9 = (bf16[2,128,1024]{2,1,0:T(8,128)(2,1)}, bf16[2,128,1024]{2,1,0:T(8,128)(2,1)}, u32[]{:S(2)}, u32[]{:S(2)}) collective-permute-start(bf16[2,128,1024]{2,1,0:T(8,128)(2,1)} %pad_maximum_fusion.refs_0_), channel_id=1, source_target_pairs={{0,8},{8,0},{1,9},{9,1},{2,10},{10,2},{3,11},{11,3},{4,12},{12,4},... | collective-permute-start | bytes 1572872 | tf_op jit(solution)/shard_map/ppermute | solution.py:26
  139.6 8.6 %collective-permute-start.12 = (bf16[2,128,1024]{2,1,0:T(8,128)(2,1)}, bf16[2,128,1024]{2,1,0:T(8,128)(2,1)}, u32[]{:S(2)}, u32[]{:S(2)}) collective-permute-start(bf16[2,128,1024]{2,1,0:T(8,128)(2,1)} %collective-permute-done.8.refs_3_), channel_id=1, source_target_pairs={{0,8},{8,0},{1,9},{9,1},{2,10},{10,2},{3,11},{11,3},{4,12},{12,4},... | collective-permute-start | bytes 1572872 | tf_op jit(solution)/shard_map/ppermute | solution.py:26
  141.5 6.7 %collective-permute-start.11 = (bf16[2,128,1024]{2,1,0:T(8,128)(2,1)}, bf16[2,128,1024]{2,1,0:T(8,128)(2,1)}, u32[]{:S(2)}, u32[]{:S(2)}) collective-permute-start(bf16[2,128,1024]{2,1,0:T(8,128)(2,1)} %collective-permute-done.7.refs_2_), channel_id=1, source_target_pairs={{0,8},{8,0},{1,9},{9,1},{2,10},{10,2},{3,11},{11,3},{4,12},{12,4},... | collective-permute-start | bytes 1572872 | tf_op jit(solution)/shard_map/ppermute | solution.py:26
  146.0 4.1 %collective-permute-start.10 = (bf16[2,128,1024]{2,1,0:T(8,128)(2,1)}, bf16[2,128,1024]{2,1,0:T(8,128)(2,1)}, u32[]{:S(2)}, u32[]{:S(2)}) collective-permute-start(bf16[2,128,1024]{2,1,0:T(8,128)(2,1)} %collective-permute-done.6.refs_1_), channel_id=1, source_target_pairs={{0,8},{8,0},{1,9},{9,1},{2,10},{10,2},{3,11},{11,3},{4,12},{12,4},... | collective-permute-start | bytes 1572872 | tf_op jit(solution)/shard_map/ppermute | solution.py:26
Sparse Core Ops, SparseCore 0:
  49.4 53.7 all-gather.2
